TPU v7x, 32 devices: a whole 2x2x4 slice. The times are simulated.
32 devices in a mesh: dp: 16 (over z, x, core), tensor: 2 (over y).
Axes of the slice: x: 2, y: 2, z: 4, core: 2. Of those that a mesh axis runs over, the one named last changes fastest.
Arguments:
- tokens: bfloat16 [16384, 1024], P(('dp', 'tensor')), may hold values from -6 to 6
- cotangent: bfloat16 [16384, 1024], P(('dp', 'tensor')), may hold values from -6 to 6
- sequence_lengths: int32 [64], replicated, may hold values from 0 to 1024, as said below
- sequence_group: int32 [64], replicated, may hold values from 0 to 15
- sequence_offset: int32 [64], replicated, may hold values from 0 to 15, as said below
- mixer_gain: bfloat16 [1024], replicated, may hold values from 0.5 to 1.5
- query_weight: bfloat16 [1024, 512], P('dp', 'tensor'), may hold values from -0.1875 to 0.1875
- key_weight: bfloat16 [1024, 512], P('dp', 'tensor'), may hold values from -0.1875 to 0.1875
- value_weight: bfloat16 [1024, 1024], P('dp', 'tensor'), may hold values from -0.1875 to 0.1875
- output_gate: bfloat16 [1024, 1024], P('dp', 'tensor'), may hold values from -0.1875 to 0.1875
- output_weight: bfloat16 [1024, 1024], P('dp', 'tensor'), may hold values from -0.375 to 0.375
- decay_down: bfloat16 [1024, 16], replicated, may hold values from -0.1875 to 0.1875
- decay_up: bfloat16 [16, 512], replicated, may hold values from -1.5 to 1.5
- decay_bias: bfloat16 [512], replicated, may hold values from -2 to 6
- head_gain: bfloat16 [256], replicated, may hold values from 0.5 to 1.5
- feed_gain: bfloat16 [1024], replicated, may hold values from 0.5 to 1.5
- feed_gate: bfloat16 [1024, 2816], P('dp', 'tensor'), may hold values from -0.1875 to 0.1875
- feed_up: bfloat16 [1024, 2816], P('dp', 'tensor'), may hold values from -0.1875 to 0.1875
- feed_down: bfloat16 [1024, 2816], P('dp', 'tensor'), may hold values from -0.15625 to 0.15625
Outputs:
- output: bfloat16 [16384, 1024], P(('dp', 'tensor'))
- input_grad: float32 [16384, 1024], P(('dp', 'tensor'))
- mixer_gain_grad: float32 [1024], replicated
- query_weight_grad: float32 [1024, 512], P('dp', 'tensor')
- key_weight_grad: float32 [1024, 512], P('dp', 'tensor')
- value_weight_grad: float32 [1024, 1024], P('dp', 'tensor')
- output_gate_grad: float32 [1024, 1024], P('dp', 'tensor')
- output_weight_grad: float32 [1024, 1024], P('dp', 'tensor')
- decay_down_grad: float32 [1024, 16], replicated
- decay_up_grad: float32 [16, 512], replicated
- decay_bias_grad: float32 [512], replicated
- head_gain_grad: float32 [256], replicated
- feed_gain_grad: float32 [1024], replicated
- feed_gate_grad: float32 [1024, 2816], P('dp', 'tensor')
- feed_up_grad: float32 [1024, 2816], P('dp', 'tensor')
- feed_down_grad: float32 [1024, 2816], P('dp', 'tensor')
Inputs may be any that keep to these rules, and one draw needn't show every extreme that they name: Record i is one sequence of sequence_lengths[i] tokens, held by index sequence_group[i] along dp and starting at span sequence_offset[i] of 64 tokens within that index's 1024 slots; a length of 0 marks an unused record. Each index along dp has 4 records and at least one live sequence; its live sequences, each rounded up to whole spans, are disjoint and lie within its 1024 slots, and one of them starts at span 0. Some index holds a single sequence of 1024 tokens. `sequence_offset`: an unused record has offset 0. Some index has a sequence that starts at its last span.
All inputs are finite; a program needn't handle non-finite values.
Results may differ from a plain program's by a relative error of at most 0.015.
Values may be sent and summed in bfloat16 or wider, within the bound.
No kernel may reach another device: no remote copies, remote signals or barrier semaphores. Data moves between devices by JAX's collectives and lax.ppermute only.
A program may use at most 192 MiB of HBM per device.

v0:
```python
import functools

import jax
import jax.numpy as jnp
from jax import lax
from jax.sharding import PartitionSpec as P

KDIM = 128
VDIM = 256
SPAN = 64


epsilon = 1e-06
head_epsilon = 1.0
gate_scale = 16.0
highest = lax.Precision.HIGHEST


def rms_forward(values, norm_gain, floor_value=epsilon):
    inverse = lax.rsqrt(jnp.mean(values * values, axis=-1, keepdims=True) + floor_value)
    return (values * inverse * norm_gain, inverse)


def rms_backward(values, inverse, norm_gain, upstream):
    scaled = upstream * norm_gain
    inner = jnp.mean(scaled * values, axis=-1, keepdims=True)
    grad_values = inverse * scaled - values * (inverse * inverse * inverse) * inner
    grad_gain = jnp.sum(upstream * values * inverse, axis=0)
    return (grad_values, grad_gain)


def group_layout(sequence_lengths, sequence_group, sequence_offset, which_group, group_rows):
    span_count = group_rows // SPAN
    live_record = (sequence_group == which_group) & (sequence_lengths > 0)
    start_row = sequence_offset * SPAN
    places = jnp.arange(group_rows, dtype=jnp.int32)[:, None]
    covered = (
        live_record[None, :]
        & (places >= start_row[None, :])
        & (places < (start_row + sequence_lengths)[None, :])
    )
    live_mask = jnp.any(covered, axis=1).astype(jnp.float32)
    span_ids = jnp.arange(span_count, dtype=jnp.int32)[:, None]
    restart = jnp.any(live_record[None, :] & (span_ids == sequence_offset[None, :]), axis=1).astype(
        jnp.float32
    )
    return (live_mask, restart)


def span_mixer(queries, key_rows, values, decays, restart):
    length, head_count, key_size = queries.shape
    value_size = values.shape[2]
    spans = restart.shape[0]
    span_rows = length // spans
    block_shape = (spans, span_rows, head_count, key_size)
    query_blocks = queries.reshape(block_shape)
    key_blocks = key_rows.reshape(block_shape)
    value_blocks = values.reshape((spans, span_rows, head_count, value_size))
    within = jnp.cumsum(decays.reshape(block_shape), axis=1)
    last_sum = within[:, -1]
    span_add = jnp.einsum(
        "nchk,nchv->nhkv",
        key_blocks * jnp.exp(last_sum[:, None] - within),
        value_blocks,
        precision=highest,
    )

    def advance(memory, entries):
        fading, addend, keep_flag = entries
        entering = memory * keep_flag
        return (fading[:, :, None] * entering + addend, entering)

    start_memory = jnp.zeros((head_count, key_size, value_size), jnp.float32)
    _, entering = lax.scan(advance, start_memory, (jnp.exp(last_sum), span_add, 1.0 - restart))
    carried = jnp.einsum(
        "nchk,nhkv->nchv", query_blocks * jnp.exp(within), entering, precision=highest
    )
    sub_rows = 16
    sub_count = span_rows // sub_rows
    positions = jnp.arange(span_rows, dtype=jnp.int32)
    sub_ids = jnp.arange(sub_count, dtype=jnp.int32)
    reach = positions[None, :] < (sub_ids[:, None] + 1) * sub_rows
    target_rows = sub_ids[:, None] * sub_rows + jnp.arange(sub_rows, dtype=jnp.int32)[None, :]
    causal = positions[None, None, :] <= target_rows[:, :, None]

    def local_block(entries):
        block_query, block_key, block_value, block_decay = entries
        pair_rows = block_query.shape[0]
        ends = block_decay[:, sub_rows - 1 :: sub_rows]
        bounds = jnp.concatenate([jnp.zeros_like(ends[:, :1]), ends[:, :-1]], axis=1)
        split_shape = (pair_rows, sub_count, sub_rows, head_count, key_size)
        query_parts = block_query.reshape(split_shape) * jnp.exp(
            block_decay.reshape(split_shape) - bounds[:, :, None]
        )
        reach_full = reach[None, :, :, None, None]
        gap = bounds[:, :, None] - block_decay[:, None]
        key_parts = jnp.where(
            reach_full, block_key[:, None] * jnp.exp(jnp.where(reach_full, gap, 0.0)), 0.0
        )
        scores = jnp.einsum("bpihk,bpjhk->bphij", query_parts, key_parts, precision=highest)
        scores = jnp.where(causal[None, :, None, :, :], scores, 0.0)
        mixed = jnp.einsum("bphij,bjhv->bpihv", scores, block_value, precision=highest)
        return mixed.reshape((pair_rows, span_rows, head_count, value_size))

    pair_count = spans // 2
    pair_shape = (pair_count, 2) + block_shape[1:]
    inside = lax.map(
        jax.checkpoint(local_block),
        (
            query_blocks.reshape(pair_shape),
            key_blocks.reshape(pair_shape),
            value_blocks.reshape((pair_count, 2, span_rows, head_count, value_size)),
            within.reshape(pair_shape),
        ),
    )
    combined = carried + inside.reshape((spans, span_rows, head_count, value_size))
    return combined.reshape((length, head_count, value_size))


def mixer_branch(projected, latent, up_local, bias_local, head_norm_gain, live_mask, restart):
    key_width = up_local.shape[1]
    head_count = key_width // KDIM
    value_width = head_count * VDIM
    length = projected.shape[0]
    queries = projected[:, :key_width].reshape(length, head_count, KDIM)
    key_rows = projected[:, key_width : 2 * key_width].reshape(length, head_count, KDIM)
    values = projected[:, 2 * key_width : 2 * key_width + value_width].reshape(
        length, head_count, VDIM
    )
    gating = projected[:, 2 * key_width + value_width :]
    decays = (
        jax.nn.log_sigmoid(jnp.dot(latent, up_local, precision=highest) + bias_local) / gate_scale
    )
    mixture = span_mixer(
        queries, key_rows, values, decays.reshape(length, head_count, KDIM), restart
    )
    head_out = rms_forward(mixture, head_norm_gain, head_epsilon)[0]
    return head_out.reshape(length, value_width) * jax.nn.silu(gating) * live_mask[:, None]


def times_transposed(left, right):
    return lax.dot_general(
        left, right, (((1,), (1,)), ((), ())), preferred_element_type=jnp.float32
    )


def over_rows(left, right):
    return lax.dot_general(
        left, right, (((0,), (0,)), ((), ())), preferred_element_type=jnp.float32
    )


def on_device(
    tokens,
    cotangent,
    sequence_lengths,
    sequence_group,
    sequence_offset,
    mixer_gain,
    query_weight,
    key_weight,
    value_weight,
    output_gate,
    output_weight,
    decay_down,
    decay_up,
    decay_bias,
    head_gain,
    feed_gain,
    feed_gate,
    feed_up,
    feed_down,
):
    which_group = lax.axis_index("dp")
    half_index = lax.axis_index("tensor")
    row_count = tokens.shape[0]
    group_rows = row_count * lax.axis_size("tensor")
    live_mask, restart = group_layout(
        sequence_lengths, sequence_group, sequence_offset, which_group, group_rows
    )
    mixer_weights = (
        lax.all_gather(query_weight, "dp", axis=0, tiled=True),
        lax.all_gather(key_weight, "dp", axis=0, tiled=True),
        lax.all_gather(value_weight, "dp", axis=0, tiled=True),
        lax.all_gather(output_gate, "dp", axis=0, tiled=True),
        lax.all_gather(output_weight, "dp", axis=0, tiled=True),
    )
    query_full, key_full, value_full, gate_full, output_full = mixer_weights
    joined = jnp.concatenate([query_full, key_full, value_full, gate_full], axis=1)
    key_width = query_full.shape[1]
    value_width = value_full.shape[1]
    gain_in = mixer_gain.astype(jnp.float32)
    token_values = tokens.astype(jnp.float32)
    normed_in, inverse_in = rms_forward(token_values, gain_in)
    normed_all = lax.all_gather(normed_in.astype(jnp.bfloat16), "tensor", axis=0, tiled=True)
    projected = jnp.dot(normed_all, joined, preferred_element_type=jnp.float32)
    latent = jnp.dot(normed_all, decay_down, preferred_element_type=jnp.float32)
    up_local = lax.dynamic_slice_in_dim(decay_up, half_index * key_width, key_width, 1).astype(
        jnp.float32
    )
    bias_local = lax.dynamic_slice_in_dim(decay_bias, half_index * key_width, key_width, 0).astype(
        jnp.float32
    )
    branch = functools.partial(mixer_branch, live_mask=live_mask, restart=restart)
    gated, branch_back = jax.vjp(
        branch, projected, latent, up_local, bias_local, head_gain.astype(jnp.float32)
    )
    gated_low = gated.astype(jnp.bfloat16)
    attended = lax.psum_scatter(
        times_transposed(gated_low, output_full).astype(jnp.bfloat16),
        "tensor",
        scatter_dimension=0,
        tiled=True,
    ).astype(jnp.float32)
    middle = token_values + attended
    feed_weights = (
        lax.all_gather(feed_gate, "dp", axis=0, tiled=True),
        lax.all_gather(feed_up, "dp", axis=0, tiled=True),
        lax.all_gather(feed_down, "dp", axis=0, tiled=True),
    )
    feed_gate_full, feed_up_full, feed_down_full = feed_weights
    gain_mid = feed_gain.astype(jnp.float32)
    normed_mid, inverse_mid = rms_forward(middle, gain_mid)
    normed_mid_all = lax.all_gather(normed_mid.astype(jnp.bfloat16), "tensor", axis=0, tiled=True)
    gate_part = jnp.dot(normed_mid_all, feed_gate_full, preferred_element_type=jnp.float32)
    up_part = jnp.dot(normed_mid_all, feed_up_full, preferred_element_type=jnp.float32)
    sigmoid_gate = jax.nn.sigmoid(gate_part)
    silu_gate = gate_part * sigmoid_gate
    hidden_low = (silu_gate * up_part).astype(jnp.bfloat16)
    fed = lax.psum_scatter(
        times_transposed(hidden_low, feed_down_full).astype(jnp.bfloat16),
        "tensor",
        scatter_dimension=0,
        tiled=True,
    ).astype(jnp.float32)
    output = (middle + fed).astype(jnp.bfloat16)
    (
        query_back,
        key_back,
        value_back,
        gate_back,
        output_back,
        feed_gate_back,
        feed_up_back,
        feed_down_back,
    ) = (
        lax.all_gather(query_weight, "dp", axis=0, tiled=True),
        lax.all_gather(key_weight, "dp", axis=0, tiled=True),
        lax.all_gather(value_weight, "dp", axis=0, tiled=True),
        lax.all_gather(output_gate, "dp", axis=0, tiled=True),
        lax.all_gather(output_weight, "dp", axis=0, tiled=True),
        lax.all_gather(feed_gate, "dp", axis=0, tiled=True),
        lax.all_gather(feed_up, "dp", axis=0, tiled=True),
        lax.all_gather(feed_down, "dp", axis=0, tiled=True),
    )
    joined_back = jnp.concatenate([query_back, key_back, value_back, gate_back], axis=1)
    upstream = cotangent.astype(jnp.float32)
    cotangent_all = lax.all_gather(cotangent, "tensor", axis=0, tiled=True)
    grad_feed_down = over_rows(cotangent_all, hidden_low)
    grad_hidden = jnp.dot(cotangent_all, feed_down_back, preferred_element_type=jnp.float32)
    grad_gate_low = (
        grad_hidden * up_part * (sigmoid_gate + silu_gate * (1.0 - sigmoid_gate))
    ).astype(jnp.bfloat16)
    grad_up_low = (grad_hidden * silu_gate).astype(jnp.bfloat16)
    grad_feed_gate = over_rows(normed_mid_all, grad_gate_low)
    grad_feed_up = over_rows(normed_mid_all, grad_up_low)
    from_gate = times_transposed(grad_gate_low, feed_gate_back)
    grad_normed_mid = lax.psum_scatter(
        (from_gate + times_transposed(grad_up_low, feed_up_back)).astype(jnp.bfloat16),
        "tensor",
        scatter_dimension=0,
        tiled=True,
    ).astype(jnp.float32)
    grad_mid_in, grad_feed_gain = rms_backward(middle, inverse_mid, gain_mid, grad_normed_mid)
    grad_middle = upstream + grad_mid_in
    attended_all = lax.all_gather(grad_middle.astype(jnp.bfloat16), "tensor", axis=0, tiled=True)
    grad_output_weight = over_rows(attended_all, gated_low)
    grad_gated = jnp.dot(attended_all, output_back, preferred_element_type=jnp.float32)
    grad_projected, grad_latent, grad_up_local, grad_bias_local, grad_head_gain = branch_back(
        grad_gated
    )
    projected_low = grad_projected.astype(jnp.bfloat16)
    grad_joined = over_rows(normed_all, projected_low)
    grad_query = grad_joined[:, :key_width]
    grad_key = grad_joined[:, key_width : 2 * key_width]
    grad_value = grad_joined[:, 2 * key_width : 2 * key_width + value_width]
    grad_gating = grad_joined[:, 2 * key_width + value_width :]
    latent_high = grad_latent.astype(jnp.bfloat16)
    latent_rest = (grad_latent - latent_high.astype(jnp.float32)).astype(jnp.bfloat16)
    grad_decay_down = over_rows(normed_all, latent_high) + over_rows(normed_all, latent_rest)
    down_values = decay_down.astype(jnp.float32)
    from_projected = times_transposed(projected_low, joined_back)
    from_latent = jnp.dot(grad_latent, down_values.T, precision=highest)
    grad_normed = lax.psum_scatter(
        (from_projected + from_latent).astype(jnp.bfloat16),
        "tensor",
        scatter_dimension=0,
        tiled=True,
    ).astype(jnp.float32)
    grad_in_part, grad_mixer_gain = rms_backward(token_values, inverse_in, gain_in, grad_normed)
    input_grad = grad_middle + grad_in_part
    weight_sums = (
        lax.psum_scatter(grad_query, "dp", scatter_dimension=0, tiled=True),
        lax.psum_scatter(grad_key, "dp", scatter_dimension=0, tiled=True),
        lax.psum_scatter(grad_value, "dp", scatter_dimension=0, tiled=True),
        lax.psum_scatter(grad_gating, "dp", scatter_dimension=0, tiled=True),
        lax.psum_scatter(grad_output_weight, "dp", scatter_dimension=0, tiled=True),
        lax.psum_scatter(grad_feed_gate, "dp", scatter_dimension=0, tiled=True),
        lax.psum_scatter(grad_feed_up, "dp", scatter_dimension=0, tiled=True),
        lax.psum_scatter(grad_feed_down, "dp", scatter_dimension=0, tiled=True),
    )
    up_grad_full = lax.dynamic_update_slice_in_dim(
        jnp.zeros(decay_up.shape, jnp.float32), grad_up_local, half_index * key_width, 1
    )
    bias_grad_full = lax.dynamic_update_slice_in_dim(
        jnp.zeros(decay_bias.shape, jnp.float32), grad_bias_local, half_index * key_width, 0
    )
    small_sums = lax.psum(
        (
            grad_mixer_gain,
            grad_decay_down,
            up_grad_full,
            bias_grad_full,
            grad_head_gain,
            grad_feed_gain,
        ),
        ("dp", "tensor"),
    )
    return (
        output,
        input_grad,
        small_sums[0],
        weight_sums[0],
        weight_sums[1],
        weight_sums[2],
        weight_sums[3],
        weight_sums[4],
        small_sums[1],
        small_sums[2],
        small_sums[3],
        small_sums[4],
        small_sums[5],
        weight_sums[5],
        weight_sums[6],
        weight_sums[7],
    )


def solution(mesh):
    return jax.shard_map(
        on_device,
        mesh=mesh,
        in_specs=(
            P(("dp", "tensor"), None),
            P(("dp", "tensor"), None),
            P(),
            P(),
            P(),
            P(),
            P("dp", "tensor"),
            P("dp", "tensor"),
            P("dp", "tensor"),
            P("dp", "tensor"),
            P("dp", "tensor"),
            P(),
            P(),
            P(),
            P(),
            P(),
            P("dp", "tensor"),
            P("dp", "tensor"),
            P("dp", "tensor"),
        ),
        out_specs=(
            P(("dp", "tensor"), None),
            P(("dp", "tensor"), None),
            P(),
            P("dp", "tensor"),
            P("dp", "tensor"),
            P("dp", "tensor"),
            P("dp", "tensor"),
            P("dp", "tensor"),
            P(),
            P(),
            P(),
            P(),
            P(),
            P("dp", "tensor"),
            P("dp", "tensor"),
            P("dp", "tensor"),
        ),
        check_vma=False,
    )
```

profile of v0, /device:TPU:0, one launch (start us, length us, event | category | flops | bytes accessed | tf_op | source)
XLA Modules:
  0.0 1734.8 jit_solution(7402013915677785487)
XLA Ops:
  65.3 25.7 %all-gather.15.cloned.1.call-done = bf16[1024,512]{1,0:T(8,128)(2,1)} async-done(((bf16[64,512]{1,0:T(8,128)(2,1)}), bf16[1024,512]{1,0:T(8,128)(2,1)}) %all-gather.15.cloned.1.call-update) | async-done | bytes 1048592 | tf_op jit(solution)/shard_map/all_gather | solution.py:185
  93.4 31.9 %all-gather.11.cloned.1.call-done = bf16[1024,1024]{1,0:T(8,128)(2,1)} async-done(((bf16[512,1024]{1,0:T(8,128)(2,1)}), bf16[1024,1024]{1,0:T(8,128)(2,1)}) %all-gather.11.cloned.1.call-update) | async-done | bytes 2097168 | tf_op jit(solution)/shard_map/all_gather | solution.py:195
  162.3 68.1 %while.71 = (s32[]{:T(128)}, f32[2,128,256]{2,1,0:T(8,128)S(1)}, f32[16,2,128,256]{3,2,1,0:T(8,128)}, f32[16,2,128,1]{2,1,3,0:T(2,128)}, f32[16,2,128]{2,1,0:T(2...) while((s32[]{:T(128)}, f32[2,128,256]{2,1,0:T(8,128)S(1)}, ...), condition=%wide.region_4.5_spmd.clone, body=%wide.region_3.4_spmd.clone.sunk | while | flops 393219 | bytes 1317504 | solution.py:74
  238.7 34.4 %while.70 = (s32[]{:T(128)}, f32[8,2,64,2,256]{4,2,3,1,0:T(8,128)}, f32[8,2,64,2,256]{4,2,3,1,0:T(8,128)S(1)}, f32[8,2,64,2,128]{4,2,3,1,0:T(8,128)}, f32[8,2,64...) while((s32[]{:T(128)}, f32[8,2,64,2,256]{4,2,3,1,0:T(8,128)}, ...), condition=%wide.region_6.7_spmd.clone.clone, body=%wide.region_5.6_spmd.clone.clone.sunk | while | flops 76103680 | bytes 2599797 | solution.py:107
  299.7 31.3 %reduce-scatter.15.cloned.1.call-done = bf16[512,1024]{1,0:T(8,128)(2,1)} async-done(((bf16[1024,1024]{1,0:T(8,128)(2,1)}), bf16[512,1024]{1,0:T(8,128)(2,1)}) %reduce-scatter.15.cloned.1.call-update) | async-done | bytes 1048592 | tf_op jit(solution)/shard_map/reduce_scatter | solution.py:209
  336.9 40.9 %all-gather.21.cloned.1.call-done = bf16[1024,1408]{1,0:T(8,128)(2,1)} async-done(((bf16[64,1408]{1,0:T(8,128)(2,1)}), bf16[1024,1408]{1,0:T(8,128)(2,1)}) %all-gather.21.cloned.1.call-update) | async-done | bytes 2883600 | tf_op jit(solution)/shard_map/all_gather | solution.py:217
  377.9 33.7 %all-gather.19.cloned.1.call-done = bf16[1024,1024]{1,0:T(8,128)(2,1)} async-done(((bf16[512,1024]{1,0:T(8,128)(2,1)}), bf16[1024,1024]{1,0:T(8,128)(2,1)}) %all-gather.19.cloned.1.call-update) | async-done | bytes 2097168 | tf_op jit(solution)/shard_map/all_gather | solution.py:224
  419.8 38.6 %all-gather.23.cloned.1.call-done = bf16[1024,1408]{1,0:T(8,128)(2,1)} async-done(((bf16[64,1408]{1,0:T(8,128)(2,1)}), bf16[1024,1408]{1,0:T(8,128)(2,1)}) %all-gather.23.cloned.1.call-update) | async-done | bytes 2883600 | tf_op jit(solution)/shard_map/all_gather | solution.py:218
  466.8 24.8 %all-gather.27.cloned.1.call-done = bf16[1024,1024]{1,0:T(8,128)(2,1)} async-done(((bf16[512,1024]{1,0:T(8,128)(2,1)}), bf16[1024,1024]{1,0:T(8,128)(2,1)}) %all-gather.27.cloned.1.call-update) | async-done | bytes 2097168 | tf_op jit(solution)/shard_map/all_gather | solution.py:258
  491.6 46.8 %all-gather.25.cloned.1.call-done = bf16[1024,1408]{1,0:T(8,128)(2,1)} async-done(((bf16[64,1408]{1,0:T(8,128)(2,1)}), bf16[1024,1408]{1,0:T(8,128)(2,1)}) %all-gather.25.cloned.1.call-update) | async-done | bytes 2883600 | tf_op jit(solution)/shard_map/all_gather | solution.py:219
  558.0 30.3 %reduce-scatter.19.cloned.1.call-done = bf16[512,1024]{1,0:T(8,128)(2,1)} async-done(((bf16[1024,1024]{1,0:T(8,128)(2,1)}), bf16[512,1024]{1,0:T(8,128)(2,1)}) %reduce-scatter.19.cloned.1.call-update) | async-done | bytes 1048592 | tf_op jit(solution)/shard_map/reduce_scatter | solution.py:268
  595.3 32.8 %all-gather.29.cloned.1.call-done = bf16[1024,1024]{1,0:T(8,128)(2,1)} async-done(((bf16[512,1024]{1,0:T(8,128)(2,1)}), bf16[1024,1024]{1,0:T(8,128)(2,1)}) %all-gather.29.cloned.1.call-update) | async-done | bytes 2097168 | tf_op jit(solution)/shard_map/all_gather | solution.py:276
  654.9 70.6 %while.72 = (s32[]{:T(128)}, f32[2,128,256]{2,1,0:T(8,128)S(1)}, f32[16,2,128]{2,1,0:T(2,128)}, f32[16,2,128,256]{3,2,1,0:T(8,128)}, f32[16,2,128,256]{3,2,1,0:T...) while((s32[]{:T(128)}, f32[2,128,256]{2,1,0:T(8,128)S(1)}, ...), condition=%wide.region_23.24_spmd.clone, body=%wide.region_21.23_spmd.clone.sunk | while | flops 458500 | bytes 1579172 | solution.py:74
  741.7 189.8 %while.69 = (s32[]{:T(128)}, f32[8,2,64,2,128]{4,2,3,1,0:T(8,128)}, f32[8,2,64,2,128]{4,2,3,1,0:T(8,128)}, f32[8,2,64,2,256]{4,2,3,1,0:T(8,128)}, f32[8,2,64,2,1...) while((s32[]{:T(128)}, f32[8,2,64,2,128]{4,2,3,1,0:T(8,128)}, ...), condition=%wide.region_20.21_spmd.clone, body=%wide.region_15.20_spmd.clone.sunk | while | flops 178523392 | bytes 9395493 | solution.py:107
  1029.7 40.5 %all-reduce.9 = (f32[1024]{0:T(1024)}, f32[16,512]{1,0:T(8,128)}, f32[512]{0:T(512)}, f32[256]{0:T(256)}, f32[1024]{0:T(1024)}) all-reduce(f32[1024]{0:T(1024)S(1)} %get-tuple-element.892, f32[16,512]{1,0:T(8,128)S(1)} %convolution_dynamic-update-slice_fusion, ...), channel_id=1, replica_groups=mesh['dp'=16,'tensor'=2] {'dp','tensor'}, use_global_device_ids=true, to_apply=%region_29.30 | all-reduce | flops 11008 | bytes 88064 | tf_op jit(solution)/shard_map/psum | solution.py:318
  1074.4 78.5 %all-reduce.12.cloned.1.call-done = f32[1024,16]{0,1:T(8,128)} async-done(((f32[1024,16]{0,1:T(8,128)}), f32[1024,16]{0,1:T(8,128)}) %all-reduce.12.cloned.1.call-update) | async-done | bytes 65552 | tf_op jit(solution)/shard_map/psum | solution.py:318
  1152.9 62.2 %reduce-scatter.23.cloned.1.call-done = f32[64,256]{1,0:T(8,128)} async-done(((f32[1024,256]{1,0:T(8,128)}), f32[64,256]{1,0:T(8,128)}) %reduce-scatter.23.cloned.1.call-update) | async-done | bytes 65552 | tf_op jit(solution)/shard_map/reduce_scatter | solution.py:303
  1215.1 61.0 %reduce-scatter.25.cloned.1.call-done = f32[64,256]{1,0:T(8,128)} async-done(((f32[1024,256]{1,0:T(8,128)}), f32[64,256]{1,0:T(8,128)}) %reduce-scatter.25.cloned.1.call-update) | async-done | bytes 65552 | tf_op jit(solution)/shard_map/reduce_scatter | solution.py:304
  1276.0 84.9 %reduce-scatter.35.cloned.1.call-done = f32[64,1408]{1,0:T(8,128)} async-done(((f32[1024,1408]{1,0:T(8,128)}), f32[64,1408]{1,0:T(8,128)}) %reduce-scatter.35.cloned.1.call-update) | async-done | bytes 360464 | tf_op jit(solution)/shard_map/reduce_scatter | solution.py:309
  1361.0 85.2 %reduce-scatter.33.cloned.1.call-done = f32[64,1408]{1,0:T(8,128)} async-done(((f32[1024,1408]{1,0:T(8,128)}), f32[64,1408]{1,0:T(8,128)}) %reduce-scatter.33.cloned.1.call-update) | async-done | bytes 360464 | tf_op jit(solution)/shard_map/reduce_scatter | solution.py:308
  1446.1 85.1 %reduce-scatter.37.cloned.1.call-done = f32[64,1408]{1,0:T(8,128)} async-done(((f32[1024,1408]{1,0:T(8,128)}), f32[64,1408]{1,0:T(8,128)}) %reduce-scatter.37.cloned.1.call-update) | async-done | bytes 360464
  1531.2 65.1 %reduce-scatter.31.cloned.1.call-done = f32[64,512]{1,0:T(8,128)} async-done(((f32[1024,512]{1,0:T(8,128)}), f32[64,512]{1,0:T(8,128)}) %reduce-scatter.31.cloned.1.call-update) | async-done | bytes 131088 | tf_op jit(solution)/shard_map/reduce_scatter | solution.py:307
  1596.3 65.3 %reduce-scatter.27.cloned.1.call-done = f32[64,512]{1,0:T(8,128)} async-done(((f32[1024,512]{1,0:T(8,128)}), f32[64,512]{1,0:T(8,128)}) %reduce-scatter.27.cloned.1.call-update) | async-done | bytes 131088 | tf_op jit(solution)/shard_map/reduce_scatter | solution.py:305
  1661.7 64.9 %reduce-scatter.29.cloned.1.call-done = f32[64,512]{1,0:T(8,128)} async-done(((f32[1024,512]{1,0:T(8,128)}), f32[64,512]{1,0:T(8,128)}) %reduce-scatter.29.cloned.1.call-update) | async-done | bytes 131088 | tf_op jit(solution)/shard_map/reduce_scatter | solution.py:306
  (759 shorter events, 689.1 us)
Async XLA Ops:
  7.2 55.7 %all-gather.13.cloned.1.call-start = ((), (), s32[]{:S(2)}) async-start(), calls=%async_computation.13 | async-start | bytes 1114112 | tf_op jit(solution)/shard_map/all_gather | solution.py:184
  7.9 83.2 %all-gather.15.cloned.1.call-start = ((), (), s32[]{:S(2)}) async-start(), calls=%async_computation.14 | async-start | bytes 1114112 | tf_op jit(solution)/shard_map/all_gather | solution.py:185
  8.7 116.6 %all-gather.11.cloned.1.call-start = ((), (), s32[]{:S(2)}) async-start(), calls=%async_computation.12 | async-start | bytes 3145728 | tf_op jit(solution)/shard_map/all_gather | solution.py:195
  14.1 280.8 %all-gather.17.cloned.1.call-start = ((), (), s32[]{:S(2)}) async-start(), calls=%async_computation.15 | async-start | bytes 1114112 | tf_op jit(solution)/shard_map/all_gather | solution.py:186
  14.7 316.4 %reduce-scatter.15.cloned.1.call-start = ((), (), s32[]{:S(2)}) async-start(), calls=%async_computation.16 | async-start | bytes 3145728 | tf_op jit(solution)/shard_map/reduce_scatter | solution.py:209
  299.1 78.8 %all-gather.21.cloned.1.call-start = ((), (), s32[]{:S(2)}) async-start(), calls=%async_computation.18 | async-start | bytes 3063808 | tf_op jit(solution)/shard_map/all_gather | solution.py:217
  299.7 111.9 %all-gather.19.cloned.1.call-start = ((), (), s32[]{:S(2)}) async-start(), calls=%async_computation.17 | async-start | bytes 3145728 | tf_op jit(solution)/shard_map/all_gather | solution.py:224
  333.2 258.6 %copy-start.46 = (f32[512]{0:T(512)}, f32[512]{0:T(512)S(1)}, u32[]{:S(2)}) copy-start(f32[512]{0:T(512)S(1)} %get-tuple-element.1009) | copy-start | bytes 6148
  334.6 123.9 %all-gather.23.cloned.1.call-start = ((), (), s32[]{:S(2)}) async-start(), calls=%async_computation.19 | async-start | bytes 3063808 | tf_op jit(solution)/shard_map/all_gather | solution.py:218
  335.4 156.2 %all-gather.27.cloned.1.call-start = ((), (), s32[]{:S(2)}) async-start(), calls=%async_computation.22 | async-start | bytes 3145728 | tf_op jit(solution)/shard_map/all_gather | solution.py:258
  336.1 202.3 %all-gather.25.cloned.1.call-start = ((), (), s32[]{:S(2)}) async-start(), calls=%async_computation.20 | async-start | bytes 3063808 | tf_op jit(solution)/shard_map/all_gather | solution.py:219
  336.7 251.6 %reduce-scatter.19.cloned.1.call-start = ((), (), s32[]{:S(2)}) async-start(), calls=%async_computation.23 | async-start | bytes 3145728 | tf_op jit(solution)/shard_map/reduce_scatter | solution.py:268
  558.0 70.1 %all-gather.29.cloned.1.call-start = ((), (), s32[]{:S(2)}) async-start(), calls=%async_computation.24 | async-start | bytes 3145728 | tf_op jit(solution)/shard_map/all_gather | solution.py:276
  594.9 432.7 %reduce-scatter.21.cloned.1.call-start = ((), (), s32[]{:S(2)}) async-start(), calls=%async_computation.25 | async-start | bytes 3145728 | tf_op jit(solution)/shard_map/reduce_scatter | solution.py:294
  963.8 106.4 %reduce-scatter.17.cloned.1.call-start = ((), (), s32[]{:S(2)}) async-start(), calls=%async_computation.21 | async-start | bytes 3145728 | tf_op jit(solution)/shard_map/reduce_scatter | solution.py:230
  971.3 181.6 %all-reduce.12.cloned.1.call-start = ((), (), s32[]{:S(2)}) async-start(), calls=%async_computation.31 | async-start | bytes 131072 | tf_op jit(solution)/shard_map/psum | solution.py:318
  974.3 240.8 %reduce-scatter.23.cloned.1.call-start = ((), (), s32[]{:S(2)}) async-start(), calls=%async_computation.26 | async-start | bytes 1114112 | tf_op jit(solution)/shard_map/reduce_scatter | solution.py:303
  984.6 291.4 %reduce-scatter.25.cloned.1.call-start = ((), (), s32[]{:S(2)}) async-start(), calls=%async_computation.27 | async-start | bytes 1114112 | tf_op jit(solution)/shard_map/reduce_scatter | solution.py:304
  985.2 375.7 %reduce-scatter.35.cloned.1.call-start = ((), (), s32[]{:S(2)}) async-start(), calls=%async_computation.33 | async-start | bytes 6127616 | tf_op jit(solution)/shard_map/reduce_scatter | solution.py:309
  993.3 452.8 %reduce-scatter.33.cloned.1.call-start = ((), (), s32[]{:S(2)}) async-start(), calls=%async_computation.32 | async-start | bytes 6127616 | tf_op jit(solution)/shard_map/reduce_scatter | solution.py:308
  1000.5 530.7 %reduce-scatter.37.cloned.1.call-start = ((), (), s32[]{:S(2)}) async-start(), calls=%async_computation.34 | async-start | bytes 6127616
  1015.3 581.0 %reduce-scatter.31.cloned.1.call-start = ((), (), s32[]{:S(2)}) async-start(), calls=%async_computation.30 | async-start | bytes 2228224 | tf_op jit(solution)/shard_map/reduce_scatter | solution.py:307
  1019.9 641.8 %reduce-scatter.27.cloned.1.call-start = ((), (), s32[]{:S(2)}) async-start(), calls=%async_computation.28 | async-start | bytes 2228224 | tf_op jit(solution)/shard_map/reduce_scatter | solution.py:305
  1024.7 701.9 %reduce-scatter.29.cloned.1.call-start = ((), (), s32[]{:S(2)}) async-start(), calls=%async_computation.29 | async-start | bytes 2228224 | tf_op jit(solution)/shard_map/reduce_scatter | solution.py:306
  (92 other events, 1218.4 us)
Sparse Core Ops, SparseCore 0:
  10.2 41.7 all-gather.12
  54.1 36.9 all-gather.14
  93.2 32.0 all-gather.10
  127.3 37.9 all-gather.16
  299.2 31.8 reduce-scatter.14
  333.5 44.3 all-gather.20
  380.0 31.4 all-gather.18
  414.1 44.3 all-gather.22
  460.1 31.4 all-gather.26
  494.0 44.3 all-gather.24
  558.1 30.1 reduce-scatter.18
  595.0 33.0 all-gather.28
  963.9 31.8 reduce-scatter.20
  997.9 31.8 reduce-scatter.16
  1035.2 117.6 all-reduce.11
  1156.9 58.1 reduce-scatter.22
  1219.6 56.4 reduce-scatter.24
  1280.4 80.5 reduce-scatter.34
  1365.4 80.6 reduce-scatter.32
  1450.5 80.7 reduce-scatter.36
  1535.6 60.7 reduce-scatter.30
  1601.1 60.5 reduce-scatter.26
  1666.0 60.5 reduce-scatter.28
where the time goes:
time: 1740 us; the launch traced here: 1730 us
  waiting for transfers between devices  995 us (57%)
  matrix products  243 us (14%)
  local copies, waits for them, and re-layouts  242 us (14%)
  other arithmetic  152 us (9%)
  blocking collectives  84.4 us (5%)
    unnamed x24, waiting for transfers between devices  90.9 us
    reduce_scatter x1, waiting for transfers between devices, on_device(): lax.psum_scatter(grad_feed_gate, 'dp', scatter_dimension=0, tiled=True)  85.2 us
    reduce_scatter x1, waiting for transfers between devices, on_device(): lax.psum_scatter(grad_feed_up, 'dp', scatter_dimension=0, tiled=True)  84.9 us
    psum x1, waiting for transfers between devices, on_device(): lax.psum((grad_mixer_gain, grad_decay_down, up_grad_full, bias_grad_full,...  78.5 us
    dot_general x32, matrix products, local_block(): jnp.einsum('bpihk,bpjhk->bphij', query_parts, key_parts, precision=highest)  76.1 us
    reduce_scatter x1, waiting for transfers between devices, on_device(): lax.psum_scatter(grad_value, 'dp', scatter_dimension=0, tiled=True)  65.3 us
    reduce_scatter x1, waiting for transfers between devices, on_device(): lax.psum_scatter(grad_output_weight, 'dp', scatter_dimension=0, tiled=True)  65.1 us
    reduce_scatter x1, waiting for transfers between devices, on_device(): lax.psum_scatter(grad_gating, 'dp', scatter_dimension=0, tiled=True)  64.9 us
  transfers between devices with their start and end apart: 23, of which 19 were waited for; matrix products, arithmetic and copies ran while one was open for 15% of the time, Pallas kernels for 0%

commit v1 on v0

v1 whole, which is shorter than its diff:
```python
import functools

import jax
import jax.numpy as jnp
import numpy as np
from jax import lax
from jax.experimental import pallas as pl
from jax.experimental.pallas import tpu as pltpu
from jax.sharding import PartitionSpec as P

KDIM = 128
VDIM = 256
SPAN = 64
LEVELS = 6
KINDS = LEVELS + 2
STEP_SPANS = 2

epsilon = 1e-06
head_epsilon = 1.0
gate_scale = 16.0
highest = lax.Precision.HIGHEST
f32 = jnp.float32
bf16 = jnp.bfloat16


def rms_forward(values, norm_gain, floor_value=epsilon):
    inverse = lax.rsqrt(jnp.mean(values * values, axis=-1, keepdims=True) + floor_value)
    return (values * inverse * norm_gain, inverse)


def rms_backward(values, inverse, norm_gain, upstream):
    scaled = upstream * norm_gain
    inner = jnp.mean(scaled * values, axis=-1, keepdims=True)
    grad_values = inverse * scaled - values * (inverse * inverse * inverse) * inner
    grad_gain = jnp.sum(upstream * values * inverse, axis=0)
    return (grad_values, grad_gain)


def group_layout(sequence_lengths, sequence_group, sequence_offset, which_group, places, span_count):
    live_record = (sequence_group == which_group) & (sequence_lengths > 0)
    start_row = sequence_offset * SPAN
    covered = (
        live_record[None, :]
        & (places >= start_row[None, :])
        & (places < (start_row + sequence_lengths)[None, :])
    )
    live_mask = jnp.any(covered, axis=1).astype(f32)
    span_ids = jnp.arange(span_count, dtype=jnp.int32)[:, None]
    restart = jnp.any(live_record[None, :] & (span_ids == sequence_offset[None, :]), axis=1)
    return (live_mask, restart.astype(jnp.int32))


def nn(left, right):
    return lax.dot_general(left, right, (((1,), (0,)), ((), ())), preferred_element_type=f32)


def nt(left, right):
    return lax.dot_general(left, right, (((1,), (1,)), ((), ())), preferred_element_type=f32)


def tn(left, right):
    return lax.dot_general(left, right, (((0,), (0,)), ((), ())), preferred_element_type=f32)


def decay_sums():
    rows = np.arange(SPAN)[:, None]
    cols = np.arange(SPAN)[None, :]
    blocks = [cols <= rows]
    for level in range(LEVELS):
        half = 1 << level
        edge = (rows // (2 * half)) * (2 * half) + half
        right = rows >= edge
        blocks.append(np.where(right, (cols >= edge) & (cols <= rows), (cols > rows) & (cols < edge)))
    blocks.append(cols > rows)
    return np.concatenate(blocks, axis=0).astype(np.float32)


def pair_levels():
    rows = lax.broadcasted_iota(jnp.int32, (SPAN, SPAN), 0)
    cols = lax.broadcasted_iota(jnp.int32, (SPAN, SPAN), 1)
    apart = rows ^ cols
    later = rows > cols
    masks = [later & (lax.shift_right_logical(apart, level) == 1) for level in range(LEVELS)]
    return masks, rows == cols


def span_factors(z_part, sums):
    decays = (jnp.minimum(z_part, 0.0) - jnp.log1p(jnp.exp(-jnp.abs(z_part)))) * (1.0 / gate_scale)
    high = decays.astype(bf16)
    low = (decays - high.astype(f32)).astype(bf16)
    return jnp.exp(nn(sums, jnp.concatenate([high, low], axis=0)))


def span_scores(queries, keys, factors, masks, diagonal):
    scores = jnp.where(diagonal, nt(queries.astype(bf16), keys.astype(bf16)), 0.0)
    query_levels = []
    key_levels = []
    for level in range(LEVELS):
        factor = factors[(level + 1) * SPAN : (level + 2) * SPAN]
        query_level = (queries * factor).astype(bf16)
        key_level = (keys * factor).astype(bf16)
        scores = jnp.where(masks[level], nt(query_level, key_level), scores)
        query_levels.append(query_level)
        key_levels.append(key_level)
    return scores, query_levels, key_levels


def forward_kernel(heads, scal, projected, z, live, gain, sums, gated, mixture, states, state):
    step = pl.program_id(0)
    key_width = heads * KDIM
    value_width = heads * VDIM

    @pl.when(step == 0)
    def _():
        state[...] = jnp.zeros_like(state)

    masks, diagonal = pair_levels()
    head_gain = gain[...]
    for part in range(STEP_SPANS):
        rows = slice(part * SPAN, (part + 1) * SPAN)
        factors_all = span_factors(z[rows, :], sums[...])
        keep = jnp.where(scal[1 + step * STEP_SPANS + part] == 0, 1.0, 0.0)
        for head in range(heads):
            keys_at = slice(head * KDIM, (head + 1) * KDIM)
            queries = projected[rows, keys_at]
            keys = projected[rows, key_width + head * KDIM : key_width + (head + 1) * KDIM]
            value_at = 2 * key_width + head * VDIM
            values = projected[rows, value_at : value_at + VDIM].astype(bf16)
            gating = projected[rows, value_at + value_width : value_at + value_width + VDIM]
            factors = factors_all[:, keys_at]
            scores, _, _ = span_scores(queries, keys, factors, masks, diagonal)
            entering = state[head] * keep
            entering_low = entering.astype(bf16)
            states[part, head] = entering_low
            whole = factors[:SPAN]
            after = factors[(KINDS - 1) * SPAN :]
            mixed = nn(scores.astype(bf16), values) + nt(
                (queries * whole).astype(bf16), entering_low
            )
            state[head] = entering * whole[SPAN - 1 :] + tn(values, (keys * after).astype(bf16))
            value_cols = slice(head * VDIM, (head + 1) * VDIM)
            mixture[rows, value_cols] = mixed
            inverse = lax.rsqrt(jnp.mean(mixed * mixed, axis=-1, keepdims=True) + head_epsilon)
            silu = gating * jax.nn.sigmoid(gating)
            gated[rows, value_cols] = (mixed * inverse * head_gain * silu * live[rows, :]).astype(bf16)


def backward_kernel(
    heads,
    scal,
    projected,
    z,
    live,
    gain,
    sums,
    mixture,
    states,
    grad_gated,
    grad_projected,
    grad_z,
    grad_gain,
    grad_state,
):
    step = pl.program_id(0)
    natural = pl.num_programs(0) - 1 - step
    key_width = heads * KDIM
    value_width = heads * VDIM

    @pl.when(step == 0)
    def _():
        grad_state[...] = jnp.zeros_like(grad_state)
        grad_gain[...] = jnp.zeros_like(grad_gain)

    masks, diagonal = pair_levels()
    head_gain = gain[...]
    last_row = lax.broadcasted_iota(jnp.int32, (SPAN, KDIM), 0) == SPAN - 1
    for part in reversed(range(STEP_SPANS)):
        rows = slice(part * SPAN, (part + 1) * SPAN)
        z_part = z[rows, :]
        factors_all = span_factors(z_part, sums[...])
        keep = jnp.where(scal[1 + natural * STEP_SPANS + part] == 0, 1.0, 0.0)
        live_part = live[rows, :]
        exponents = []
        for head in range(heads):
            keys_at = slice(head * KDIM, (head + 1) * KDIM)
            key_cols = slice(key_width + head * KDIM, key_width + (head + 1) * KDIM)
            value_at = 2 * key_width + head * VDIM
            value_cols = slice(value_at, value_at + VDIM)
            gate_cols = slice(value_at + value_width, value_at + value_width + VDIM)
            mixed_cols = slice(head * VDIM, (head + 1) * VDIM)
            queries = projected[rows, keys_at]
            keys = projected[rows, key_cols]
            values = projected[rows, value_cols].astype(bf16)
            gating = projected[rows, gate_cols]
            factors = factors_all[:, keys_at]
            scores, query_levels, key_levels = span_scores(queries, keys, factors, masks, diagonal)
            scores_low = scores.astype(bf16)
            whole = factors[:SPAN]
            after = factors[(KINDS - 1) * SPAN :]

            mixed = mixture[rows, mixed_cols]
            inverse = lax.rsqrt(jnp.mean(mixed * mixed, axis=-1, keepdims=True) + head_epsilon)
            unit = mixed * inverse
            sigmoid = jax.nn.sigmoid(gating)
            silu = gating * sigmoid
            upstream = grad_gated[rows, mixed_cols] * live_part
            grad_projected[rows, gate_cols] = (
                upstream * unit * head_gain * (sigmoid + silu * (1.0 - sigmoid))
            ).astype(bf16)
            normed_back = upstream * silu
            gain_part = normed_back * unit
            grad_gain[...] += jnp.sum(gain_part.reshape(SPAN // 8, 8, VDIM), axis=0)
            scaled = normed_back * head_gain
            inner = jnp.mean(scaled * unit, axis=-1, keepdims=True)
            grad_mixed = (inverse * (scaled - unit * inner)).astype(bf16)

            entering = states[part, head]
            leaving = grad_state[head]
            leaving_low = leaving.astype(bf16)
            grad_scores = nt(grad_mixed, values)
            after_keys = (keys * after).astype(bf16)
            whole_queries = (queries * whole).astype(bf16)
            grad_projected[rows, value_cols] = (
                tn(scores_low, grad_mixed) + nt(after_keys, leaving_low)
            ).astype(bf16)
            grad_queries = whole * nn(grad_mixed, entering)
            grad_keys = after * nn(values, leaving_low)
            fading = whole[SPAN - 1 :]
            last_sum = fading * jnp.sum(entering.astype(f32) * leaving, axis=0, keepdims=True)
            exponents_head = [queries * grad_queries + jnp.where(last_row, last_sum, 0.0)]
            last_exponent = keys * grad_keys
            for level in range(LEVELS):
                factor = factors[(level + 1) * SPAN : (level + 2) * SPAN]
                level_back = jnp.where(masks[level], grad_scores, 0.0).astype(bf16)
                query_part = factor * nn(level_back, key_levels[level])
                key_part = factor * tn(level_back, query_levels[level])
                grad_queries += query_part
                grad_keys += key_part
                exponents_head.append(queries * query_part + keys * key_part)
            exponents_head.append(last_exponent)
            same = jnp.sum(jnp.where(diagonal, grad_scores, 0.0), axis=1, keepdims=True)
            grad_projected[rows, keys_at] = (grad_queries + same * keys).astype(bf16)
            grad_projected[rows, key_cols] = (grad_keys + same * queries).astype(bf16)
            exponents.append(jnp.concatenate(exponents_head, axis=0).astype(bf16))
            grad_state[head] = keep * (leaving * fading + tn(grad_mixed, whole_queries))
        grad_decays = tn(sums[:, :SPAN], jnp.concatenate(exponents, axis=1))
        grad_z[rows, :] = grad_decays * jax.nn.sigmoid(-z_part) * (1.0 / gate_scale)


def mixer_specs(length, projected_width, key_width, value_width, reverse):
    steps = length // (SPAN * STEP_SPANS)
    step_rows = SPAN * STEP_SPANS
    heads = key_width // KDIM

    def natural(step):
        return steps - 1 - step if reverse else step

    def by_rows(step, scal):
        return (lax.rem(natural(step) + scal[0] * (steps // 2), steps), 0)

    def whole(step, scal):
        return (0, 0)

    return dict(
        steps=steps,
        projected=pl.BlockSpec((step_rows, projected_width), by_rows),
        z=pl.BlockSpec((step_rows, key_width), by_rows),
        live=pl.BlockSpec((step_rows, 1), by_rows),
        gain=pl.BlockSpec((1, VDIM), whole),
        sums=pl.BlockSpec((KINDS * SPAN, 2 * SPAN), whole),
        values=pl.BlockSpec((step_rows, value_width), by_rows),
        states=pl.BlockSpec(
            (STEP_SPANS, heads, VDIM, KDIM), lambda step, scal: (natural(step), 0, 0, 0)
        ),
        gain_grad=pl.BlockSpec((8, VDIM), whole),
    )


def mixer_forward(scal, projected, z, live, gain, sums):
    length, projected_width = projected.shape
    key_width = z.shape[1]
    heads = key_width // KDIM
    value_width = heads * VDIM
    spans = length // SPAN
    specs = mixer_specs(length, projected_width, key_width, value_width, False)
    return pl.pallas_call(
        functools.partial(forward_kernel, heads),
        grid_spec=pltpu.PrefetchScalarGridSpec(
            num_scalar_prefetch=1,
            grid=(specs["steps"],),
            in_specs=[specs[name] for name in ("projected", "z", "live", "gain", "sums")],
            out_specs=[specs[name] for name in ("values", "values", "states")],
            scratch_shapes=[pltpu.VMEM((heads, VDIM, KDIM), f32)],
        ),
        out_shape=[
            jax.ShapeDtypeStruct((length, value_width), bf16),
            jax.ShapeDtypeStruct((length, value_width), f32),
            jax.ShapeDtypeStruct((spans, heads, VDIM, KDIM), bf16),
        ],
        compiler_params=pltpu.CompilerParams(vmem_limit_bytes=40 * 1024 * 1024),
        cost_estimate=pl.CostEstimate(
            flops=10**10, bytes_accessed=15 * 10**6, transcendentals=4 * 10**6
        ),
        name="mixer_forward",
    )(scal, projected, z, live, gain, sums)


def mixer_backward(scal, projected, z, live, gain, sums, mixture, states, grad_gated):
    length, projected_width = projected.shape
    key_width = z.shape[1]
    heads = key_width // KDIM
    value_width = heads * VDIM
    specs = mixer_specs(length, projected_width, key_width, value_width, True)
    names = ("projected", "z", "live", "gain", "sums", "values", "states", "values")
    return pl.pallas_call(
        functools.partial(backward_kernel, heads),
        grid_spec=pltpu.PrefetchScalarGridSpec(
            num_scalar_prefetch=1,
            grid=(specs["steps"],),
            in_specs=[specs[name] for name in names],
            out_specs=[specs[name] for name in ("projected", "z", "gain_grad")],
            scratch_shapes=[pltpu.VMEM((heads, VDIM, KDIM), f32)],
        ),
        out_shape=[
            jax.ShapeDtypeStruct((length, projected_width), bf16),
            jax.ShapeDtypeStruct((length, key_width), f32),
            jax.ShapeDtypeStruct((8, VDIM), f32),
        ],
        compiler_params=pltpu.CompilerParams(vmem_limit_bytes=40 * 1024 * 1024),
        cost_estimate=pl.CostEstimate(
            flops=25 * 10**9, bytes_accessed=20 * 10**6, transcendentals=4 * 10**6
        ),
        name="mixer_backward",
    )(scal, projected, z, live, gain, sums, mixture, states, grad_gated)


def swap_tensor(values):
    return lax.ppermute(values, "tensor", [(0, 1), (1, 0)])


def butterfly_sum(values):
    total = values + swap_tensor(values)
    count = lax.axis_size("dp")
    reach = 1
    while reach < count:
        total = total + lax.ppermute(total, "dp", [(i, i ^ reach) for i in range(count)])
        reach *= 2
    return total


def on_device(
    tokens,
    cotangent,
    sequence_lengths,
    sequence_group,
    sequence_offset,
    mixer_gain,
    query_weight,
    key_weight,
    value_weight,
    output_gate,
    output_weight,
    decay_down,
    decay_up,
    decay_bias,
    head_gain,
    feed_gain,
    feed_gate,
    feed_up,
    feed_down,
):
    which_group = lax.axis_index("dp")
    half_index = lax.axis_index("tensor")
    own = tokens.shape[0]
    group_rows = own * 2
    key_width = query_weight.shape[1]
    value_width = value_weight.shape[1]
    feed_width = feed_gate.shape[1]
    places = (jnp.arange(group_rows, dtype=jnp.int32) + half_index * own) % group_rows
    live_mask, restart = group_layout(
        sequence_lengths,
        sequence_group,
        sequence_offset,
        which_group,
        places[:, None],
        group_rows // SPAN,
    )
    live = live_mask[:, None]
    scal = jnp.concatenate([half_index.astype(jnp.int32)[None], restart])
    sums = jnp.asarray(np.tile(decay_sums(), (1, 2)), bf16)
    gain_head = head_gain.astype(f32)[None, :]

    joined = lax.all_gather(
        jnp.concatenate([query_weight, key_weight, value_weight, output_gate], axis=1),
        "dp",
        axis=0,
        tiled=True,
    )
    feed_all = lax.all_gather(
        jnp.concatenate([feed_gate, feed_up, feed_down, output_weight], axis=1),
        "dp",
        axis=0,
        tiled=True,
    )
    gate_up_full = feed_all[:, : 2 * feed_width]
    feed_down_full = feed_all[:, 2 * feed_width : 3 * feed_width]
    output_full = feed_all[:, 3 * feed_width :]

    gain_in = mixer_gain.astype(f32)
    token_values = tokens.astype(f32)
    normed_in, inverse_in = rms_forward(token_values, gain_in)
    normed_low = normed_in.astype(bf16)
    normed_all = jnp.concatenate([normed_low, swap_tensor(normed_low)], axis=0)
    cotangent_all = jnp.concatenate([cotangent, swap_tensor(cotangent)], axis=0)
    projected = nn(normed_all, joined)
    latent = nn(normed_all, decay_down)
    up_local = lax.dynamic_slice_in_dim(decay_up, half_index * key_width, key_width, 1).astype(f32)
    bias_local = lax.dynamic_slice_in_dim(decay_bias, half_index * key_width, key_width, 0)
    z = jnp.dot(latent, up_local, precision=highest) + bias_local.astype(f32)
    gated, mixture, states = mixer_forward(scal, projected, z, live, gain_head, sums)

    partial = nt(gated, output_full).astype(bf16)
    attended = partial[:own].astype(f32) + swap_tensor(partial[own:]).astype(f32)
    middle = token_values + attended
    gain_mid = feed_gain.astype(f32)
    normed_mid, inverse_mid = rms_forward(middle, gain_mid)
    mid_low = normed_mid.astype(bf16)
    mid_all = jnp.concatenate([mid_low, swap_tensor(mid_low)], axis=0)
    both = nn(mid_all, gate_up_full)
    gate_part = both[:, :feed_width]
    up_part = both[:, feed_width:]
    sigmoid_gate = jax.nn.sigmoid(gate_part)
    silu_gate = gate_part * sigmoid_gate
    hidden_low = (silu_gate * up_part).astype(bf16)
    fed_part = nt(hidden_low, feed_down_full).astype(bf16)
    fed = fed_part[:own].astype(f32) + swap_tensor(fed_part[own:]).astype(f32)
    output = (middle + fed).astype(bf16)

    upstream = cotangent.astype(f32)
    grad_hidden = nn(cotangent_all, feed_down_full)
    grad_gate_low = (
        grad_hidden * up_part * (sigmoid_gate + silu_gate * (1.0 - sigmoid_gate))
    ).astype(bf16)
    grad_up_low = (grad_hidden * silu_gate).astype(bf16)
    grad_both = jnp.concatenate([grad_gate_low, grad_up_low], axis=1)
    mid_part = nt(grad_both, gate_up_full).astype(bf16)
    grad_normed_mid = mid_part[:own].astype(f32) + swap_tensor(mid_part[own:]).astype(f32)
    grad_mid_in, grad_feed_gain = rms_backward(middle, inverse_mid, gain_mid, grad_normed_mid)
    grad_middle = upstream + grad_mid_in
    attended_low = grad_middle.astype(bf16)
    attended_all = jnp.concatenate([attended_low, swap_tensor(attended_low)], axis=0)
    feed_grads = jnp.concatenate(
        [
            tn(mid_all, grad_both).astype(bf16),
            tn(cotangent_all, hidden_low).astype(bf16),
            tn(attended_all, gated).astype(bf16),
        ],
        axis=1,
    )
    grad_gated = nn(attended_all, output_full)
    grad_gated, feed_grads = lax.optimization_barrier((grad_gated, feed_grads))
    grad_projected, grad_z, grad_gain_rows = mixer_backward(
        scal, projected, z, live, gain_head, sums, mixture, states, grad_gated
    )
    feed_sum = lax.psum_scatter(feed_grads, "dp", scatter_dimension=0, tiled=True).astype(f32)
    grad_joined = tn(normed_all, grad_projected).astype(bf16)
    joined_sum = lax.psum_scatter(grad_joined, "dp", scatter_dimension=0, tiled=True).astype(f32)

    grad_latent = lax.dot_general(
        grad_z, up_local, (((1,), (1,)), ((), ())), precision=highest, preferred_element_type=f32
    )
    grad_up_local = lax.dot_general(
        latent, grad_z, (((0,), (0,)), ((), ())), precision=highest, preferred_element_type=f32
    )
    grad_bias_local = jnp.sum(grad_z, axis=0)
    latent_high = grad_latent.astype(bf16)
    latent_rest = (grad_latent - latent_high.astype(f32)).astype(bf16)
    grad_down_parts = tn(normed_all, jnp.concatenate([latent_high, latent_rest], axis=1))
    low_rank = decay_down.shape[1]
    grad_decay_down = grad_down_parts[:, :low_rank] + grad_down_parts[:, low_rank:]
    from_latent = nt(latent_high, decay_down) + nt(latent_rest, decay_down)
    normed_part = (nt(grad_projected, joined) + from_latent).astype(bf16)
    grad_normed = normed_part[:own].astype(f32) + swap_tensor(normed_part[own:]).astype(f32)
    grad_in_part, grad_mixer_gain = rms_backward(token_values, inverse_in, gain_in, grad_normed)
    input_grad = grad_middle + grad_in_part

    up_full = lax.dynamic_update_slice_in_dim(
        jnp.zeros(decay_up.shape, f32), grad_up_local, half_index * key_width, 1
    )
    bias_full = lax.dynamic_update_slice_in_dim(
        jnp.zeros(decay_bias.shape, f32), grad_bias_local, half_index * key_width, 0
    )
    small = (
        grad_mixer_gain,
        grad_decay_down,
        up_full,
        bias_full,
        jnp.sum(grad_gain_rows, axis=0),
        grad_feed_gain,
    )
    flat = butterfly_sum(jnp.concatenate([part.reshape(-1, 128) for part in small], axis=0))
    small_sums = []
    row = 0
    for part in small:
        taken = part.size // 128
        small_sums.append(flat[row : row + taken].reshape(part.shape))
        row += taken
    return (
        output,
        input_grad,
        small_sums[0],
        joined_sum[:, :key_width],
        joined_sum[:, key_width : 2 * key_width],
        joined_sum[:, 2 * key_width : 2 * key_width + value_width],
        joined_sum[:, 2 * key_width + value_width :],
        feed_sum[:, 3 * feed_width :],
        small_sums[1],
        small_sums[2],
        small_sums[3],
        small_sums[4],
        small_sums[5],
        feed_sum[:, :feed_width],
        feed_sum[:, feed_width : 2 * feed_width],
        feed_sum[:, 2 * feed_width : 3 * feed_width],
    )


def solution(mesh):
    rows = P(("dp", "tensor"), None)
    weight = P("dp", "tensor")
    return jax.shard_map(
        on_device,
        mesh=mesh,
        in_specs=(rows, rows, P(), P(), P(), P())
        + (weight,) * 5
        + (P(), P(), P(), P(), P())
        + (weight,) * 3,
        out_specs=(rows, rows, P()) + (weight,) * 5 + (P(),) * 5 + (weight,) * 3,
        check_vma=False,
    )
```

time: 1740 us -> 553 us (0.32)
  waiting for transfers between devices: 995 us -> 368 us
  local copies, waits for them, and re-layouts: 242 us -> 22.3 us
  matrix products: 243 us -> 72.9 us
  other arithmetic: 152 us -> 21.9 us
  blocking collectives: 84.4 us -> 0 us
  Pallas kernels: 0 us -> 32.2 us
    reduce_scatter x11 -> x2, waiting for transfers between devices: 550 us -> 113 us  [the longest x1 113 us: on_device(): lax.psum_scatter(feed_grads, 'dp', scatter_dimension=0, tiled=True)]
    all_gather x10 -> x2, waiting for transfers between devices: 275 us -> 80.5 us  [the longest x1 61.8 us: on_device(): lax.all_gather(jnp.concatenate([feed_gate, feed_up, feed_down, output_wei...]
    ppermute x0 -> x13, waiting for transfers between devices: none -> 175 us  [the longest x9 159 us: swap_tensor(): return lax.ppermute(values, 'tensor', [(0, 1), (1, 0)])]
    dot_general x84 -> x19, matrix products: 243 us -> 72.9 us  [the longest x5 28.7 us: nn(): lax.dot_general(left, right, (((1,), (0,)), ((), ())), preferred_element_...]
    unnamed x24 -> x4, waiting for transfers between devices: 90.9 us -> 0.36 us
    psum x1 -> x0, waiting for transfers between devices: 78.5 us -> none  [on_device(): lax.psum((grad_mixer_gain, grad_decay_down, up_grad_full, bias_grad_full,...]
    dynamic_update_slice x41 -> x0, other arithmetic: 47 us -> none  [the longest x32 33.7 us: span_mixer(): lax.scan(advance, start_memory, (jnp.exp(last_sum), span_add, 1.0 - resta...]
    all_gather x2 -> x0, blocking collectives: 43.9 us -> none  [the longest x1 24.7 us: on_device(): lax.all_gather(query_weight, 'dp', axis=0, tiled=True)]
  transfers between devices with their start and end apart: 23 -> 17, of which waited for: 19 -> 16; matrix products, arithmetic and copies ran while one was open for 15% -> 10% of each run, Pallas kernels for 0% -> 2%
where the time goes in v1:
time: 553 us; the launch traced here: 549 us
  waiting for transfers between devices  368 us (67%)
  matrix products  72.9 us (13%)
  Pallas kernels  32.2 us (6%)
  local copies, waits for them, and re-layouts  22.3 us (4%)
  other arithmetic  21.9 us (4%)
  starting transfers between devices  16.6 us (3%)
  between operations  14.5 us (3%)
    ppermute x9, waiting for transfers between devices, swap_tensor(): return lax.ppermute(values, 'tensor', [(0, 1), (1, 0)])  159 us
    reduce_scatter x1, waiting for transfers between devices, on_device(): lax.psum_scatter(feed_grads, 'dp', scatter_dimension=0, tiled=True)  113 us
    all_gather x1, waiting for transfers between devices, on_device(): lax.all_gather(jnp.concatenate([feed_gate, feed_up, feed_down, output_wei...  61.8 us
    dot_general x5, matrix products, nn(): lax.dot_general(left, right, (((1,), (0,)), ((), ())), preferred_element_...  28.7 us
    dot_general x6, matrix products, nt(): lax.dot_general(left, right, (((1,), (1,)), ((), ())), preferred_element_...  23.4 us
    pallas_call x1, Pallas kernels, mixer_backward(): pl.pallas_call(functools.partial(backward_kernel, heads), grid_spec=pltpu...  20.6 us
    dot_general x5, matrix products, tn(): lax.dot_general(left, right, (((0,), (0,)), ((), ())), preferred_element_...  19 us
    all_gather x1, waiting for transfers between devices, on_device(): lax.all_gather(jnp.concatenate([query_weight, key_weight, value_weight, o...  18.7 us
  transfers between devices with their start and end apart: 17, of which 16 were waited for; matrix products, arithmetic and copies ran while one was open for 10% of the time, Pallas kernels for 2%

profile of v1, /device:TPU:0, one launch (start us, length us, event | category | flops | bytes accessed | tf_op | source)
XLA Modules:
  0.0 548.8 jit_solution(13881005538475924139)
XLA Ops:
  16.2 22.4 %collective-permute-done = bf16[512,1024]{1,0:T(8,128)(2,1)S(1)} collective-permute-done((bf16[512,1024]{1,0:T(8,128)(2,1)S(1)}, bf16[512,1024]{1,0:T(8,128)(2,1)S(1)}, u32[]{:S(2)}, u32[]{:S(2)}) %collective-permute-start) | collective-permute-done | bytes 1048608 | tf_op jit(solution)/shard_map/ppermute | solution.py:338
  40.9 18.7 %all-gather.3.cloned.1.call-done = bf16[1024,1536]{1,0:T(8,128)(2,1)} async-done(((bf16[64,1536]{1,0:T(8,128)(2,1)}), bf16[1024,1536]{1,0:T(8,128)(2,1)}) %all-gather.3.cloned.1.call-update) | async-done | bytes 3145744 | tf_op jit(solution)/shard_map/all_gather | solution.py:393
  59.6 5.6 %fusion.51.projected = f32[1024,1536]{1,0:T(8,128)S(1)} fusion(bf16[1024,1536]{1,0:T(8,128)(2,1)} %all-gather.3.cloned.1.call-done, bf16[512,1024]{1,0:T(8,128)(2,1)} %copy-done.25, bf16[512,1024]{1,0:T(8,128)(2,1)S(1)} %fusion.10), kind=kOutput, calls=%fused_computation.104 | convolution fusion | flops 3225419776 | bytes 11534336 | tf_op jit(solution)/shard_map/dot_general | solution.py:54
  65.2 11.6 %mixer_forward.1 = (bf16[1024,512]{1,0:T(8,128)(2,1)S(1)}, f32[1024,512]{1,0:T(8,128)S(1)}, bf16[16,2,256,128]{3,2,1,0:T(8,128)(2,1)S(1)}) custom-call(s32[17]{0:T(128)S(1)} %pad_add_fusion.scal, f32[1024,1536]{1,0:T(8,128)S(1)} %fusion.51.projected, f32[1024,256]{1,0:T(8,128)S(1)} %convolution_add_fusion.z, f32[1024,1]{1,0:T(8,128)S(1)} %copy.42.live, ...), custom_call_target="tpu_custom_call" | custom-call | flops 10000000000 | bytes 15000000 | tf_op jit(solution)/shard_map/mixer_forward/pallas_call | solution.py:286
  82.2 61.8 %all-gather.5.cloned.1.call-done = bf16[1024,4736]{1,0:T(8,128)(2,1)} async-done(((bf16[64,4736]{1,0:T(8,128)(2,1)}), bf16[1024,4736]{1,0:T(8,128)(2,1)}) %all-gather.5.cloned.1.call-update) | async-done | bytes 9699344 | tf_op jit(solution)/shard_map/all_gather | solution.py:399
  148.9 23.9 %collective-permute-done.1 = bf16[512,1024]{1,0:T(8,128)(2,1)S(1)} collective-permute-done((bf16[512,1024]{1,0:T(8,128)(2,1)S(1)}, bf16[512,1024]{1,0:T(8,128)(2,1)S(1)}, u32[]{:S(2)}, u32[]{:S(2)}) %collective-permute-start.1) | collective-permute-done | bytes 1048608 | tf_op jit(solution)/shard_map/ppermute | solution.py:338
  175.3 20.0 %collective-permute-done.4 = bf16[512,1024]{1,0:T(8,128)(2,1)S(1)} collective-permute-done((bf16[512,1024]{1,0:T(8,128)(2,1)S(1)}, bf16[512,1024]{1,0:T(8,128)(2,1)S(1)}, u32[]{:S(2)}, u32[]{:S(2)}) %collective-permute-start.4) | collective-permute-done | bytes 1048608 | tf_op jit(solution)/shard_map/ppermute | solution.py:338
  195.4 21.7 %collective-permute-done.2 = bf16[512,1024]{1,0:T(8,128)(2,1)S(1)} collective-permute-done((bf16[512,1024]{1,0:T(8,128)(2,1)S(1)}, bf16[512,1024]{1,0:T(8,128)(2,1)S(1)}, u32[]{:S(2)}, u32[]{:S(2)}) %collective-permute-start.2) | collective-permute-done | bytes 1048608 | tf_op jit(solution)/shard_map/ppermute | solution.py:338
  217.1 9.6 %fusion.2 = f32[1024,2816]{1,0:T(8,128)} fusion(bf16[1024,4736]{1,0:T(8,128)(2,1)S(1)} %bitcast.42, bf16[512,1024]{1,0:T(8,128)(2,1)S(1)} %collective-permute-done.2, bf16[512,1024]{1,0:T(8,128)(2,1)S(1)} %multiply_convert_fusion.3), kind=kOutput, calls=%fused_computation.10 | convolution fusion | flops 5909774336 | bytes 19398656 | tf_op jit(solution)/shard_map/dot_general | solution.py:54
  226.8 9.9 %multiply_convert_fusion.1 = (bf16[1024,1408]{1,0:T(8,128)(2,1)}, bf16[1024,1408]{1,0:T(8,128)(2,1)}, bf16[1024,1408]{1,0:T(8,128)(2,1)}) fusion(f32[1024,2816]{1,0:T(8,128)} %fusion.2, bf16[1024,1024]{1,0:T(8,128)(2,1)S(1)} %constant_dynamic-update-slice_fusion, bf16[1024,4736]{1,0:T(8,128)(2,1)S(1)} %bitcast.42), kind=kOutput, calls=%fused_computation.3 | convolution fusion | flops 2972975104 | bytes 25165824 | tf_op jit(solution)/shard_map/dot_general | solution.py:54
  236.7 8.2 %fusion.19 = bf16[1024,1024]{1,0:T(8,128)(2,1)S(1)} fusion(bf16[1024,4736]{1,0:T(8,128)(2,1)S(1)} %bitcast.42, bf16[1024,1408]{1,0:T(8,128)(2,1)} %get-tuple-element.75, bf16[1024,1408]{1,0:T(8,128)(2,1)} %get-tuple-element.74), kind=kOutput, calls=%fused_computation.47 | convolution fusion | flops 5918162944 | bytes 13631488 | tf_op jit(solution)/shard_map/dot_general | solution.py:58
  246.5 5.6 %fusion.22 = bf16[1024,1024]{1,0:T(8,128)(2,1)S(1)} fusion(bf16[1024,1408]{1,0:T(8,128)(2,1)} %get-tuple-element.76, bf16[1024,4736]{1,0:T(8,128)(2,1)S(1)} %bitcast.42), kind=kOutput, calls=%fused_computation.48 | convolution fusion | flops 2953838592 | bytes 7864320 | tf_op jit(solution)/shard_map/dot_general | solution.py:58
  256.7 14.4 %collective-permute-done.5 = bf16[512,1024]{1,0:T(8,128)(2,1)S(1)} collective-permute-done((bf16[512,1024]{1,0:T(8,128)(2,1)S(1)}, bf16[512,1024]{1,0:T(8,128)(2,1)S(1)}, u32[]{:S(2)}, u32[]{:S(2)}) %collective-permute-start.5) | collective-permute-done | bytes 1048608 | tf_op jit(solution)/shard_map/ppermute | solution.py:338
  271.9 20.1 %collective-permute-done.3 = bf16[512,1024]{1,0:T(8,128)(2,1)S(1)} collective-permute-done((bf16[512,1024]{1,0:T(8,128)(2,1)S(1)}, bf16[512,1024]{1,0:T(8,128)(2,1)S(1)}, u32[]{:S(2)}, u32[]{:S(2)}) %collective-permute-start.3) | collective-permute-done | bytes 1048608 | tf_op jit(solution)/shard_map/ppermute | solution.py:338
  295.9 8.4 %convolution_convert_fusion = bf16[1024,2816]{1,0:T(8,128)(2,1)S(1)} fusion(bf16[1024,1408]{1,0:T(8,128)(2,1)} %get-tuple-element.75, bf16[1024,1408]{1,0:T(8,128)(2,1)S(1)} %copy-done.30, bf16[512,1024]{1,0:T(8,128)(2,1)S(1)} %collective-permute-done.2, bf16[512,1024]{1,0:T(8,128)(2,1)S(1)} %multiply_convert_fusion.3), kind=kOutput, calls=%fused_computation.6 | convolution fusion | flops 5924192256 | bytes 13631488 | tf_op jit(solution)/shard_map/dot_general | solution.py:62
  304.4 13.7 %collective-permute-done.6 = bf16[512,1024]{1,0:T(8,128)(2,1)S(1)} collective-permute-done((bf16[512,1024]{1,0:T(8,128)(2,1)S(1)}, bf16[512,1024]{1,0:T(8,128)(2,1)S(1)}, u32[]{:S(2)}, u32[]{:S(2)}) %collective-permute-start.6) | collective-permute-done | bytes 1048608 | tf_op jit(solution)/shard_map/ppermute | solution.py:338
  319.4 5.6 %pad_maximum_fusion = bf16[1024,4736]{1,0:T(8,128)(2,1)} fusion(bf16[1024,512]{1,0:T(8,128)(2,1)S(1)} %convolution_convert_fusion.4, bf16[1024,1408]{1,0:T(8,128)(2,1)S(1)} %convolution_convert_fusion.2, bf16[1024,2816]{1,0:T(8,128)(2,1)S(1)} %convolution_convert_fusion), kind=kLoop, calls=%fused_computation | loop fusion | flops 29097984 | bytes 19398656 | tf_op jit(solution)/shard_map/concatenate | solution.py:452
  327.9 20.6 %mixer_backward.1 = (bf16[1024,1536]{1,0:T(8,128)(2,1)S(1)}, f32[1024,256]{1,0:T(8,128)S(1)}, f32[8,256]{1,0:T(8,128)S(1)}) custom-call(s32[17]{0:T(128)S(1)} %pad_add_fusion.scal, f32[1024,1536]{1,0:T(8,128)} %copy-done.2, f32[1024,256]{1,0:T(8,128)S(1)} %convolution_add_fusion.z, f32[1024,1]{1,0:T(8,128)S(1)} %copy.42.live, f32[1,256]{1,0:T(1,128)S(1)} %bitcast.35, ...), custom_call_target="tpu_custom_call" | custom-call | flops 24999999488 | bytes 20000000 | tf_op jit(solution)/shard_map/mixer_backward/pallas_call | solution.py:315
  350.2 4.9 convolution_convert_fusion.1
  357.6 5.5 fusion.56
  369.4 19.5 %collective-permute-done.7 = bf16[512,1024]{1,0:T(8,128)(2,1)} collective-permute-done((bf16[512,1024]{1,0:T(8,128)(2,1)}, bf16[512,1024]{1,0:T(8,128)(2,1)}, u32[]{:S(2)}, u32[]{:S(2)}) %collective-permute-start.7) | collective-permute-done | bytes 1048608 | tf_op jit(solution)/shard_map/ppermute | solution.py:338
  398.4 4.6 collective-permute-done.10
  413.5 6.0 %collective-permute-done.12 = f32[214,128]{1,0:T(8,128)S(1)} collective-permute-done((f32[214,128]{1,0:T(8,128)S(1)}, f32[214,128]{1,0:T(8,128)S(1)}, u32[]{:S(2)}, u32[]{:S(2)}) %collective-permute-start.12) | collective-permute-done | bytes 109600 | tf_op jit(solution)/shard_map/ppermute | solution.py:346
  425.9 112.5 %reduce-scatter.5.cloned.1.call-done = bf16[64,4736]{1,0:T(8,128)(2,1)} async-done(((bf16[1024,4736]{1,0:T(8,128)(2,1)}), bf16[64,4736]{1,0:T(8,128)(2,1)}) %reduce-scatter.5.cloned.1.call-update) | async-done | bytes 606224 | tf_op jit(solution)/shard_map/reduce_scatter | solution.py:465
  (167 shorter events, 79.4 us)
Async XLA Ops:
  7.2 32.4 %copy-start = (bf16[1024,16]{0,1:T(8,128)(2,1)S(1)}, bf16[1024,16]{0,1:T(8,128)(2,1)}, u32[]{:S(2)}) copy-start(bf16[1024,16]{0,1:T(8,128)(2,1)} %param.31) | copy-start | bytes 98308
  7.2 52.4 %all-gather.3.cloned.1.call-start = ((), (), s32[]{:S(2)}) async-start(), calls=%async_computation.2 | async-start | bytes 3342336 | tf_op jit(solution)/shard_map/all_gather | solution.py:393
  9.0 135.1 %all-gather.5.cloned.1.call-start = ((), (), s32[]{:S(2)}) async-start(), calls=%async_computation.3 | async-start | bytes 10305536 | tf_op jit(solution)/shard_map/all_gather | solution.py:399
  11.0 411.9 %reduce-scatter.3.cloned.1.call-start = ((), (), s32[]{:S(2)}) async-start(), calls=%async_computation.4 | async-start | bytes 3342336 | tf_op jit(solution)/shard_map/reduce_scatter | solution.py:467
  12.1 28.1 %copy-start.19 = (bf16[16,512]{1,0:T(8,128)(2,1)S(1)}, bf16[16,512]{1,0:T(8,128)(2,1)}, u32[]{:S(2)}) copy-start(bf16[16,512]{1,0:T(8,128)(2,1)} %param.32) | copy-start | bytes 49156
  12.4 52.8 %copy-start.14 = (bf16[512,1024]{1,0:T(8,128)(2,1)}, bf16[512,1024]{1,0:T(8,128)(2,1)S(1)}, u32[]{:S(2)}) copy-start(bf16[512,1024]{1,0:T(8,128)(2,1)S(1)} %fusion.10) | copy-start | bytes 3145732
  12.4 26.2 %collective-permute-start = (bf16[512,1024]{1,0:T(8,128)(2,1)S(1)}, bf16[512,1024]{1,0:T(8,128)(2,1)S(1)}, u32[]{:S(2)}, u32[]{:S(2)}) collective-permute-start(bf16[512,1024]{1,0:T(8,128)(2,1)S(1)} %fusion.10), channel_id=1, source_target_pairs={{0,1},{1,0},{2,3},{3,2},{4,5},{5,4},{6,7},{7,6},{8,9},{9,8},{10,11... | collective-permute-start | bytes 3145736 | tf_op jit(solution)/shard_map/ppermute | solution.py:338
  144.0 28.8 %copy-start.10 = (bf16[512,1024]{1,0:T(8,128)(2,1)S(1)}, bf16[512,1024]{1,0:T(8,128)(2,1)}, u32[]{:S(2)}) copy-start(bf16[512,1024]{1,0:T(8,128)(2,1)} %param.20) | copy-start | bytes 3145732
  144.0 73.1 %slice-start = ((s8[9699328]{0:T(1024)(128)(4,1)}), s8[4194304]{0:T(1024)(128)(4,1)S(1)}, s32[]{:S(2)}) async-start(s8[9699328]{0:T(1024)(128)(4,1)} %bitcast.41), calls=%async_computation.6 | async-start | bytes 8388608
  144.0 73.1 %slice-start.1 = ((s8[9699328]{0:T(1024)(128)(4,1)}), s8[4194304]{0:T(1024)(128)(4,1)S(1)}, s32[]{:S(2)}) async-start(s8[9699328]{0:T(1024)(128)(4,1)} %bitcast.41), calls=%async_computation.7 | async-start | bytes 8388608
  146.8 26.1 %collective-permute-start.1 = (bf16[512,1024]{1,0:T(8,128)(2,1)S(1)}, bf16[512,1024]{1,0:T(8,128)(2,1)S(1)}, u32[]{:S(2)}, u32[]{:S(2)}) collective-permute-start(bf16[512,1024]{1,0:T(8,128)(2,1)S(1)} %slice.118), channel_id=1, source_target_pairs={{0,1},{1,0},{2,3},{3,2},{4,5},{5,4},{6,7},{7,6},{8,9},{9,8},{10,11... | collective-permute-start | bytes 3145736 | tf_op jit(solution)/shard_map/ppermute | solution.py:338
  148.3 47.0 %collective-permute-start.4 = (bf16[512,1024]{1,0:T(8,128)(2,1)S(1)}, bf16[512,1024]{1,0:T(8,128)(2,1)S(1)}, u32[]{:S(2)}, u32[]{:S(2)}) collective-permute-start(bf16[512,1024]{1,0:T(8,128)(2,1)S(1)} %copy-done.13), channel_id=1, source_target_pairs={{0,1},{1,0},{2,3},{3,2},{4,5},{5,4},{6,7},{7,6},{8,9},{9,8},{10,11... | collective-permute-start | bytes 3145736 | tf_op jit(solution)/shard_map/ppermute | solution.py:338
  148.9 68.2 %slice-start.2 = ((s8[9699328]{0:T(1024)(128)(4,1)}), s8[1310720]{0:T(1024)(128)(4,1)S(1)}, s32[]{:S(2)}) async-start(s8[9699328]{0:T(1024)(128)(4,1)} %bitcast.41), calls=%async_computation.8 | async-start | bytes 2621440
  173.6 43.5 %collective-permute-start.2 = (bf16[512,1024]{1,0:T(8,128)(2,1)S(1)}, bf16[512,1024]{1,0:T(8,128)(2,1)S(1)}, u32[]{:S(2)}, u32[]{:S(2)}) collective-permute-start(bf16[512,1024]{1,0:T(8,128)(2,1)S(1)} %multiply_convert_fusion.3), channel_id=1, source_target_pairs={{0,1},{1,0},{2,3},{3,2},{4,5},{5,4},{6,7},{7,6},{8,9},{9,8},{10,11... | collective-permute-start | bytes 3145736 | tf_op jit(solution)/shard_map/ppermute | solution.py:338
  244.9 26.2 %collective-permute-start.5 = (bf16[512,1024]{1,0:T(8,128)(2,1)S(1)}, bf16[512,1024]{1,0:T(8,128)(2,1)S(1)}, u32[]{:S(2)}, u32[]{:S(2)}) collective-permute-start(bf16[512,1024]{1,0:T(8,128)(2,1)S(1)} %slice.126), channel_id=1, source_target_pairs={{0,1},{1,0},{2,3},{3,2},{4,5},{5,4},{6,7},{7,6},{8,9},{9,8},{10,11... | collective-permute-start | bytes 3145736 | tf_op jit(solution)/shard_map/ppermute | solution.py:338
  252.2 39.8 %collective-permute-start.3 = (bf16[512,1024]{1,0:T(8,128)(2,1)S(1)}, bf16[512,1024]{1,0:T(8,128)(2,1)S(1)}, u32[]{:S(2)}, u32[]{:S(2)}) collective-permute-start(bf16[512,1024]{1,0:T(8,128)(2,1)S(1)} %slice.124), channel_id=1, source_target_pairs={{0,1},{1,0},{2,3},{3,2},{4,5},{5,4},{6,7},{7,6},{8,9},{9,8},{10,11... | collective-permute-start | bytes 3145736 | tf_op jit(solution)/shard_map/ppermute | solution.py:338
  294.4 23.6 %collective-permute-start.6 = (bf16[512,1024]{1,0:T(8,128)(2,1)S(1)}, bf16[512,1024]{1,0:T(8,128)(2,1)S(1)}, u32[]{:S(2)}, u32[]{:S(2)}) collective-permute-start(bf16[512,1024]{1,0:T(8,128)(2,1)S(1)} %get-tuple-element.70), channel_id=1, source_target_pairs={{0,1},{1,0},{2,3},{3,2},{4,5},{5,4},{6,7},{7,6},{8,9},{9,8},{10,11... | collective-permute-start | bytes 3145736 | tf_op jit(solution)/shard_map/ppermute | solution.py:338
  355.1 183.4 %reduce-scatter.5.cloned.1.call-start = ((), (), s32[]{:S(2)}) async-start(), calls=%async_computation.5 | async-start | bytes 10305536 | tf_op jit(solution)/shard_map/reduce_scatter | solution.py:465
  366.1 22.8 %collective-permute-start.7 = (bf16[512,1024]{1,0:T(8,128)(2,1)}, bf16[512,1024]{1,0:T(8,128)(2,1)}, u32[]{:S(2)}, u32[]{:S(2)}) collective-permute-start(bf16[512,1024]{1,0:T(8,128)(2,1)} %slice.128), channel_id=1, source_target_pairs={{0,1},{1,0},{2,3},{3,2},{4,5},{5,4},{6,7},{7,6},{8,9},{9,8},{10,11... | collective-permute-start | bytes 3145736 | tf_op jit(solution)/shard_map/ppermute | solution.py:338
  391.5 4.8 collective-permute-start.8
  396.4 1.4 collective-permute-start.9
  397.8 5.2 collective-permute-start.10
  403.0 4.8 collective-permute-start.11
  407.8 11.7 %collective-permute-start.12 = (f32[214,128]{1,0:T(8,128)S(1)}, f32[214,128]{1,0:T(8,128)S(1)}, u32[]{:S(2)}, u32[]{:S(2)}) collective-permute-start(f32[214,128]{1,0:T(8,128)S(1)} %add.142), channel_id=1, source_target_pairs={{0,16},{2,18},{4,20},{6,22},{8,24},{10,26},{12,28},{14,30},{16,0},... | collective-permute-start | bytes 328712 | tf_op jit(solution)/shard_map/ppermute | solution.py:346
  (28 other events, 211.4 us)
Sparse Core Ops, SparseCore 0:
  10.9 48.6 all-gather.2
  62.5 81.5 all-gather.4
  355.2 66.9 reduce-scatter.2
  426.2 112.1 reduce-scatter.4

commit v2 on v1

--- a/solution.py
+++ b/solution.py
@@ -122,11 +122,11 @@
         keep = jnp.where(scal[1 + step * STEP_SPANS + part] == 0, 1.0, 0.0)
         for head in range(heads):
             keys_at = slice(head * KDIM, (head + 1) * KDIM)
-            queries = projected[rows, keys_at]
-            keys = projected[rows, key_width + head * KDIM : key_width + (head + 1) * KDIM]
+            queries = projected[rows, keys_at].astype(f32)
+            keys = projected[rows, key_width + head * KDIM : key_width + (head + 1) * KDIM].astype(f32)
             value_at = 2 * key_width + head * VDIM
-            values = projected[rows, value_at : value_at + VDIM].astype(bf16)
-            gating = projected[rows, value_at + value_width : value_at + value_width + VDIM]
+            values = projected[rows, value_at : value_at + VDIM]
+            gating = projected[rows, value_at + value_width : value_at + value_width + VDIM].astype(f32)
             factors = factors_all[:, keys_at]
             scores, _, _ = span_scores(queries, keys, factors, masks, diagonal)
             entering = state[head] * keep
@@ -139,7 +139,7 @@
             )
             state[head] = entering * whole[SPAN - 1 :] + tn(values, (keys * after).astype(bf16))
             value_cols = slice(head * VDIM, (head + 1) * VDIM)
-            mixture[rows, value_cols] = mixed
+            mixture[rows, value_cols] = mixed.astype(bf16)
             inverse = lax.rsqrt(jnp.mean(mixed * mixed, axis=-1, keepdims=True) + head_epsilon)
             silu = gating * jax.nn.sigmoid(gating)
             gated[rows, value_cols] = (mixed * inverse * head_gain * silu * live[rows, :]).astype(bf16)
@@ -188,22 +188,22 @@
             value_cols = slice(value_at, value_at + VDIM)
             gate_cols = slice(value_at + value_width, value_at + value_width + VDIM)
             mixed_cols = slice(head * VDIM, (head + 1) * VDIM)
-            queries = projected[rows, keys_at]
-            keys = projected[rows, key_cols]
-            values = projected[rows, value_cols].astype(bf16)
-            gating = projected[rows, gate_cols]
+            queries = projected[rows, keys_at].astype(f32)
+            keys = projected[rows, key_cols].astype(f32)
+            values = projected[rows, value_cols]
+            gating = projected[rows, gate_cols].astype(f32)
             factors = factors_all[:, keys_at]
             scores, query_levels, key_levels = span_scores(queries, keys, factors, masks, diagonal)
             scores_low = scores.astype(bf16)
             whole = factors[:SPAN]
             after = factors[(KINDS - 1) * SPAN :]
 
-            mixed = mixture[rows, mixed_cols]
+            mixed = mixture[rows, mixed_cols].astype(f32)
             inverse = lax.rsqrt(jnp.mean(mixed * mixed, axis=-1, keepdims=True) + head_epsilon)
             unit = mixed * inverse
             sigmoid = jax.nn.sigmoid(gating)
             silu = gating * sigmoid
-            upstream = grad_gated[rows, mixed_cols] * live_part
+            upstream = grad_gated[rows, mixed_cols].astype(f32) * live_part
             grad_projected[rows, gate_cols] = (
                 upstream * unit * head_gain * (sigmoid + silu * (1.0 - sigmoid))
             ).astype(bf16)
@@ -294,7 +294,7 @@
         ),
         out_shape=[
             jax.ShapeDtypeStruct((length, value_width), bf16),
-            jax.ShapeDtypeStruct((length, value_width), f32),
+            jax.ShapeDtypeStruct((length, value_width), bf16),
             jax.ShapeDtypeStruct((spans, heads, VDIM, KDIM), bf16),
         ],
         compiler_params=pltpu.CompilerParams(vmem_limit_bytes=40 * 1024 * 1024),
@@ -336,6 +336,25 @@
 
 def swap_tensor(values):
     return lax.ppermute(values, "tensor", [(0, 1), (1, 0)])
+
+
+def chip_sum(values):
+    count = lax.axis_size("dp")
+    parity = lax.axis_index("dp") % 2
+    blocks = values.reshape(count // 2, 2, values.shape[0] // count, values.shape[1])
+    kept = lax.dynamic_index_in_dim(blocks, parity, 1, keepdims=False)
+    sent = lax.dynamic_index_in_dim(blocks, 1 - parity, 1, keepdims=False)
+    arrived = lax.ppermute(sent, "dp", [(i, i ^ 1) for i in range(count)])
+    total = (kept.astype(f32) + arrived.astype(f32)).astype(bf16)
+    return total.reshape(values.shape[0] // 2, values.shape[1])
+
+
+def chips_scatter(values):
+    count = lax.axis_size("dp")
+    groups = [list(range(parity, count, 2)) for parity in range(2)]
+    return lax.psum_scatter(
+        values, "dp", scatter_dimension=0, axis_index_groups=groups, tiled=True
+    )
 
 
 def butterfly_sum(values):
@@ -391,80 +410,101 @@
     gain_head = head_gain.astype(f32)[None, :]
 
     joined = lax.all_gather(
-        jnp.concatenate([query_weight, key_weight, value_weight, output_gate], axis=1),
+        jnp.concatenate(
+            [query_weight, key_weight, value_weight, output_gate, output_weight], axis=1
+        ),
         "dp",
         axis=0,
         tiled=True,
     )
     feed_all = lax.all_gather(
-        jnp.concatenate([feed_gate, feed_up, feed_down, output_weight], axis=1),
-        "dp",
-        axis=0,
-        tiled=True,
-    )
-    gate_up_full = feed_all[:, : 2 * feed_width]
-    feed_down_full = feed_all[:, 2 * feed_width : 3 * feed_width]
-    output_full = feed_all[:, 3 * feed_width :]
-
+        jnp.concatenate([feed_gate, feed_up, feed_down], axis=1), "dp", axis=0, tiled=True
+    )
     gain_in = mixer_gain.astype(f32)
     token_values = tokens.astype(f32)
     normed_in, inverse_in = rms_forward(token_values, gain_in)
     normed_low = normed_in.astype(bf16)
-    normed_all = jnp.concatenate([normed_low, swap_tensor(normed_low)], axis=0)
-    cotangent_all = jnp.concatenate([cotangent, swap_tensor(cotangent)], axis=0)
-    projected = nn(normed_all, joined)
+    normed_other = swap_tensor(normed_low)
+    normed_other, cotangent_low = lax.optimization_barrier((normed_other, cotangent))
+    cotangent_other = swap_tensor(cotangent_low)
+    joined, cotangent_other = lax.optimization_barrier((joined, cotangent_other))
+    projected_width = 2 * key_width + 2 * value_width
+    joined_in = joined[:, :projected_width]
+    output_full = joined[:, projected_width:]
+    gate_up_full = feed_all[:, : 2 * feed_width]
+    feed_down_full = feed_all[:, 2 * feed_width :]
+
+    normed_all = jnp.concatenate([normed_low, normed_other], axis=0)
+    projected = nn(normed_all, joined_in).astype(bf16)
     latent = nn(normed_all, decay_down)
     up_local = lax.dynamic_slice_in_dim(decay_up, half_index * key_width, key_width, 1).astype(f32)
     bias_local = lax.dynamic_slice_in_dim(decay_bias, half_index * key_width, key_width, 0)
     z = jnp.dot(latent, up_local, precision=highest) + bias_local.astype(f32)
     gated, mixture, states = mixer_forward(scal, projected, z, live, gain_head, sums)
 
-    partial = nt(gated, output_full).astype(bf16)
-    attended = partial[:own].astype(f32) + swap_tensor(partial[own:]).astype(f32)
-    middle = token_values + attended
+    attended_other = swap_tensor(nt(gated[own:], output_full).astype(bf16))
+    attended_own = nt(gated[:own], output_full)
+    middle = token_values + (attended_own + attended_other.astype(f32))
     gain_mid = feed_gain.astype(f32)
     normed_mid, inverse_mid = rms_forward(middle, gain_mid)
     mid_low = normed_mid.astype(bf16)
-    mid_all = jnp.concatenate([mid_low, swap_tensor(mid_low)], axis=0)
-    both = nn(mid_all, gate_up_full)
-    gate_part = both[:, :feed_width]
-    up_part = both[:, feed_width:]
-    sigmoid_gate = jax.nn.sigmoid(gate_part)
-    silu_gate = gate_part * sigmoid_gate
-    hidden_low = (silu_gate * up_part).astype(bf16)
-    fed_part = nt(hidden_low, feed_down_full).astype(bf16)
-    fed = fed_part[:own].astype(f32) + swap_tensor(fed_part[own:]).astype(f32)
-    output = (middle + fed).astype(bf16)
+    mid_other = swap_tensor(mid_low)
+
+    def feed_rows(mid_rows, cotangent_rows):
+        both = nn(mid_rows, gate_up_full)
+        gate_part = both[:, :feed_width]
+        up_part = both[:, feed_width:]
+        sigmoid_gate = jax.nn.sigmoid(gate_part)
+        silu_gate = gate_part * sigmoid_gate
+        hidden_low = (silu_gate * up_part).astype(bf16)
+        grad_hidden = nn(cotangent_rows, feed_down_full)
+        grad_gate_low = (
+            grad_hidden * up_part * (sigmoid_gate + silu_gate * (1.0 - sigmoid_gate))
+        ).astype(bf16)
+        grad_up_low = (grad_hidden * silu_gate).astype(bf16)
+        grad_both = jnp.concatenate([grad_gate_low, grad_up_low], axis=1)
+        return hidden_low, grad_both, nt(grad_both, gate_up_full)
+
+    hidden_own, grad_both_own, mid_back_own = feed_rows(mid_low, cotangent)
+    hidden_other, grad_both_other, mid_back_other = feed_rows(mid_other, cotangent_other)
+    mid_back = swap_tensor(mid_back_other.astype(bf16))
 
     upstream = cotangent.astype(f32)
-    grad_hidden = nn(cotangent_all, feed_down_full)
-    grad_gate_low = (
-        grad_hidden * up_part * (sigmoid_gate + silu_gate * (1.0 - sigmoid_gate))
-    ).astype(bf16)
-    grad_up_low = (grad_hidden * silu_gate).astype(bf16)
-    grad_both = jnp.concatenate([grad_gate_low, grad_up_low], axis=1)
-    mid_part = nt(grad_both, gate_up_full).astype(bf16)
-    grad_normed_mid = mid_part[:own].astype(f32) + swap_tensor(mid_part[own:]).astype(f32)
+    grad_normed_mid = mid_back_own + mid_back.astype(f32)
     grad_mid_in, grad_feed_gain = rms_backward(middle, inverse_mid, gain_mid, grad_normed_mid)
     grad_middle = upstream + grad_mid_in
-    attended_low = grad_middle.astype(bf16)
-    attended_all = jnp.concatenate([attended_low, swap_tensor(attended_low)], axis=0)
+    grad_attended = grad_middle.astype(bf16)
+    attended_back = swap_tensor(grad_attended)
+
+    mid_all = jnp.concatenate([mid_low, mid_other], axis=0)
+    cotangent_all = jnp.concatenate([cotangent, cotangent_other], axis=0)
+    hidden_all = jnp.concatenate([hidden_own, hidden_other], axis=0)
+    grad_both_all = jnp.concatenate([grad_both_own, grad_both_other], axis=0)
     feed_grads = jnp.concatenate(
         [
-            tn(mid_all, grad_both).astype(bf16),
-            tn(cotangent_all, hidden_low).astype(bf16),
-            tn(attended_all, gated).astype(bf16),
+            tn(mid_all, grad_both_all).astype(bf16),
+            tn(cotangent_all, hidden_all).astype(bf16),
         ],
         axis=1,
     )
-    grad_gated = nn(attended_all, output_full)
-    grad_gated, feed_grads = lax.optimization_barrier((grad_gated, feed_grads))
+    feed_chip = chip_sum(feed_grads)
+
+    attended_all = jnp.concatenate([grad_attended, attended_back], axis=0)
+    grad_gated = nn(attended_all, output_full).astype(bf16)
+    fed_send = nt(hidden_other, feed_down_full).astype(bf16)
+    grad_gated, feed_chip, fed_send = lax.optimization_barrier((grad_gated, feed_chip, fed_send))
+    fed = nt(hidden_own, feed_down_full) + swap_tensor(fed_send).astype(f32)
+    output = (middle + fed).astype(bf16)
+    feed_sum = chips_scatter(feed_chip)
     grad_projected, grad_z, grad_gain_rows = mixer_backward(
         scal, projected, z, live, gain_head, sums, mixture, states, grad_gated
     )
-    feed_sum = lax.psum_scatter(feed_grads, "dp", scatter_dimension=0, tiled=True).astype(f32)
-    grad_joined = tn(normed_all, grad_projected).astype(bf16)
-    joined_sum = lax.psum_scatter(grad_joined, "dp", scatter_dimension=0, tiled=True).astype(f32)
+    joined_grads = jnp.concatenate(
+        [tn(normed_all, grad_projected).astype(bf16), tn(attended_all, gated).astype(bf16)], axis=1
+    )
+    joined_chip, feed_sum = lax.optimization_barrier((chip_sum(joined_grads), feed_sum))
+    joined_sum = chips_scatter(joined_chip).astype(f32)
+    feed_sum = feed_sum.astype(f32)
 
     grad_latent = lax.dot_general(
         grad_z, up_local, (((1,), (1,)), ((), ())), precision=highest, preferred_element_type=f32
@@ -479,7 +519,7 @@
     low_rank = decay_down.shape[1]
     grad_decay_down = grad_down_parts[:, :low_rank] + grad_down_parts[:, low_rank:]
     from_latent = nt(latent_high, decay_down) + nt(latent_rest, decay_down)
-    normed_part = (nt(grad_projected, joined) + from_latent).astype(bf16)
+    normed_part = (nt(grad_projected, joined_in) + from_latent).astype(bf16)
     grad_normed = normed_part[:own].astype(f32) + swap_tensor(normed_part[own:]).astype(f32)
     grad_in_part, grad_mixer_gain = rms_backward(token_values, inverse_in, gain_in, grad_normed)
     input_grad = grad_middle + grad_in_part
@@ -512,8 +552,8 @@
         joined_sum[:, :key_width],
         joined_sum[:, key_width : 2 * key_width],
         joined_sum[:, 2 * key_width : 2 * key_width + value_width],
-        joined_sum[:, 2 * key_width + value_width :],
-        feed_sum[:, 3 * feed_width :],
+        joined_sum[:, 2 * key_width + value_width : projected_width],
+        joined_sum[:, projected_width:],
         small_sums[1],
         small_sums[2],
         small_sums[3],

time: 553 us -> 439 us (0.79)
  waiting for transfers between devices: 368 us -> 222 us
  matrix products: 72.9 us -> 96.3 us
    reduce_scatter x2, waiting for transfers between devices: 113 us -> 49.5 us  [chips_scatter(): lax.psum_scatter(values, 'dp', scatter_dimension=0, axis_index_groups=gro...]
    all_gather x1, waiting for transfers between devices: 61.8 us -> 29.2 us  [on_device(): lax.all_gather(jnp.concatenate([feed_gate, feed_up, feed_down], axis=1),...]
    ppermute x9, waiting for transfers between devices: 159 us -> 131 us  [swap_tensor(): return lax.ppermute(values, 'tensor', [(0, 1), (1, 0)])]
    all_gather x1, waiting for transfers between devices: 18.7 us -> 0.01 us  [on_device(): lax.all_gather(jnp.concatenate([query_weight, key_weight, value_weight, o...]
    dot_general x6 -> x9, matrix products: 23.4 us -> 35.2 us  [nt(): lax.dot_general(left, right, (((1,), (1,)), ((), ())), preferred_element_...]
    convert_element_type x1 -> x4, other arithmetic: 2.48 us -> 11.6 us  [the longest x2 7.6 us: chip_sum(): total = (kept.astype(f32) + arrived.astype(f32)).astype(bf16)]
    dot_general x5, matrix products: 19 us -> 26.7 us  [tn(): lax.dot_general(left, right, (((0,), (0,)), ((), ())), preferred_element_...]
    dot_general x5 -> x7, matrix products: 28.7 us -> 32.6 us  [nn(): lax.dot_general(left, right, (((1,), (0,)), ((), ())), preferred_element_...]
  transfers between devices with their start and end apart: 17 -> 19, of which waited for: 16 -> 13; matrix products, arithmetic and copies ran while one was open for 10% -> 22% of each run, Pallas kernels for 2% -> 7%
where the time goes in v2:
time: 439 us; the launch traced here: 435 us
  waiting for transfers between devices  222 us (51%)
  matrix products  96.3 us (22%)
  Pallas kernels  30.7 us (7%)
  local copies, waits for them, and re-layouts  26.9 us (6%)
  other arithmetic  25.7 us (6%)
  starting transfers between devices  17.9 us (4%)
  between operations  14.8 us (3%)
    ppermute x9, waiting for transfers between devices, swap_tensor(): return lax.ppermute(values, 'tensor', [(0, 1), (1, 0)])  131 us
    reduce_scatter x2, waiting for transfers between devices, chips_scatter(): lax.psum_scatter(values, 'dp', scatter_dimension=0, axis_index_groups=gro...  49.5 us
    dot_general x9, matrix products, nt(): lax.dot_general(left, right, (((1,), (1,)), ((), ())), preferred_element_...  35.2 us
    dot_general x7, matrix products, nn(): lax.dot_general(left, right, (((1,), (0,)), ((), ())), preferred_element_...  32.6 us
    all_gather x1, waiting for transfers between devices, on_device(): lax.all_gather(jnp.concatenate([feed_gate, feed_up, feed_down], axis=1),...  29.2 us
    dot_general x5, matrix products, tn(): lax.dot_general(left, right, (((0,), (0,)), ((), ())), preferred_element_...  26.7 us
    pallas_call x1, Pallas kernels, mixer_backward(): pl.pallas_call(functools.partial(backward_kernel, heads), grid_spec=pltpu...  19.3 us
    ppermute x9, starting transfers between devices, swap_tensor(): return lax.ppermute(values, 'tensor', [(0, 1), (1, 0)])  13.9 us
  transfers between devices with their start and end apart: 19, of which 13 were waited for; matrix products, arithmetic and copies ran while one was open for 22% of the time, Pallas kernels for 7%

profile of v2, /device:TPU:0, one launch (start us, length us, event | category | flops | bytes accessed | tf_op | source)
XLA Modules:
  0.0 434.6 jit_solution(16184676954491783157)
XLA Ops:
  20.3 23.3 %collective-permute-done = bf16[512,1024]{1,0:T(8,128)(2,1)} collective-permute-done((bf16[512,1024]{1,0:T(8,128)(2,1)}, bf16[512,1024]{1,0:T(8,128)(2,1)}, u32[]{:S(2)}, u32[]{:S(2)}) %collective-permute-start) | collective-permute-done | bytes 1048608 | tf_op jit(solution)/shard_map/ppermute | solution.py:338
  49.4 18.7 %collective-permute-done.1 = bf16[512,1024]{1,0:T(8,128)(2,1)} collective-permute-done((bf16[512,1024]{1,0:T(8,128)(2,1)S(1)}, bf16[512,1024]{1,0:T(8,128)(2,1)}, u32[]{:S(2)}, u32[]{:S(2)}) %collective-permute-start.1) | collective-permute-done | bytes 1048608 | tf_op jit(solution)/shard_map/ppermute | solution.py:338
  68.0 5.9 %convolution_convert_fusion.2.projected = bf16[1024,1536]{1,0:T(8,128)(2,1)S(1)} fusion(bf16[1024,2048]{1,0:T(8,128)(2,1)} %all-gather.3.cloned.1.call-done, bf16[512,1024]{1,0:T(8,128)(2,1)} %collective-permute-done, bf16[512,1024]{1,0:T(8,128)(2,1)} %fusion.35), kind=kOutput, calls=%fused_computation.25 | convolution fusion | flops 3226992640 | bytes 8388608 | tf_op jit(solution)/shard_map/dot_general | solution.py:54
  74.0 11.3 %mixer_forward.1 = (bf16[1024,512]{1,0:T(8,128)(2,1)S(1)}, bf16[1024,512]{1,0:T(8,128)(2,1)S(1)}, bf16[16,2,256,128]{3,2,1,0:T(8,128)(2,1)S(1)}) custom-call(s32[17]{0:T(128)S(1)} %pad_add_fusion.scal, bf16[1024,1536]{1,0:T(8,128)(2,1)S(1)} %convolution_convert_fusion.2.projected, f32[1024,256]{1,0:T(8,128)S(1)} %convolution_add_fusion.z, ...), custom_call_target="tpu_custom_call" | custom-call | flops 10000000000 | bytes 15000000 | tf_op jit(solution)/shard_map/mixer_forward/pallas_call | solution.py:286
  87.7 22.0 %collective-permute-done.2 = bf16[512,1024]{1,0:T(8,128)(2,1)S(1)} collective-permute-done((bf16[512,1024]{1,0:T(8,128)(2,1)S(1)}, bf16[512,1024]{1,0:T(8,128)(2,1)S(1)}, u32[]{:S(2)}, u32[]{:S(2)}) %collective-permute-start.2) | collective-permute-done | bytes 1048608 | tf_op jit(solution)/shard_map/ppermute | solution.py:338
  114.3 29.2 %all-gather.5.cloned.1.call-done = bf16[1024,4224]{1,0:T(8,128)(2,1)} async-done(((bf16[64,4224]{1,0:T(8,128)(2,1)}), bf16[1024,4224]{1,0:T(8,128)(2,1)}) %all-gather.5.cloned.1.call-update) | async-done | bytes 8650768 | tf_op jit(solution)/shard_map/all_gather | solution.py:420
  143.6 6.2 %fusion.19 = f32[512,2816]{1,0:T(8,128)S(1)} fusion(bf16[512,1024]{1,0:T(8,128)(2,1)} %multiply_convert_fusion.6, bf16[1024,4224]{1,0:T(8,128)(2,1)} %all-gather.5.cloned.1.call-done), kind=kOutput, calls=%fused_computation.32 | convolution fusion | flops 2952790016 | bytes 12582912 | tf_op jit(solution)/shard_map/dot_general | solution.py:54
  149.9 4.5 %fusion.15 = f32[512,2816]{1,0:T(8,128)S(1)} fusion(bf16[512,1024]{1,0:T(8,128)(2,1)} %collective-permute-done.3, bf16[1024,4224]{1,0:T(8,128)(2,1)S(1)} %copy-done.37), kind=kOutput, calls=%fused_computation.28 | convolution fusion | flops 2952790016 | bytes 12582912 | tf_op jit(solution)/shard_map/dot_general | solution.py:54
  158.3 5.7 %multiply_convert_fusion.2 = (bf16[512,1408]{1,0:T(8,128)(2,1)}, bf16[512,1408]{1,0:T(8,128)(2,1)}, bf16[512,1408]{1,0:T(8,128)(2,1)S(1)}) fusion(f32[512,2816]{1,0:T(8,128)S(1)} %fusion.15, bf16[512,1024]{1,0:T(8,128)(2,1)} %collective-permute-done.1, bf16[1024,4224]{1,0:T(8,128)(2,1)S(1)} %copy-done.37), kind=kOutput, calls=%fused_computation.46 | convolution fusion | flops 1486487552 | bytes 14024704 | tf_op jit(solution)/shard_map/dot_general | solution.py:54
  164.0 5.5 %convolution_convert_fusion.1 = bf16[1024,1408]{1,0:T(8,128)(2,1)S(1)} fusion(bf16[512,1408]{1,0:T(8,128)(2,1)S(1)} %get-tuple-element.90, bf16[512,1408]{1,0:T(8,128)(2,1)S(1)} %get-tuple-element.91, bf16[512,1024]{1,0:T(8,128)(2,1)} %collective-permute-done.1, bf16[512,1024]{1,0:T(8,128)(2,1)S(1)} %copy-done.22), kind=kOutput, calls=%fused_computation.24 | convolution fusion | flops 2964193280 | bytes 7864320 | tf_op jit(solution)/shard_map/dot_general | solution.py:62
  169.6 9.5 %fusion.9 = bf16[1024,2816]{1,0:T(8,128)(2,1)S(1)} fusion(bf16[512,1408]{1,0:T(8,128)(2,1)} %get-tuple-element.87, bf16[512,1408]{1,0:T(8,128)(2,1)} %get-tuple-element.86, bf16[512,1408]{1,0:T(8,128)(2,1)} %get-tuple-element.89, bf16[512,1408]{1,0:T(8,128)(2,1)} %get-tuple-element.88, bf16[512,1024]{1,0:T(8,128)(2,1)} %collective-permute-done.3, ...), kind=kOutput, calls=%fused_computation.11 | convolution fusion | flops 5935726592 | bytes 13631488 | tf_op jit(solution)/shard_map/dot_general | solution.py:62
  186.7 6.4 %fusion.59 = bf16[512,1024]{1,0:T(8,128)(2,1)S(1)} fusion(bf16[1024,4224]{1,0:T(8,128)(2,1)} %all-gather.5.cloned.1.call-done, bf16[512,1408]{1,0:T(8,128)(2,1)} %get-tuple-element.87, bf16[512,1408]{1,0:T(8,128)(2,1)S(1)} %copy-done.44), kind=kOutput, calls=%fused_computation.95 | convolution fusion | flops 2959081472 | bytes 9699328 | tf_op jit(solution)/shard_map/dot_general | solution.py:58
  194.6 23.8 %collective-permute-done.4 = bf16[512,1024]{1,0:T(8,128)(2,1)S(1)} collective-permute-done((bf16[512,1024]{1,0:T(8,128)(2,1)S(1)}, bf16[512,1024]{1,0:T(8,128)(2,1)S(1)}, u32[]{:S(2)}, u32[]{:S(2)}) %collective-permute-start.4) | collective-permute-done | bytes 1048608 | tf_op jit(solution)/shard_map/ppermute | solution.py:338
  225.9 5.2 %fusion.56 = bf16[512,1024]{1,0:T(8,128)(2,1)} fusion(bf16[512,1408]{1,0:T(8,128)(2,1)} %copy-done.41, bf16[1024,4224]{1,0:T(8,128)(2,1)} %all-gather.5.cloned.1.call-done), kind=kOutput, calls=%fused_computation.91 | convolution fusion | flops 1476919296 | bytes 5373952 | tf_op jit(solution)/shard_map/dot_general | solution.py:58
  231.1 18.1 %collective-permute-done.5 = bf16[512,1024]{1,0:T(8,128)(2,1)} collective-permute-done((bf16[512,1024]{1,0:T(8,128)(2,1)}, bf16[512,1024]{1,0:T(8,128)(2,1)}, u32[]{:S(2)}, u32[]{:S(2)}) %collective-permute-start.5) | collective-permute-done | bytes 1048608 | tf_op jit(solution)/shard_map/ppermute | solution.py:338
  249.3 4.1 convolution_convert_fusion.4.grad_gated
  253.4 5.5 %fusion = bf16[8,64,4224]{2,1,0:T(8,128)(2,1)} fusion(bf16[8,64,4224]{2,1,0:T(8,128)(2,1)} %collective-permute-done.6, bf16[8,2,64,4224]{3,2,1,0:T(8,128)(2,1)S(1)} %bitcast.54, s32[]{:T(128)S(6)} %select_n.38), kind=kLoop, calls=%fused_computation.2 | loop fusion | flops 8650752 | bytes 12976132 | tf_op jit(solution)/shard_map/convert_element_type | solution.py:348
  262.7 19.3 %mixer_backward.1 = (bf16[1024,1536]{1,0:T(8,128)(2,1)S(1)}, f32[1024,256]{1,0:T(8,128)S(1)}, f32[8,256]{1,0:T(8,128)S(1)}) custom-call(s32[17]{0:T(128)S(1)} %pad_add_fusion.scal, bf16[1024,1536]{1,0:T(8,128)(2,1)S(1)} %copy-done.3, f32[1024,256]{1,0:T(8,128)S(1)} %convolution_add_fusion.z, f32[1024,1]{1,0:T(8,128)S(1)} %copy.44.live, ...), custom_call_target="tpu_custom_call" | custom-call | flops 24999999488 | bytes 20000000 | tf_op jit(solution)/shard_map/mixer_backward/pallas_call | solution.py:315
  282.0 6.5 %convolution_convert_fusion = bf16[1024,1536]{1,0:T(8,128)(2,1)S(1)} fusion(bf16[1024,1536]{1,0:T(8,128)(2,1)S(1)} %get-tuple-element.40, bf16[512,1024]{1,0:T(8,128)(2,1)} %collective-permute-done, bf16[512,1024]{1,0:T(8,128)(2,1)} %fusion.35), kind=kOutput, calls=%fused_computation.23 | convolution fusion | flops 3226992640 | bytes 8388608 | tf_op jit(solution)/shard_map/dot_general | solution.py:62
  297.6 49.5 %reduce-scatter.3.cloned.1.call-done = bf16[64,4224]{1,0:T(8,128)(2,1)} async-done(((bf16[512,4224]{1,0:T(8,128)(2,1)}), bf16[64,4224]{1,0:T(8,128)(2,1)}) %reduce-scatter.3.cloned.1.call-update) | async-done | bytes 540688 | tf_op jit(solution)/shard_map/reduce_scatter | solution.py:355
  347.1 8.7 %add_convert_fusion = bf16[1024,1024]{1,0:T(8,128)(2,1)S(1)} fusion(f32[1024,1024]{1,0:T(8,128)} %fusion.99, f32[1024,1024]{1,0:T(8,128)} %fusion.100, bf16[1024,1536]{1,0:T(8,128)(2,1)} %copy-done.4, bf16[1024,2048]{1,0:T(8,128)(2,1)} %all-gather.3.cloned.1.call-done), kind=kOutput, calls=%fused_computation.22 | convolution fusion | flops 3224371200 | bytes 16777216 | tf_op jit(solution)/shard_map/dot_general | solution.py:58
  365.1 18.3 %collective-permute-done.8 = bf16[512,1024]{1,0:T(8,128)(2,1)} collective-permute-done((bf16[512,1024]{1,0:T(8,128)(2,1)}, bf16[512,1024]{1,0:T(8,128)(2,1)}, u32[]{:S(2)}, u32[]{:S(2)}) %collective-permute-start.8) | collective-permute-done | bytes 1048608 | tf_op jit(solution)/shard_map/ppermute | solution.py:338
  392.0 4.2 fusion.54
  414.2 6.2 %collective-permute-done.13 = f32[214,128]{1,0:T(8,128)S(1)} collective-permute-done((f32[214,128]{1,0:T(8,128)S(1)}, f32[214,128]{1,0:T(8,128)S(1)}, u32[]{:S(2)}, u32[]{:S(2)}) %collective-permute-start.13) | collective-permute-done | bytes 109600 | tf_op jit(solution)/shard_map/ppermute | solution.py:365
  (211 shorter events, 102.0 us)
Async XLA Ops:
  7.2 38.7 %copy-start = (bf16[1024,16]{0,1:T(8,128)(2,1)S(1)}, bf16[1024,16]{0,1:T(8,128)(2,1)}, u32[]{:S(2)}) copy-start(bf16[1024,16]{0,1:T(8,128)(2,1)} %param.31) | copy-start | bytes 98308
  7.2 36.3 %copy-start.21 = (bf16[512,1024]{1,0:T(8,128)(2,1)S(1)}, bf16[512,1024]{1,0:T(8,128)(2,1)}, u32[]{:S(2)}) copy-start(bf16[512,1024]{1,0:T(8,128)(2,1)} %param.21) | copy-start | bytes 3145732
  7.3 60.8 %all-gather.3.cloned.1.call-start = ((), (), s32[]{:S(2)}) async-start(), calls=%async_computation.2 | async-start | bytes 4456448 | tf_op jit(solution)/shard_map/all_gather | solution.py:412
  10.6 35.1 %copy-start.36 = (bf16[512]{0:T(512)(128)(2,1)S(1)}, bf16[512]{0:T(512)(128)(2,1)}, u32[]{:S(2)}) copy-start(bf16[512]{0:T(512)(128)(2,1)} %param.33) | copy-start | bytes 3076
  12.2 131.3 %all-gather.5.cloned.1.call-start = ((), (), s32[]{:S(2)}) async-start(), calls=%async_computation.3 | async-start | bytes 9191424 | tf_op jit(solution)/shard_map/all_gather | solution.py:420
  14.2 332.9 %reduce-scatter.3.cloned.1.call-start = ((), (), s32[]{:S(2)}) async-start(), calls=%async_computation.4 | async-start | bytes 4866048 | tf_op jit(solution)/shard_map/reduce_scatter | solution.py:355
  15.9 32.9 %copy-start.30 = (bf16[16,512]{1,0:T(8,128)(2,1)S(1)}, bf16[16,512]{1,0:T(8,128)(2,1)}, u32[]{:S(2)}) copy-start(bf16[16,512]{1,0:T(8,128)(2,1)} %param.32) | copy-start | bytes 49156
  17.1 26.4 %collective-permute-start = (bf16[512,1024]{1,0:T(8,128)(2,1)}, bf16[512,1024]{1,0:T(8,128)(2,1)}, u32[]{:S(2)}, u32[]{:S(2)}) collective-permute-start(bf16[512,1024]{1,0:T(8,128)(2,1)} %fusion.35), channel_id=1, source_target_pairs={{0,1},{1,0},{2,3},{3,2},{4,5},{5,4},{6,7},{7,6},{8,9},{9,8},{10,11... | collective-permute-start | bytes 3145736 | tf_op jit(solution)/shard_map/ppermute | solution.py:338
  43.6 24.5 %collective-permute-start.1 = (bf16[512,1024]{1,0:T(8,128)(2,1)S(1)}, bf16[512,1024]{1,0:T(8,128)(2,1)}, u32[]{:S(2)}, u32[]{:S(2)}) collective-permute-start(bf16[512,1024]{1,0:T(8,128)(2,1)S(1)} %copy-done.21), channel_id=1, source_target_pairs={{0,1},{1,0},{2,3},{3,2},{4,5},{5,4},{6,7},{7,6},{8,9},{9,8},{10,11... | collective-permute-start | bytes 3145736 | tf_op jit(solution)/shard_map/ppermute | solution.py:338
  86.2 23.5 %collective-permute-start.2 = (bf16[512,1024]{1,0:T(8,128)(2,1)S(1)}, bf16[512,1024]{1,0:T(8,128)(2,1)S(1)}, u32[]{:S(2)}, u32[]{:S(2)}) collective-permute-start(bf16[512,1024]{1,0:T(8,128)(2,1)S(1)} %convolution_convert_fusion.5), channel_id=1, source_target_pairs={{0,1},{1,0},{2,3},{3,2},{4,5},{5,4},{6,7},{7,6},{8,9},{9,8},{10,11... | collective-permute-start | bytes 3145736 | tf_op jit(solution)/shard_map/ppermute | solution.py:338
  113.2 36.6 %collective-permute-start.3 = (bf16[512,1024]{1,0:T(8,128)(2,1)}, bf16[512,1024]{1,0:T(8,128)(2,1)}, u32[]{:S(2)}, u32[]{:S(2)}) collective-permute-start(bf16[512,1024]{1,0:T(8,128)(2,1)} %multiply_convert_fusion.6), channel_id=1, source_target_pairs={{0,1},{1,0},{2,3},{3,2},{4,5},{5,4},{6,7},{7,6},{8,9},{9,8},{10,11... | collective-permute-start | bytes 3145736 | tf_op jit(solution)/shard_map/ppermute | solution.py:338
  180.2 38.2 %slice-start.3 = ((s8[8650752]{0:T(1024)(128)(4,1)}), s8[4194304]{0:T(1024)(128)(4,1)S(1)}, s32[]{:S(2)}) async-start(s8[8650752]{0:T(1024)(128)(4,1)} %bitcast.64), calls=%async_computation.9 | async-start | bytes 8388608
  186.4 66.9 %collective-permute-start.6 = (bf16[8,64,4224]{2,1,0:T(8,128)(2,1)}, bf16[8,64,4224]{2,1,0:T(8,128)(2,1)}, u32[]{:S(2)}, u32[]{:S(2)}) collective-permute-start(bf16[8,64,4224]{2,1,0:T(8,128)(2,1)} %dynamic-slice_bitcast_fusion), channel_id=1, source_target_pairs={{0,2},{2,0},{4,6},{6,4},{8,10},{10,8},{12,14},{14,12},{16,18},{18,... | collective-permute-start | bytes 12976136 | tf_op jit(solution)/shard_map/ppermute | solution.py:347
  193.1 25.4 %collective-permute-start.4 = (bf16[512,1024]{1,0:T(8,128)(2,1)S(1)}, bf16[512,1024]{1,0:T(8,128)(2,1)S(1)}, u32[]{:S(2)}, u32[]{:S(2)}) collective-permute-start(bf16[512,1024]{1,0:T(8,128)(2,1)S(1)} %fusion.59), channel_id=1, source_target_pairs={{0,1},{1,0},{2,3},{3,2},{4,5},{5,4},{6,7},{7,6},{8,9},{9,8},{10,11... | collective-permute-start | bytes 3145736 | tf_op jit(solution)/shard_map/ppermute | solution.py:338
  224.4 24.8 %collective-permute-start.5 = (bf16[512,1024]{1,0:T(8,128)(2,1)}, bf16[512,1024]{1,0:T(8,128)(2,1)}, u32[]{:S(2)}, u32[]{:S(2)}) collective-permute-start(bf16[512,1024]{1,0:T(8,128)(2,1)} %get-tuple-element.84), channel_id=1, source_target_pairs={{0,1},{1,0},{2,3},{3,2},{4,5},{5,4},{6,7},{7,6},{8,9},{9,8},{10,11... | collective-permute-start | bytes 3145736 | tf_op jit(solution)/shard_map/ppermute | solution.py:338
  258.9 165.8 %reduce-scatter.5.cloned.1.call-start = ((), (), s32[]{:S(2)}) async-start(), calls=%async_computation.5 | async-start | bytes 2359296 | tf_op jit(solution)/shard_map/reduce_scatter | solution.py:355
  289.4 6.1 %collective-permute-start.14 = (bf16[8,64,2048]{2,1,0:T(8,128)(2,1)S(1)}, bf16[8,64,2048]{2,1,0:T(8,128)(2,1)S(1)}, u32[]{:S(2)}, u32[]{:S(2)}) collective-permute-start(bf16[8,64,2048]{2,1,0:T(8,128)(2,1)S(1)} %dynamic-slice_bitcast_fusion.1), channel_id=1, source_target_pairs={{0,2},{2,0},{4,6},{6,4},{8,10},{10,8},{12,14},{14,12},{16,18},{18,... | collective-permute-start | bytes 6291464 | tf_op jit(solution)/shard_map/ppermute | solution.py:347
  358.2 25.2 %collective-permute-start.8 = (bf16[512,1024]{1,0:T(8,128)(2,1)}, bf16[512,1024]{1,0:T(8,128)(2,1)}, u32[]{:S(2)}, u32[]{:S(2)}) collective-permute-start(bf16[512,1024]{1,0:T(8,128)(2,1)} %slice.119), channel_id=1, source_target_pairs={{0,1},{1,0},{2,3},{3,2},{4,5},{5,4},{6,7},{7,6},{8,9},{9,8},{10,11... | collective-permute-start | bytes 3145736 | tf_op jit(solution)/shard_map/ppermute | solution.py:338
  385.9 5.9 %collective-permute-start.9 = (f32[214,128]{1,0:T(8,128)S(1)}, f32[214,128]{1,0:T(8,128)S(1)}, u32[]{:S(2)}, u32[]{:S(2)}) collective-permute-start(f32[214,128]{1,0:T(8,128)S(1)} %concatenate.58), channel_id=1, source_target_pairs={{0,1},{1,0},{2,3},{3,2},{4,5},{5,4},{6,7},{7,6},{8,9},{9,8},{10,11... | collective-permute-start | bytes 328712 | tf_op jit(solution)/shard_map/ppermute | solution.py:338
  387.5 25.1 %collective-permute-start.7 = (bf16[512,1024]{1,0:T(8,128)(2,1)}, bf16[512,1024]{1,0:T(8,128)(2,1)S(1)}, u32[]{:S(2)}, u32[]{:S(2)}) collective-permute-start(bf16[512,1024]{1,0:T(8,128)(2,1)} %fusion.56), channel_id=1, source_target_pairs={{0,1},{1,0},{2,3},{3,2},{4,5},{5,4},{6,7},{7,6},{8,9},{9,8},{10,11... | collective-permute-start | bytes 3145736 | tf_op jit(solution)/shard_map/ppermute | solution.py:338
  391.9 4.3 collective-permute-start.10
  396.2 5.4 %collective-permute-start.11 = (f32[214,128]{1,0:T(8,128)S(1)}, f32[214,128]{1,0:T(8,128)S(1)}, u32[]{:S(2)}, u32[]{:S(2)}) collective-permute-start(f32[214,128]{1,0:T(8,128)S(1)} %add.174), channel_id=1, source_target_pairs={{0,4},{2,6},{4,0},{6,2},{8,12},{10,14},{12,8},{14,10},{16,20},{18,... | collective-permute-start | bytes 328712 | tf_op jit(solution)/shard_map/ppermute | solution.py:365
  401.6 7.3 %collective-permute-start.12 = (f32[214,128]{1,0:T(8,128)S(1)}, f32[214,128]{1,0:T(8,128)S(1)}, u32[]{:S(2)}, u32[]{:S(2)}) collective-permute-start(f32[214,128]{1,0:T(8,128)S(1)} %add.175), channel_id=1, source_target_pairs={{0,8},{2,10},{4,12},{6,14},{8,0},{10,2},{12,4},{14,6},{16,24},{18,... | collective-permute-start | bytes 328712 | tf_op jit(solution)/shard_map/ppermute | solution.py:365
  408.9 11.4 %collective-permute-start.13 = (f32[214,128]{1,0:T(8,128)S(1)}, f32[214,128]{1,0:T(8,128)S(1)}, u32[]{:S(2)}, u32[]{:S(2)}) collective-permute-start(f32[214,128]{1,0:T(8,128)S(1)} %add.176), channel_id=1, source_target_pairs={{0,16},{2,18},{4,20},{6,22},{8,24},{10,26},{12,28},{14,30},{16,0},... | collective-permute-start | bytes 328712 | tf_op jit(solution)/shard_map/ppermute | solution.py:365
  (46 other events, 683.7 us)
Sparse Core Ops, SparseCore 0:
  12.4 53.2 all-gather.2
  68.5 75.0 all-gather.4
  259.0 88.0 reduce-scatter.2
  350.9 70.3 reduce-scatter.4

commit v3 on v2

--- a/solution.py
+++ b/solution.py
@@ -349,12 +349,59 @@
     return total.reshape(values.shape[0] // 2, values.shape[1])
 
 
-def chips_scatter(values):
+def halving_stages():
+    return (lax.axis_size("dp") // 2).bit_length() - 1
+
+
+def by_chip(values):
+    stages = halving_stages()
+    return values.reshape((2,) * stages + (values.shape[0] >> stages, values.shape[1]))
+
+
+def halving_stage(held, stage):
     count = lax.axis_size("dp")
-    groups = [list(range(parity, count, 2)) for parity in range(2)]
-    return lax.psum_scatter(
-        values, "dp", scatter_dimension=0, axis_index_groups=groups, tiled=True
-    )
+    stages = halving_stages()
+    bit = 2 << stage
+    side = (lax.axis_index("dp") // bit) % 2
+    axis = stages - 1 - stage
+    kept = lax.dynamic_index_in_dim(held, side, axis, keepdims=False)
+    sent = lax.dynamic_index_in_dim(held, 1 - side, axis, keepdims=False)
+    arrived = lax.ppermute(sent, "dp", [(i, i ^ bit) for i in range(count)])
+    total = kept.astype(f32) + arrived.astype(f32)
+    return total if stage == stages - 1 else total.astype(bf16)
+
+
+def halving_rest(held):
+    for stage in range(1, halving_stages()):
+        held = halving_stage(held, stage)
+    return held
+
+
+def both_ways(side, mine, other, axis):
+    first = jnp.where(side == 0, mine, other)
+    second = jnp.where(side == 0, other, mine)
+    return jnp.stack([first, second], axis=axis)
+
+
+def gather_doubling(values):
+    count = lax.axis_size("dp")
+    place = lax.axis_index("dp")
+    stages = count.bit_length() - 1
+    held = values
+    for stage in range(stages):
+        bit = count >> (stage + 1)
+        arrived = lax.ppermute(held, "dp", [(i, i ^ bit) for i in range(count)])
+        held = both_ways((place // bit) % 2, held, arrived, stage)
+    return held.reshape(values.shape[0] * count, values.shape[1])
+
+
+def swap_whole(values):
+    count = lax.axis_size("dp")
+    parity = lax.axis_index("dp") % 2
+    half = values.shape[0] // 2
+    mine = swap_tensor(lax.dynamic_slice_in_dim(values, parity * half, half, 0))
+    other = lax.ppermute(mine, "dp", [(i, i ^ 1) for i in range(count)])
+    return both_ways(parity, mine, other, 0).reshape(values.shape)
 
 
 def butterfly_sum(values):
@@ -417,22 +464,21 @@
         axis=0,
         tiled=True,
     )
-    feed_all = lax.all_gather(
-        jnp.concatenate([feed_gate, feed_up, feed_down], axis=1), "dp", axis=0, tiled=True
-    )
+    gate_up_full = lax.all_gather(
+        jnp.concatenate([feed_gate, feed_up], axis=1), "dp", axis=0, tiled=True
+    )
+    feed_down_full = gather_doubling(feed_down)
     gain_in = mixer_gain.astype(f32)
     token_values = tokens.astype(f32)
     normed_in, inverse_in = rms_forward(token_values, gain_in)
     normed_low = normed_in.astype(bf16)
     normed_other = swap_tensor(normed_low)
-    normed_other, cotangent_low = lax.optimization_barrier((normed_other, cotangent))
-    cotangent_other = swap_tensor(cotangent_low)
+    cotangent_other = swap_tensor(cotangent)
     joined, cotangent_other = lax.optimization_barrier((joined, cotangent_other))
     projected_width = 2 * key_width + 2 * value_width
     joined_in = joined[:, :projected_width]
-    output_full = joined[:, projected_width:]
-    gate_up_full = feed_all[:, : 2 * feed_width]
-    feed_down_full = feed_all[:, 2 * feed_width :]
+    output_half = joined[:, projected_width:]
+    output_other = swap_whole(output_half)
 
     normed_all = jnp.concatenate([normed_low, normed_other], axis=0)
     projected = nn(normed_all, joined_in).astype(bf16)
@@ -442,9 +488,10 @@
     z = jnp.dot(latent, up_local, precision=highest) + bias_local.astype(f32)
     gated, mixture, states = mixer_forward(scal, projected, z, live, gain_head, sums)
 
-    attended_other = swap_tensor(nt(gated[own:], output_full).astype(bf16))
-    attended_own = nt(gated[:own], output_full)
-    middle = token_values + (attended_own + attended_other.astype(f32))
+    gated_own = gated[:own]
+    gated_rest = swap_tensor(gated[own:])
+    attended = nt(gated_own, output_half) + nt(gated_rest, output_other)
+    middle = token_values + attended
     gain_mid = feed_gain.astype(f32)
     normed_mid, inverse_mid = rms_forward(middle, gain_mid)
     mid_low = normed_mid.astype(bf16)
@@ -465,46 +512,59 @@
         grad_both = jnp.concatenate([grad_gate_low, grad_up_low], axis=1)
         return hidden_low, grad_both, nt(grad_both, gate_up_full)
 
-    hidden_own, grad_both_own, mid_back_own = feed_rows(mid_low, cotangent)
     hidden_other, grad_both_other, mid_back_other = feed_rows(mid_other, cotangent_other)
-    mid_back = swap_tensor(mid_back_other.astype(bf16))
+    mid_send, mid_here, cotangent_here = lax.optimization_barrier(
+        (mid_back_other.astype(bf16), mid_low, cotangent)
+    )
+    mid_back = swap_tensor(mid_send)
+    hidden_own, grad_both_own, mid_back_own = feed_rows(mid_here, cotangent_here)
 
     upstream = cotangent.astype(f32)
     grad_normed_mid = mid_back_own + mid_back.astype(f32)
     grad_mid_in, grad_feed_gain = rms_backward(middle, inverse_mid, gain_mid, grad_normed_mid)
     grad_middle = upstream + grad_mid_in
     grad_attended = grad_middle.astype(bf16)
-    attended_back = swap_tensor(grad_attended)
+    gated_back = swap_tensor(nn(grad_attended, output_other).astype(bf16))
+    grad_gated = jnp.concatenate([nn(grad_attended, output_half).astype(bf16), gated_back], axis=0)
 
     mid_all = jnp.concatenate([mid_low, mid_other], axis=0)
     cotangent_all = jnp.concatenate([cotangent, cotangent_other], axis=0)
     hidden_all = jnp.concatenate([hidden_own, hidden_other], axis=0)
     grad_both_all = jnp.concatenate([grad_both_own, grad_both_other], axis=0)
-    feed_grads = jnp.concatenate(
-        [
-            tn(mid_all, grad_both_all).astype(bf16),
-            tn(cotangent_all, hidden_all).astype(bf16),
-        ],
-        axis=1,
-    )
-    feed_chip = chip_sum(feed_grads)
-
-    attended_all = jnp.concatenate([grad_attended, attended_back], axis=0)
-    grad_gated = nn(attended_all, output_full).astype(bf16)
+    down_sum = by_chip(chip_sum(tn(cotangent_all, hidden_all).astype(bf16)))
+    down_sum = halving_stage(down_sum, 0)
+    both_chip = chip_sum(tn(mid_all, grad_both_all).astype(bf16))
     fed_send = nt(hidden_other, feed_down_full).astype(bf16)
-    grad_gated, feed_chip, fed_send = lax.optimization_barrier((grad_gated, feed_chip, fed_send))
-    fed = nt(hidden_own, feed_down_full) + swap_tensor(fed_send).astype(f32)
-    output = (middle + fed).astype(bf16)
-    feed_sum = chips_scatter(feed_chip)
+    grad_gated, down_sum, both_chip, fed_send = lax.optimization_barrier(
+        (grad_gated, down_sum, both_chip, fed_send)
+    )
+    gate_sum = halving_stage(by_chip(both_chip[:, :feed_width]), 0)
+    up_sum = halving_stage(by_chip(both_chip[:, feed_width:]), 0)
+    fed_back = swap_tensor(fed_send)
+    output_chip = chip_sum(
+        jnp.concatenate(
+            [
+                tn(grad_attended, gated_own).astype(bf16),
+                tn(grad_attended, gated_rest).astype(bf16),
+            ],
+            axis=1,
+        )
+    )
+    output_back = swap_tensor(output_chip[:, value_width:])
     grad_projected, grad_z, grad_gain_rows = mixer_backward(
         scal, projected, z, live, gain_head, sums, mixture, states, grad_gated
     )
-    joined_grads = jnp.concatenate(
-        [tn(normed_all, grad_projected).astype(bf16), tn(attended_all, gated).astype(bf16)], axis=1
-    )
-    joined_chip, feed_sum = lax.optimization_barrier((chip_sum(joined_grads), feed_sum))
-    joined_sum = chips_scatter(joined_chip).astype(f32)
-    feed_sum = feed_sum.astype(f32)
+    grad_projected, gate_sum = lax.optimization_barrier((grad_projected, gate_sum))
+    projected_chip = chip_sum(tn(normed_all, grad_projected).astype(bf16))
+    output_total = output_chip[:, :value_width].astype(f32) + output_back.astype(f32)
+    joined_chip = jnp.concatenate([projected_chip, output_total.astype(bf16)], axis=1)
+    joined_chip, up_sum = lax.optimization_barrier((joined_chip, up_sum))
+    joined_sums = [
+        halving_stage(by_chip(piece), 0) for piece in jnp.split(joined_chip, 2, axis=1)
+    ]
+    hidden_late, grad_projected = lax.optimization_barrier((hidden_own, grad_projected))
+    fed = nt(hidden_late, feed_down_full) + fed_back.astype(f32)
+    output = (middle + fed).astype(bf16)
 
     grad_latent = lax.dot_general(
         grad_z, up_local, (((1,), (1,)), ((), ())), precision=highest, preferred_element_type=f32
@@ -519,9 +579,14 @@
     low_rank = decay_down.shape[1]
     grad_decay_down = grad_down_parts[:, :low_rank] + grad_down_parts[:, low_rank:]
     from_latent = nt(latent_high, decay_down) + nt(latent_rest, decay_down)
-    normed_part = (nt(grad_projected, joined_in) + from_latent).astype(bf16)
-    grad_normed = normed_part[:own].astype(f32) + swap_tensor(normed_part[own:]).astype(f32)
-    grad_in_part, grad_mixer_gain = rms_backward(token_values, inverse_in, gain_in, grad_normed)
+    normed_part = nt(grad_projected, joined_in) + from_latent
+    grad_mixer_gain = jnp.sum(normed_part * normed_all.astype(f32), axis=0) / gain_in
+    normed_part = normed_part.astype(bf16)
+    normed_back, joined_sums[1] = lax.optimization_barrier(
+        (swap_tensor(normed_part[own:]), joined_sums[1])
+    )
+    grad_normed = normed_part[:own].astype(f32) + normed_back.astype(f32)
+    grad_in_part = rms_backward(token_values, inverse_in, gain_in, grad_normed)[0]
     input_grad = grad_middle + grad_in_part
 
     up_full = lax.dynamic_update_slice_in_dim(
@@ -538,7 +603,11 @@
         jnp.sum(grad_gain_rows, axis=0),
         grad_feed_gain,
     )
-    flat = butterfly_sum(jnp.concatenate([part.reshape(-1, 128) for part in small], axis=0))
+    flat = jnp.concatenate([part.reshape(-1, 128) for part in small], axis=0)
+    flat, joined_sums[0] = lax.optimization_barrier((flat, joined_sums[0]))
+    flat = butterfly_sum(flat)
+    down_sum, gate_sum, up_sum = (halving_rest(held) for held in (down_sum, gate_sum, up_sum))
+    joined_sum = jnp.concatenate([halving_rest(held) for held in joined_sums], axis=1)
     small_sums = []
     row = 0
     for part in small:
@@ -559,9 +628,9 @@
         small_sums[3],
         small_sums[4],
         small_sums[5],
-        feed_sum[:, :feed_width],
-        feed_sum[:, feed_width : 2 * feed_width],
-        feed_sum[:, 2 * feed_width : 3 * feed_width],
+        gate_sum,
+        up_sum,
+        down_sum,
     )
 
 

time: 439 us -> 411 us (0.936)
  waiting for transfers between devices: 222 us -> 164 us
  starting transfers between devices: 17.9 us -> 42.2 us
  matrix products: 96.3 us -> 77.2 us
  other arithmetic: 25.7 us -> 37.7 us
  local copies, waits for them, and re-layouts: 26.9 us -> 38.1 us
    ppermute x0 -> x20, waiting for transfers between devices: none -> 87.5 us  [the longest x15 57.4 us: halving_stage(): arrived = lax.ppermute(sent, 'dp', [(i, i ^ bit) for i in range(count)])]
    ppermute x9 -> x11, waiting for transfers between devices: 131 us -> 70 us  [swap_tensor(): return lax.ppermute(values, 'tensor', [(0, 1), (1, 0)])]
    reduce_scatter x2 -> x0, waiting for transfers between devices: 49.5 us -> none  [chips_scatter(): lax.psum_scatter(values, 'dp', scatter_dimension=0, axis_index_groups=gro...]
    all_gather x1, waiting for transfers between devices: 29.2 us -> 0.01 us  [on_device(): lax.all_gather(jnp.concatenate([feed_gate, feed_up], axis=1), 'dp', axis=...]
    ppermute x0 -> x20, starting transfers between devices: none -> 26.9 us  [the longest x15 19.6 us: halving_stage(): arrived = lax.ppermute(sent, 'dp', [(i, i ^ bit) for i in range(count)])]
    dot_general x9, matrix products: 35.2 us -> 24.4 us  [nt(): lax.dot_general(left, right, (((1,), (1,)), ((), ())), preferred_element_...]
    another operation x0 -> x10, other arithmetic: none -> 8.45 us  [both_ways(): return jnp.stack([first, second], axis=axis)]
    ppermute x4, waiting for transfers between devices: 12.2 us -> 6.04 us  [butterfly_sum(): lax.ppermute(total, 'dp', [(i, i ^ reach) for i in range(count)])]
  transfers between devices with their start and end apart: 19 -> 41, of which waited for: 13 -> 22; matrix products, arithmetic and copies ran while one was open for 22% -> 29% of each run, Pallas kernels for 7% -> 8%
where the time goes in v3:
time: 411 us; the launch traced here: 405 us
  waiting for transfers between devices  164 us (40%)
  matrix products  77.2 us (19%)
  starting transfers between devices  42.2 us (10%)
  local copies, waits for them, and re-layouts  38.1 us (9%)
  other arithmetic  37.7 us (9%)
  Pallas kernels  30.4 us (7%)
  between operations  15.6 us (4%)
    ppermute x11, waiting for transfers between devices, swap_tensor(): return lax.ppermute(values, 'tensor', [(0, 1), (1, 0)])  70 us
    ppermute x15, waiting for transfers between devices, halving_stage(): arrived = lax.ppermute(sent, 'dp', [(i, i ^ bit) for i in range(count)])  57.4 us
    ppermute x4, waiting for transfers between devices, gather_doubling(): arrived = lax.ppermute(held, 'dp', [(i, i ^ bit) for i in range(count)])  30.1 us
    dot_general x8, matrix products, nn(): lax.dot_general(left, right, (((1,), (0,)), ((), ())), preferred_element_...  27.1 us
    dot_general x9, matrix products, nt(): lax.dot_general(left, right, (((1,), (1,)), ((), ())), preferred_element_...  24.4 us
    dot_general x6, matrix products, tn(): lax.dot_general(left, right, (((0,), (0,)), ((), ())), preferred_element_...  23.9 us
    ppermute x15, starting transfers between devices, halving_stage(): arrived = lax.ppermute(sent, 'dp', [(i, i ^ bit) for i in range(count)])  19.6 us
    pallas_call x1, Pallas kernels, mixer_backward(): pl.pallas_call(functools.partial(backward_kernel, heads), grid_spec=pltpu...  19.1 us
  transfers between devices with their start and end apart: 41, of which 22 were waited for; matrix products, arithmetic and copies ran while one was open for 29% of the time, Pallas kernels for 8%

profile of v3, /device:TPU:0, one launch (start us, length us, event | category | flops | bytes accessed | tf_op | source)
XLA Modules:
  0.0 404.9 jit_solution(12879255732581859451)
XLA Ops:
  22.1 13.5 %collective-permute-done.5 = bf16[64,1408]{1,0:T(8,128)(2,1)S(1)} collective-permute-done((bf16[64,1408]{1,0:T(8,128)(2,1)S(1)}, bf16[64,1408]{1,0:T(8,128)(2,1)S(1)}, u32[]{:S(2)}, u32[]{:S(2)}) %collective-permute-start.5) | collective-permute-done | bytes 180256 | tf_op jit(solution)/shard_map/ppermute | solution.py:393
  38.5 8.1 %collective-permute-done.6 = bf16[2,64,1408]{2,1,0:T(8,128)(2,1)S(1)} collective-permute-done((bf16[2,64,1408]{2,1,0:T(8,128)(2,1)S(1)}, bf16[2,64,1408]{2,1,0:T(8,128)(2,1)S(1)}, u32[]{:S(2)}, u32[]{:S(2)}) %collective-permute-start.6) | collective-permute-done | bytes 360480 | tf_op jit(solution)/shard_map/ppermute | solution.py:393
  49.6 13.4 %collective-permute-done = bf16[512,1024]{1,0:T(8,128)(2,1)} collective-permute-done((bf16[512,1024]{1,0:T(8,128)(2,1)S(1)}, bf16[512,1024]{1,0:T(8,128)(2,1)}, u32[]{:S(2)}, u32[]{:S(2)}) %collective-permute-start) | collective-permute-done | bytes 1048608 | tf_op jit(solution)/shard_map/ppermute | solution.py:338
  65.5 8.5 %collective-permute-done.7 = bf16[2,2,64,1408]{3,2,1,0:T(8,128)(2,1)} collective-permute-done((bf16[2,2,64,1408]{3,2,1,0:T(8,128)(2,1)}, bf16[2,2,64,1408]{3,2,1,0:T(8,128)(2,1)}, u32[]{:S(2)}, u32[]{:S(2)}) %collective-permute-start.7) | collective-permute-done | bytes 720928 | tf_op jit(solution)/shard_map/ppermute | solution.py:393
  79.4 5.6 %convolution_convert_fusion.2.projected = bf16[1024,1536]{1,0:T(8,128)(2,1)S(1)} fusion(bf16[1024,2048]{1,0:T(8,128)(2,1)} %all-gather.3.cloned.1.call-done, bf16[512,1024]{1,0:T(8,128)(2,1)} %collective-permute-done, bf16[512,1024]{1,0:T(8,128)(2,1)S(1)} %copy-done.40), kind=kOutput, calls=%fused_computation.20 | convolution fusion | flops 3226992640 | bytes 8388608 | tf_op jit(solution)/shard_map/dot_general | solution.py:54
  85.0 6.2 %collective-permute-done.3 = bf16[512,512]{1,0:T(8,128)(2,1)S(1)} collective-permute-done((bf16[512,512]{1,0:T(8,128)(2,1)S(1)}, bf16[512,512]{1,0:T(8,128)(2,1)S(1)}, u32[]{:S(2)}, u32[]{:S(2)}) %collective-permute-start.3) | collective-permute-done | bytes 524320 | tf_op jit(solution)/shard_map/ppermute | solution.py:338
  91.2 11.3 %mixer_forward.1 = (bf16[1024,512]{1,0:T(8,128)(2,1)S(1)}, bf16[1024,512]{1,0:T(8,128)(2,1)S(1)}, bf16[16,2,256,128]{3,2,1,0:T(8,128)(2,1)S(1)}) custom-call(s32[17]{0:T(128)S(1)} %pad_add_fusion.scal, bf16[1024,1536]{1,0:T(8,128)(2,1)S(1)} %convolution_convert_fusion.2.projected, f32[1024,256]{1,0:T(8,128)S(1)} %convolution_add_fusion.z, ...), custom_call_target="tpu_custom_call" | custom-call | flops 10000000000 | bytes 15000000 | tf_op jit(solution)/shard_map/mixer_forward/pallas_call | solution.py:286
  105.9 11.1 %collective-permute-done.2 = bf16[512,512]{1,0:T(8,128)(2,1)S(1)} collective-permute-done((bf16[512,512]{1,0:T(8,128)(2,1)S(1)}, bf16[512,512]{1,0:T(8,128)(2,1)S(1)}, u32[]{:S(2)}, u32[]{:S(2)}) %collective-permute-start.2) | collective-permute-done | bytes 524320 | tf_op jit(solution)/shard_map/ppermute | solution.py:338
  127.3 20.0 %collective-permute-done.9 = bf16[512,1024]{1,0:T(8,128)(2,1)} collective-permute-done((bf16[512,1024]{1,0:T(8,128)(2,1)}, bf16[512,1024]{1,0:T(8,128)(2,1)}, u32[]{:S(2)}, u32[]{:S(2)}) %collective-permute-start.9) | collective-permute-done | bytes 1048608 | tf_op jit(solution)/shard_map/ppermute | solution.py:338
  147.3 6.2 %fusion.85 = f32[512,2816]{1,0:T(8,128)S(1)} fusion(bf16[512,1024]{1,0:T(8,128)(2,1)} %collective-permute-done.9, bf16[1024,2816]{1,0:T(8,128)(2,1)} %all-gather.5.cloned.1.call-done), kind=kOutput, calls=%fused_computation.202 | convolution fusion | flops 2952790016 | bytes 12582912 | tf_op jit(solution)/shard_map/dot_general | solution.py:54
  172.3 6.0 %convolution_convert_fusion.1 = bf16[1024,1408]{1,0:T(8,128)(2,1)S(1)} fusion(bf16[512,1408]{1,0:T(8,128)(2,1)S(1)} %get-tuple-element.108, bf16[512,1408]{1,0:T(8,128)(2,1)S(1)} %get-tuple-element.53, bf16[512,1024]{1,0:T(8,128)(2,1)} %collective-permute-done.1, bf16[512,1024]{1,0:T(8,128)(2,1)S(1)} %copy-done.36), kind=kOutput, calls=%fused_computation.19 | convolution fusion | flops 2964193280 | bytes 7864320 | tf_op jit(solution)/shard_map/dot_general | solution.py:62
  180.4 9.5 %fusion.9 = bf16[1024,2816]{1,0:T(8,128)(2,1)S(1)} fusion(bf16[512,1408]{1,0:T(8,128)(2,1)} %copy-done.73, bf16[512,1408]{1,0:T(8,128)(2,1)} %copy-done.72, bf16[512,1408]{1,0:T(8,128)(2,1)} %get-tuple-element.105, bf16[512,1408]{1,0:T(8,128)(2,1)} %get-tuple-element.104, bf16[512,1024]{1,0:T(8,128)(2,1)} %collective-permute-done.9, ...), kind=kOutput, calls=%fused_computation.10 | convolution fusion | flops 5935726592 | bytes 13631488 | tf_op jit(solution)/shard_map/dot_general | solution.py:62
  220.6 11.5 %collective-permute-done.11 = bf16[512,512]{1,0:T(8,128)(2,1)S(1)} collective-permute-done((bf16[512,512]{1,0:T(8,128)(2,1)S(1)}, bf16[512,512]{1,0:T(8,128)(2,1)S(1)}, u32[]{:S(2)}, u32[]{:S(2)}) %collective-permute-start.11) | collective-permute-done | bytes 524320 | tf_op jit(solution)/shard_map/ppermute | solution.py:338
  234.6 7.9 %collective-permute-done.20 = bf16[512,512]{1,0:T(8,128)(2,1)S(1)} collective-permute-done((bf16[512,512]{1,0:T(8,128)(2,1)S(1)}, bf16[512,512]{1,0:T(8,128)(2,1)S(1)}, u32[]{:S(2)}, u32[]{:S(2)}) %collective-permute-start.20) | collective-permute-done | bytes 524320 | tf_op jit(solution)/shard_map/ppermute | solution.py:338
  250.2 19.1 %mixer_backward.1 = (bf16[1024,1536]{1,0:T(8,128)(2,1)S(1)}, f32[1024,256]{1,0:T(8,128)S(1)}, f32[8,256]{1,0:T(8,128)S(1)}) custom-call(s32[17]{0:T(128)S(1)} %pad_add_fusion.scal, bf16[1024,1536]{1,0:T(8,128)(2,1)S(1)} %copy-done.3, f32[1024,256]{1,0:T(8,128)S(1)} %convolution_add_fusion.z, f32[1024,1]{1,0:T(8,128)S(1)} %copy.47.live, ...), custom_call_target="tpu_custom_call" | custom-call | flops 24999999488 | bytes 20000000 | tf_op jit(solution)/shard_map/mixer_backward/pallas_call | solution.py:315
  286.4 6.6 %collective-permute-done.38 = bf16[64,1408]{1,0:T(8,128)(2,1)S(1)} collective-permute-done((bf16[64,1408]{1,0:T(8,128)(2,1)S(1)}, bf16[64,1408]{1,0:T(8,128)(2,1)S(1)}, u32[]{:S(2)}, u32[]{:S(2)}) %collective-permute-start.38) | collective-permute-done | bytes 180256 | tf_op jit(solution)/shard_map/ppermute | solution.py:369
  295.1 5.4 %multiply_reduce_fusion = (f32[1024]{0:T(1024)S(1)}, bf16[1024,1024]{1,0:T(8,128)(2,1)S(1)}) fusion(bf16[512,1024]{1,0:T(8,128)(2,1)} %collective-permute-done, bf16[512,1024]{1,0:T(8,128)(2,1)S(1)} %copy-done.41, f32[1024,1024]{1,0:T(8,128)S(1)} %fusion.87, f32[1024,1024]{1,0:T(8,128)S(1)} %fusion.88, bf16[1024,1536]{1,0:T(8,128)(2,1)S(1)} %copy-done.5, ...), kind=kOutput, calls=%fused_computation.11 | convolution fusion | flops 3230661632 | bytes 18878464 | tf_op jit(solution)/shard_map/dot_general | solution.py:58
  302.0 5.0 %convolution_convert_fusion = bf16[1024,1536]{1,0:T(8,128)(2,1)S(1)} fusion(bf16[1024,1536]{1,0:T(8,128)(2,1)S(1)} %copy-done.5, bf16[512,1024]{1,0:T(8,128)(2,1)} %collective-permute-done, bf16[512,1024]{1,0:T(8,128)(2,1)S(1)} %copy-done.41), kind=kOutput, calls=%fused_computation.18 | convolution fusion | flops 3226992640 | bytes 8388608 | tf_op jit(solution)/shard_map/dot_general | solution.py:62
  311.9 8.4 %collective-permute-done.33 = bf16[2,64,1408]{2,1,0:T(8,128)(2,1)} collective-permute-done((bf16[2,64,1408]{2,1,0:T(8,128)(2,1)}, bf16[2,64,1408]{2,1,0:T(8,128)(2,1)}, u32[]{:S(2)}, u32[]{:S(2)}) %collective-permute-start.33) | collective-permute-done | bytes 360480 | tf_op jit(solution)/shard_map/ppermute | solution.py:369
  337.1 7.5 %collective-permute-done.35 = bf16[2,64,1408]{2,1,0:T(8,128)(2,1)S(1)} collective-permute-done((bf16[2,64,1408]{2,1,0:T(8,128)(2,1)S(1)}, bf16[2,64,1408]{2,1,0:T(8,128)(2,1)S(1)}, u32[]{:S(2)}, u32[]{:S(2)}) %collective-permute-start.35) | collective-permute-done | bytes 360480 | tf_op jit(solution)/shard_map/ppermute | solution.py:369
  350.7 9.1 %collective-permute-done.23 = bf16[2,2,64,1024]{3,2,1,0:T(8,128)(2,1)S(1)} collective-permute-done((bf16[2,2,64,1024]{3,2,1,0:T(8,128)(2,1)S(1)}, bf16[2,2,64,1024]{3,2,1,0:T(8,128)(2,1)S(1)}, u32[]{:S(2)}, u32[]{:S(2)}) %collective-permute-start.23) | collective-permute-done | bytes 524320 | tf_op jit(solution)/shard_map/ppermute | solution.py:369
  368.5 5.7 %collective-permute-done.31 = bf16[2,64,1024]{2,1,0:T(8,128)(2,1)S(1)} collective-permute-done((bf16[2,64,1024]{2,1,0:T(8,128)(2,1)S(1)}, bf16[2,64,1024]{2,1,0:T(8,128)(2,1)S(1)}, u32[]{:S(2)}, u32[]{:S(2)}) %collective-permute-start.31) | collective-permute-done | bytes 262176 | tf_op jit(solution)/shard_map/ppermute | solution.py:369
  378.9 7.1 %collective-permute-done.32 = bf16[64,1024]{1,0:T(8,128)(2,1)S(1)} collective-permute-done((bf16[64,1024]{1,0:T(8,128)(2,1)S(1)}, bf16[64,1024]{1,0:T(8,128)(2,1)S(1)}, u32[]{:S(2)}, u32[]{:S(2)}) %collective-permute-start.32) | collective-permute-done | bytes 131104 | tf_op jit(solution)/shard_map/ppermute | solution.py:369
  388.9 5.5 %collective-permute-done.28 = f32[214,128]{1,0:T(8,128)S(1)} collective-permute-done((f32[214,128]{1,0:T(8,128)S(1)}, f32[214,128]{1,0:T(8,128)S(1)}, u32[]{:S(2)}, u32[]{:S(2)}) %collective-permute-start.28) | collective-permute-done | bytes 109600 | tf_op jit(solution)/shard_map/ppermute | solution.py:412
  (368 shorter events, 171.0 us)
Async XLA Ops:
  7.2 69.0 %all-gather.3.cloned.1.call-start = ((), (), s32[]{:S(2)}) async-start(), calls=%async_computation | async-start | bytes 4456448 | tf_op jit(solution)/shard_map/all_gather | solution.py:459
  12.2 135.1 %all-gather.5.cloned.1.call-start = ((), (), s32[]{:S(2)}) async-start(), calls=%async_computation.1 | async-start | bytes 6127616 | tf_op jit(solution)/shard_map/all_gather | solution.py:467
  14.0 62.2 %collective-permute-start.1 = (bf16[512,1024]{1,0:T(8,128)(2,1)}, bf16[512,1024]{1,0:T(8,128)(2,1)}, u32[]{:S(2)}, u32[]{:S(2)}) collective-permute-start(bf16[512,1024]{1,0:T(8,128)(2,1)} %param.21), channel_id=1, source_target_pairs={{0,1},{1,0},{2,3},{3,2},{4,5},{5,4},{6,7},{7,6},{8,9},{9,8},{10,11... | collective-permute-start | bytes 3145736 | tf_op jit(solution)/shard_map/ppermute | solution.py:338
  18.9 44.1 %collective-permute-start = (bf16[512,1024]{1,0:T(8,128)(2,1)S(1)}, bf16[512,1024]{1,0:T(8,128)(2,1)}, u32[]{:S(2)}, u32[]{:S(2)}) collective-permute-start(bf16[512,1024]{1,0:T(8,128)(2,1)S(1)} %fusion.30), channel_id=1, source_target_pairs={{0,1},{1,0},{2,3},{3,2},{4,5},{5,4},{6,7},{7,6},{8,9},{9,8},{10,11... | collective-permute-start | bytes 3145736 | tf_op jit(solution)/shard_map/ppermute | solution.py:338
  19.0 16.6 %collective-permute-start.5 = (bf16[64,1408]{1,0:T(8,128)(2,1)S(1)}, bf16[64,1408]{1,0:T(8,128)(2,1)S(1)}, u32[]{:S(2)}, u32[]{:S(2)}) collective-permute-start(bf16[64,1408]{1,0:T(8,128)(2,1)S(1)} %copy-done.48), channel_id=1, source_target_pairs={{0,16},{2,18},{4,20},{6,22},{8,24},{10,26},{12,28},{14,30},{16,0},... | collective-permute-start | bytes 540680 | tf_op jit(solution)/shard_map/ppermute | solution.py:393
  47.6 26.4 %collective-permute-start.7 = (bf16[2,2,64,1408]{3,2,1,0:T(8,128)(2,1)}, bf16[2,2,64,1408]{3,2,1,0:T(8,128)(2,1)}, u32[]{:S(2)}, u32[]{:S(2)}) collective-permute-start(bf16[2,2,64,1408]{3,2,1,0:T(8,128)(2,1)} %pad_maximum_fusion.7), channel_id=1, source_target_pairs={{0,4},{2,6},{4,0},{6,2},{8,12},{10,14},{12,8},{14,10},{16,20},{18,... | collective-permute-start | bytes 2162696 | tf_op jit(solution)/shard_map/ppermute | solution.py:393
  91.2 14.4 %collective-permute-start.4 = (bf16[512,512]{1,0:T(8,128)(2,1)S(1)}, bf16[512,512]{1,0:T(8,128)(2,1)S(1)}, u32[]{:S(2)}, u32[]{:S(2)}) collective-permute-start(bf16[512,512]{1,0:T(8,128)(2,1)S(1)} %collective-permute-done.3), channel_id=1, source_target_pairs={{0,2},{2,0},{4,6},{6,4},{8,10},{10,8},{12,14},{14,12},{16,18},{18,... | collective-permute-start | bytes 1572872 | tf_op jit(solution)/shard_map/ppermute | solution.py:403
  105.4 18.1 %collective-permute-start.8 = (bf16[2,2,2,64,1408]{4,3,2,1,0:T(8,128)(2,1)}, bf16[2,2,2,64,1408]{4,3,2,1,0:T(8,128)(2,1)}, u32[]{:S(2)}, u32[]{:S(2)}) collective-permute-start(bf16[2,2,2,64,1408]{4,3,2,1,0:T(8,128)(2,1)} %pad_maximum_fusion.4), channel_id=1, source_target_pairs={{0,2},{2,0},{4,6},{6,4},{8,10},{10,8},{12,14},{14,12},{16,18},{18,... | collective-permute-start | bytes 4325384 | tf_op jit(solution)/shard_map/ppermute | solution.py:393
  122.1 25.2 %collective-permute-start.9 = (bf16[512,1024]{1,0:T(8,128)(2,1)}, bf16[512,1024]{1,0:T(8,128)(2,1)}, u32[]{:S(2)}, u32[]{:S(2)}) collective-permute-start(bf16[512,1024]{1,0:T(8,128)(2,1)} %multiply_convert_fusion.6), channel_id=1, source_target_pairs={{0,1},{1,0},{2,3},{3,2},{4,5},{5,4},{6,7},{7,6},{8,9},{9,8},{10,11... | collective-permute-start | bytes 3145736 | tf_op jit(solution)/shard_map/ppermute | solution.py:338
  162.7 34.4 %collective-permute-start.10 = (bf16[512,1024]{1,0:T(8,128)(2,1)}, bf16[512,1024]{1,0:T(8,128)(2,1)S(1)}, u32[]{:S(2)}, u32[]{:S(2)}) collective-permute-start(bf16[512,1024]{1,0:T(8,128)(2,1)} %fusion.44), channel_id=1, source_target_pairs={{0,1},{1,0},{2,3},{3,2},{4,5},{5,4},{6,7},{7,6},{8,9},{9,8},{10,11... | collective-permute-start | bytes 3145736 | tf_op jit(solution)/shard_map/ppermute | solution.py:338
  179.7 33.8 %collective-permute-start.12 = (bf16[8,64,1408]{2,1,0:T(8,128)(2,1)}, bf16[8,64,1408]{2,1,0:T(8,128)(2,1)}, u32[]{:S(2)}, u32[]{:S(2)}) collective-permute-start(bf16[8,64,1408]{2,1,0:T(8,128)(2,1)} %dynamic-slice_bitcast_fusion.2), channel_id=1, source_target_pairs={{0,2},{2,0},{4,6},{6,4},{8,10},{10,8},{12,14},{14,12},{16,18},{18,... | collective-permute-start | bytes 4325384 | tf_op jit(solution)/shard_map/ppermute | solution.py:347
  194.2 49.2 %collective-permute-start.14 = (bf16[8,64,2816]{2,1,0:T(8,128)(2,1)}, bf16[8,64,2816]{2,1,0:T(8,128)(2,1)}, u32[]{:S(2)}, u32[]{:S(2)}) collective-permute-start(bf16[8,64,2816]{2,1,0:T(8,128)(2,1)} %dynamic-slice_bitcast_fusion), channel_id=1, source_target_pairs={{0,2},{2,0},{4,6},{6,4},{8,10},{10,8},{12,14},{14,12},{16,18},{18,... | collective-permute-start | bytes 8650760 | tf_op jit(solution)/shard_map/ppermute | solution.py:347
  215.9 18.5 %collective-permute-start.13 = (bf16[2,2,64,1408]{3,2,1,0:T(8,128)(2,1)S(1)}, bf16[2,2,64,1408]{3,2,1,0:T(8,128)(2,1)S(1)}, u32[]{:S(2)}, u32[]{:S(2)}) collective-permute-start(bf16[2,2,64,1408]{3,2,1,0:T(8,128)(2,1)S(1)} %dynamic-slice_bitcast_fusion.6), channel_id=1, source_target_pairs={{0,4},{2,6},{4,0},{6,2},{8,12},{10,14},{12,8},{14,10},{16,20},{18,... | collective-permute-start | bytes 2162696 | tf_op jit(solution)/shard_map/ppermute | solution.py:369
  217.2 14.8 %collective-permute-start.11 = (bf16[512,512]{1,0:T(8,128)(2,1)S(1)}, bf16[512,512]{1,0:T(8,128)(2,1)S(1)}, u32[]{:S(2)}, u32[]{:S(2)}) collective-permute-start(bf16[512,512]{1,0:T(8,128)(2,1)S(1)} %convolution_convert_fusion.6), channel_id=1, source_target_pairs={{0,1},{1,0},{2,3},{3,2},{4,5},{5,4},{6,7},{7,6},{8,9},{9,8},{10,11... | collective-permute-start | bytes 1572872 | tf_op jit(solution)/shard_map/ppermute | solution.py:338
  219.3 23.2 %collective-permute-start.20 = (bf16[512,512]{1,0:T(8,128)(2,1)S(1)}, bf16[512,512]{1,0:T(8,128)(2,1)S(1)}, u32[]{:S(2)}, u32[]{:S(2)}) collective-permute-start(bf16[512,512]{1,0:T(8,128)(2,1)S(1)} %slice.115), channel_id=1, source_target_pairs={{0,1},{1,0},{2,3},{3,2},{4,5},{5,4},{6,7},{7,6},{8,9},{9,8},{10,11... | collective-permute-start | bytes 1572872 | tf_op jit(solution)/shard_map/ppermute | solution.py:338
  246.1 77.1 %collective-permute-start.16 = (bf16[512,1024]{1,0:T(8,128)(2,1)}, bf16[512,1024]{1,0:T(8,128)(2,1)}, u32[]{:S(2)}, u32[]{:S(2)}) collective-permute-start(bf16[512,1024]{1,0:T(8,128)(2,1)} %convolution_convert_fusion.3), channel_id=1, source_target_pairs={{0,1},{1,0},{2,3},{3,2},{4,5},{5,4},{6,7},{7,6},{8,9},{9,8},{10,11... | collective-permute-start | bytes 3145736 | tf_op jit(solution)/shard_map/ppermute | solution.py:338
  247.7 46.1 %collective-permute-start.15 = (bf16[2,2,64,1408]{3,2,1,0:T(8,128)(2,1)}, bf16[2,2,64,1408]{3,2,1,0:T(8,128)(2,1)}, u32[]{:S(2)}, u32[]{:S(2)}) collective-permute-start(bf16[2,2,64,1408]{3,2,1,0:T(8,128)(2,1)} %dynamic-slice_bitcast_fusion.5), channel_id=1, source_target_pairs={{0,4},{2,6},{4,0},{6,2},{8,12},{10,14},{12,8},{14,10},{16,20},{18,... | collective-permute-start | bytes 2162696 | tf_op jit(solution)/shard_map/ppermute | solution.py:369
  270.9 39.3 %collective-permute-start.21 = (bf16[2,2,64,1408]{3,2,1,0:T(8,128)(2,1)}, bf16[2,2,64,1408]{3,2,1,0:T(8,128)(2,1)}, u32[]{:S(2)}, u32[]{:S(2)}) collective-permute-start(bf16[2,2,64,1408]{3,2,1,0:T(8,128)(2,1)} %dynamic-slice_bitcast_fusion.4), channel_id=1, source_target_pairs={{0,4},{2,6},{4,0},{6,2},{8,12},{10,14},{12,8},{14,10},{16,20},{18,... | collective-permute-start | bytes 2162696 | tf_op jit(solution)/shard_map/ppermute | solution.py:369
  301.7 48.3 %collective-permute-start.17 = (bf16[512,1024]{1,0:T(8,128)(2,1)}, bf16[512,1024]{1,0:T(8,128)(2,1)S(1)}, u32[]{:S(2)}, u32[]{:S(2)}) collective-permute-start(bf16[512,1024]{1,0:T(8,128)(2,1)} %slice.113), channel_id=1, source_target_pairs={{0,1},{1,0},{2,3},{3,2},{4,5},{5,4},{6,7},{7,6},{8,9},{9,8},{10,11... | collective-permute-start | bytes 3145736 | tf_op jit(solution)/shard_map/ppermute | solution.py:338
  308.3 23.9 %collective-permute-start.18 = (bf16[8,64,1536]{2,1,0:T(8,128)(2,1)}, bf16[8,64,1536]{2,1,0:T(8,128)(2,1)}, u32[]{:S(2)}, u32[]{:S(2)}) collective-permute-start(bf16[8,64,1536]{2,1,0:T(8,128)(2,1)} %dynamic-slice_bitcast_fusion.1), channel_id=1, source_target_pairs={{0,2},{2,0},{4,6},{6,4},{8,10},{10,8},{12,14},{14,12},{16,18},{18,... | collective-permute-start | bytes 4718600 | tf_op jit(solution)/shard_map/ppermute | solution.py:347
  334.9 14.9 %collective-permute-start.22 = (bf16[2,2,64,1024]{3,2,1,0:T(8,128)(2,1)S(1)}, bf16[2,2,64,1024]{3,2,1,0:T(8,128)(2,1)S(1)}, u32[]{:S(2)}, u32[]{:S(2)}) collective-permute-start(bf16[2,2,64,1024]{3,2,1,0:T(8,128)(2,1)S(1)} %dynamic-slice_bitcast_fusion.8), channel_id=1, source_target_pairs={{0,4},{2,6},{4,0},{6,2},{8,12},{10,14},{12,8},{14,10},{16,20},{18,... | collective-permute-start | bytes 1572872 | tf_op jit(solution)/shard_map/ppermute | solution.py:369
  335.7 24.0 %collective-permute-start.23 = (bf16[2,2,64,1024]{3,2,1,0:T(8,128)(2,1)S(1)}, bf16[2,2,64,1024]{3,2,1,0:T(8,128)(2,1)S(1)}, u32[]{:S(2)}, u32[]{:S(2)}) collective-permute-start(bf16[2,2,64,1024]{3,2,1,0:T(8,128)(2,1)S(1)} %dynamic-slice_bitcast_fusion.7), channel_id=1, source_target_pairs={{0,4},{2,6},{4,0},{6,2},{8,12},{10,14},{12,8},{14,10},{16,20},{18,... | collective-permute-start | bytes 1572872 | tf_op jit(solution)/shard_map/ppermute | solution.py:369
  344.7 21.5 %collective-permute-start.36 = (bf16[64,1408]{1,0:T(8,128)(2,1)S(1)}, bf16[64,1408]{1,0:T(8,128)(2,1)S(1)}, u32[]{:S(2)}, u32[]{:S(2)}) collective-permute-start(bf16[64,1408]{1,0:T(8,128)(2,1)S(1)} %dynamic-slice_bitcast_fusion.15), channel_id=1, source_target_pairs={{0,16},{2,18},{4,20},{6,22},{8,24},{10,26},{12,28},{14,30},{16,0},... | collective-permute-start | bytes 540680 | tf_op jit(solution)/shard_map/ppermute | solution.py:369
  361.8 16.3 %collective-permute-start.29 = (bf16[2,64,1024]{2,1,0:T(8,128)(2,1)S(1)}, bf16[2,64,1024]{2,1,0:T(8,128)(2,1)S(1)}, u32[]{:S(2)}, u32[]{:S(2)}) collective-permute-start(bf16[2,64,1024]{2,1,0:T(8,128)(2,1)S(1)} %dynamic-slice_bitcast_fusion.13), channel_id=1, source_target_pairs={{0,8},{2,10},{4,12},{6,14},{8,0},{10,2},{12,4},{14,6},{16,24},{18,... | collective-permute-start | bytes 786440 | tf_op jit(solution)/shard_map/ppermute | solution.py:369
  (98 other events, 955.2 us)
Sparse Core Ops, SparseCore 0:
  12.2 62.8 all-gather.2
  78.0 59.5 all-gather.4

commit v4 on v3

--- a/solution.py
+++ b/solution.py
@@ -14,6 +14,8 @@
 LEVELS = 6
 KINDS = LEVELS + 2
 STEP_SPANS = 2
+LANES = 128
+UNPACK_FLOPS = 3 * 10**10
 
 epsilon = 1e-06
 head_epsilon = 1.0
@@ -156,9 +158,12 @@
     mixture,
     states,
     grad_gated,
+    latent,
+    up,
     grad_projected,
-    grad_z,
     grad_gain,
+    grad_up,
+    grad_bias,
     grad_state,
 ):
     step = pl.program_id(0)
@@ -170,6 +175,8 @@
     def _():
         grad_state[...] = jnp.zeros_like(grad_state)
         grad_gain[...] = jnp.zeros_like(grad_gain)
+        grad_up[...] = jnp.zeros_like(grad_up)
+        grad_bias[...] = jnp.zeros_like(grad_bias)
 
     masks, diagonal = pair_levels()
     head_gain = gain[...]
@@ -244,7 +251,12 @@
             exponents.append(jnp.concatenate(exponents_head, axis=0).astype(bf16))
             grad_state[head] = keep * (leaving * fading + tn(grad_mixed, whole_queries))
         grad_decays = tn(sums[:, :SPAN], jnp.concatenate(exponents, axis=1))
-        grad_z[rows, :] = grad_decays * jax.nn.sigmoid(-z_part) * (1.0 / gate_scale)
+        grad_z = grad_decays * jax.nn.sigmoid(-z_part) * (1.0 / gate_scale)
+        grad_bias[...] += jnp.sum(grad_z.reshape(SPAN // 8, 8, key_width), axis=0)
+        grad_z_low = grad_z.astype(bf16)
+        grad_up[...] += tn(latent[rows, :], grad_z_low)
+        latent_cols = slice(2 * key_width + 2 * value_width, grad_projected.shape[1])
+        grad_projected[rows, latent_cols] = nt(grad_z_low, up[...]).astype(bf16)
 
 
 def mixer_specs(length, projected_width, key_width, value_width, reverse):
@@ -273,6 +285,10 @@
             (STEP_SPANS, heads, VDIM, KDIM), lambda step, scal: (natural(step), 0, 0, 0)
         ),
         gain_grad=pl.BlockSpec((8, VDIM), whole),
+        latent=pl.BlockSpec((step_rows, LANES), by_rows),
+        up=pl.BlockSpec((LANES, key_width), whole),
+        extended=pl.BlockSpec((step_rows, projected_width + LANES), by_rows),
+        bias_grad=pl.BlockSpec((8, key_width), whole),
     )
 
 
@@ -305,33 +321,62 @@
     )(scal, projected, z, live, gain, sums)
 
 
-def mixer_backward(scal, projected, z, live, gain, sums, mixture, states, grad_gated):
+def mixer_backward(
+    scal, projected, z, live, gain, sums, mixture, states, grad_gated, latent, up
+):
     length, projected_width = projected.shape
     key_width = z.shape[1]
     heads = key_width // KDIM
     value_width = heads * VDIM
     specs = mixer_specs(length, projected_width, key_width, value_width, True)
     names = ("projected", "z", "live", "gain", "sums", "values", "states", "values")
+    names += ("latent", "up")
     return pl.pallas_call(
         functools.partial(backward_kernel, heads),
         grid_spec=pltpu.PrefetchScalarGridSpec(
             num_scalar_prefetch=1,
             grid=(specs["steps"],),
             in_specs=[specs[name] for name in names],
-            out_specs=[specs[name] for name in ("projected", "z", "gain_grad")],
+            out_specs=[specs[name] for name in ("extended", "gain_grad", "up", "bias_grad")],
             scratch_shapes=[pltpu.VMEM((heads, VDIM, KDIM), f32)],
         ),
         out_shape=[
-            jax.ShapeDtypeStruct((length, projected_width), bf16),
-            jax.ShapeDtypeStruct((length, key_width), f32),
+            jax.ShapeDtypeStruct((length, projected_width + LANES), bf16),
             jax.ShapeDtypeStruct((8, VDIM), f32),
+            jax.ShapeDtypeStruct((LANES, key_width), f32),
+            jax.ShapeDtypeStruct((8, key_width), f32),
         ],
         compiler_params=pltpu.CompilerParams(vmem_limit_bytes=40 * 1024 * 1024),
         cost_estimate=pl.CostEstimate(
             flops=25 * 10**9, bytes_accessed=20 * 10**6, transcendentals=4 * 10**6
         ),
         name="mixer_backward",
-    )(scal, projected, z, live, gain, sums, mixture, states, grad_gated)
+    )(scal, projected, z, live, gain, sums, mixture, states, grad_gated, latent, up)
+
+
+def unpack_kernel(packed, *parts):
+    width = parts[0].shape[1]
+    for index, part in enumerate(parts):
+        part[...] = packed[:, index * width : (index + 1) * width].astype(f32)
+
+
+def unpack_thirds(packed):
+    rows, width = packed.shape[0], packed.shape[1] // 3
+    return pl.pallas_call(
+        unpack_kernel,
+        out_shape=[jax.ShapeDtypeStruct((rows, width), f32)] * 3,
+        compiler_params=pltpu.CompilerParams(vmem_limit_bytes=8 * 1024 * 1024),
+        cost_estimate=pl.CostEstimate(
+            flops=UNPACK_FLOPS, bytes_accessed=3 * 10**6, transcendentals=0
+        ),
+        name="unpack_thirds",
+    )(packed)
+
+
+def lane_pad(values, axis):
+    widths = [(0, 0), (0, 0)]
+    widths[axis] = (0, LANES - values.shape[axis])
+    return jnp.pad(values, widths)
 
 
 def swap_tensor(values):
@@ -383,25 +428,17 @@
     return jnp.stack([first, second], axis=axis)
 
 
-def gather_doubling(values):
-    count = lax.axis_size("dp")
-    place = lax.axis_index("dp")
-    stages = count.bit_length() - 1
-    held = values
-    for stage in range(stages):
-        bit = count >> (stage + 1)
-        arrived = lax.ppermute(held, "dp", [(i, i ^ bit) for i in range(count)])
-        held = both_ways((place // bit) % 2, held, arrived, stage)
-    return held.reshape(values.shape[0] * count, values.shape[1])
-
-
-def swap_whole(values):
+def swap_half(values):
+    half = values.shape[0] // 2
+    parity = lax.axis_index("dp") % 2
+    return swap_tensor(lax.dynamic_slice_in_dim(values, parity * half, half, 0))
+
+
+def join_halves(mine):
     count = lax.axis_size("dp")
     parity = lax.axis_index("dp") % 2
-    half = values.shape[0] // 2
-    mine = swap_tensor(lax.dynamic_slice_in_dim(values, parity * half, half, 0))
     other = lax.ppermute(mine, "dp", [(i, i ^ 1) for i in range(count)])
-    return both_ways(parity, mine, other, 0).reshape(values.shape)
+    return both_ways(parity, mine, other, 0).reshape(mine.shape[0] * 2, mine.shape[1])
 
 
 def butterfly_sum(values):
@@ -464,10 +501,11 @@
         axis=0,
         tiled=True,
     )
-    gate_up_full = lax.all_gather(
-        jnp.concatenate([feed_gate, feed_up], axis=1), "dp", axis=0, tiled=True
-    )
-    feed_down_full = gather_doubling(feed_down)
+    feed_all = lax.all_gather(
+        jnp.concatenate([feed_gate, feed_up, feed_down], axis=1), "dp", axis=0, tiled=True
+    )
+    gate_up_full = feed_all[:, : 2 * feed_width]
+    feed_down_full = feed_all[:, 2 * feed_width :]
     gain_in = mixer_gain.astype(f32)
     token_values = tokens.astype(f32)
     normed_in, inverse_in = rms_forward(token_values, gain_in)
@@ -478,7 +516,7 @@
     projected_width = 2 * key_width + 2 * value_width
     joined_in = joined[:, :projected_width]
     output_half = joined[:, projected_width:]
-    output_other = swap_whole(output_half)
+    output_piece = swap_half(output_half)
 
     normed_all = jnp.concatenate([normed_low, normed_other], axis=0)
     projected = nn(normed_all, joined_in).astype(bf16)
@@ -488,6 +526,8 @@
     z = jnp.dot(latent, up_local, precision=highest) + bias_local.astype(f32)
     gated, mixture, states = mixer_forward(scal, projected, z, live, gain_head, sums)
 
+    gated, output_piece = lax.optimization_barrier((gated, output_piece))
+    output_other = join_halves(output_piece)
     gated_own = gated[:own]
     gated_rest = swap_tensor(gated[own:])
     attended = nt(gated_own, output_half) + nt(gated_rest, output_other)
@@ -531,16 +571,14 @@
     cotangent_all = jnp.concatenate([cotangent, cotangent_other], axis=0)
     hidden_all = jnp.concatenate([hidden_own, hidden_other], axis=0)
     grad_both_all = jnp.concatenate([grad_both_own, grad_both_other], axis=0)
-    down_sum = by_chip(chip_sum(tn(cotangent_all, hidden_all).astype(bf16)))
-    down_sum = halving_stage(down_sum, 0)
-    both_chip = chip_sum(tn(mid_all, grad_both_all).astype(bf16))
+    feed_grads = jnp.concatenate(
+        [
+            tn(mid_all, grad_both_all).astype(bf16),
+            tn(cotangent_all, hidden_all).astype(bf16),
+        ],
+        axis=1,
+    )
     fed_send = nt(hidden_other, feed_down_full).astype(bf16)
-    grad_gated, down_sum, both_chip, fed_send = lax.optimization_barrier(
-        (grad_gated, down_sum, both_chip, fed_send)
-    )
-    gate_sum = halving_stage(by_chip(both_chip[:, :feed_width]), 0)
-    up_sum = halving_stage(by_chip(both_chip[:, feed_width:]), 0)
-    fed_back = swap_tensor(fed_send)
     output_chip = chip_sum(
         jnp.concatenate(
             [
@@ -550,38 +588,44 @@
             axis=1,
         )
     )
+    grad_gated, feed_grads, fed_send, output_chip = lax.optimization_barrier(
+        (grad_gated, feed_grads, fed_send, output_chip)
+    )
+    feed_sum = lax.psum_scatter(feed_grads, "dp", scatter_dimension=0, tiled=True)
+    fed_back = swap_tensor(fed_send)
     output_back = swap_tensor(output_chip[:, value_width:])
-    grad_projected, grad_z, grad_gain_rows = mixer_backward(
-        scal, projected, z, live, gain_head, sums, mixture, states, grad_gated
-    )
-    grad_projected, gate_sum = lax.optimization_barrier((grad_projected, gate_sum))
-    projected_chip = chip_sum(tn(normed_all, grad_projected).astype(bf16))
+    grad_projected, grad_gain_rows, grad_up_rows, grad_bias_rows = mixer_backward(
+        scal,
+        projected,
+        z,
+        live,
+        gain_head,
+        sums,
+        mixture,
+        states,
+        grad_gated,
+        lane_pad(latent, 1).astype(bf16),
+        lane_pad(up_local, 0).astype(bf16),
+    )
+    grad_joined = tn(normed_all, grad_projected).astype(bf16)
+    grad_joined, output_back = lax.optimization_barrier((grad_joined, output_back))
+    low_rank = decay_down.shape[1]
+    grad_decay_down = grad_joined[:, projected_width : projected_width + low_rank].astype(f32)
     output_total = output_chip[:, :value_width].astype(f32) + output_back.astype(f32)
-    joined_chip = jnp.concatenate([projected_chip, output_total.astype(bf16)], axis=1)
-    joined_chip, up_sum = lax.optimization_barrier((joined_chip, up_sum))
+    joined_chip = jnp.concatenate(
+        [chip_sum(grad_joined[:, :projected_width]), output_total.astype(bf16)], axis=1
+    )
     joined_sums = [
         halving_stage(by_chip(piece), 0) for piece in jnp.split(joined_chip, 2, axis=1)
     ]
-    hidden_late, grad_projected = lax.optimization_barrier((hidden_own, grad_projected))
+
+    joined_back = jnp.concatenate([joined_in, lane_pad(decay_down, 1)], axis=1)
+    normed_part = nt(grad_projected, joined_back)
+    grad_mixer_gain = jnp.sum(normed_part * normed_all.astype(f32), axis=0) / gain_in
+    normed_part, fed_back = lax.optimization_barrier((normed_part.astype(bf16), fed_back))
+    hidden_late, normed_part = lax.optimization_barrier((hidden_own, normed_part))
     fed = nt(hidden_late, feed_down_full) + fed_back.astype(f32)
     output = (middle + fed).astype(bf16)
-
-    grad_latent = lax.dot_general(
-        grad_z, up_local, (((1,), (1,)), ((), ())), precision=highest, preferred_element_type=f32
-    )
-    grad_up_local = lax.dot_general(
-        latent, grad_z, (((0,), (0,)), ((), ())), precision=highest, preferred_element_type=f32
-    )
-    grad_bias_local = jnp.sum(grad_z, axis=0)
-    latent_high = grad_latent.astype(bf16)
-    latent_rest = (grad_latent - latent_high.astype(f32)).astype(bf16)
-    grad_down_parts = tn(normed_all, jnp.concatenate([latent_high, latent_rest], axis=1))
-    low_rank = decay_down.shape[1]
-    grad_decay_down = grad_down_parts[:, :low_rank] + grad_down_parts[:, low_rank:]
-    from_latent = nt(latent_high, decay_down) + nt(latent_rest, decay_down)
-    normed_part = nt(grad_projected, joined_in) + from_latent
-    grad_mixer_gain = jnp.sum(normed_part * normed_all.astype(f32), axis=0) / gain_in
-    normed_part = normed_part.astype(bf16)
     normed_back, joined_sums[1] = lax.optimization_barrier(
         (swap_tensor(normed_part[own:]), joined_sums[1])
     )
@@ -590,10 +634,10 @@
     input_grad = grad_middle + grad_in_part
 
     up_full = lax.dynamic_update_slice_in_dim(
-        jnp.zeros(decay_up.shape, f32), grad_up_local, half_index * key_width, 1
+        jnp.zeros(decay_up.shape, f32), grad_up_rows[:low_rank], half_index * key_width, 1
     )
     bias_full = lax.dynamic_update_slice_in_dim(
-        jnp.zeros(decay_bias.shape, f32), grad_bias_local, half_index * key_width, 0
+        jnp.zeros(decay_bias.shape, f32), jnp.sum(grad_bias_rows, axis=0), half_index * key_width, 0
     )
     small = (
         grad_mixer_gain,
@@ -606,7 +650,6 @@
     flat = jnp.concatenate([part.reshape(-1, 128) for part in small], axis=0)
     flat, joined_sums[0] = lax.optimization_barrier((flat, joined_sums[0]))
     flat = butterfly_sum(flat)
-    down_sum, gate_sum, up_sum = (halving_rest(held) for held in (down_sum, gate_sum, up_sum))
     joined_sum = jnp.concatenate([halving_rest(held) for held in joined_sums], axis=1)
     small_sums = []
     row = 0
@@ -628,9 +671,7 @@
         small_sums[3],
         small_sums[4],
         small_sums[5],
-        gate_sum,
-        up_sum,
-        down_sum,
+        *unpack_thirds(feed_sum),
     )
 
 

time: 411 us -> 372 us (0.905)
  starting transfers between devices: 42.2 us -> 20.7 us
  other arithmetic: 37.7 us -> 28.1 us
  waiting for transfers between devices: 164 us -> 157 us
  local copies, waits for them, and re-layouts: 38.1 us -> 32.4 us
    ppermute x5 -> x1, waiting for transfers between devices: 30.1 us -> 1.06 us  [join_halves(): other = lax.ppermute(mine, 'dp', [(i, i ^ 1) for i in range(count)])]
    ppermute x11, waiting for transfers between devices: 70 us -> 95.9 us  [swap_tensor(): return lax.ppermute(values, 'tensor', [(0, 1), (1, 0)])]
    ppermute x15 -> x6, waiting for transfers between devices: 57.4 us -> 40.5 us  [halving_stage(): arrived = lax.ppermute(sent, 'dp', [(i, i ^ bit) for i in range(count)])]
    ppermute x15 -> x6, starting transfers between devices: 19.6 us -> 6.4 us  [halving_stage(): arrived = lax.ppermute(sent, 'dp', [(i, i ^ bit) for i in range(count)])]
    all_gather x1, waiting for transfers between devices: 0.01 us -> 9.52 us  [on_device(): lax.all_gather(jnp.concatenate([feed_gate, feed_up, feed_down], axis=1),...]
    ppermute x5 -> x1, starting transfers between devices: 7.26 us -> 0.01 us  [join_halves(): other = lax.ppermute(mine, 'dp', [(i, i ^ 1) for i in range(count)])]
    another operation x10 -> x2, other arithmetic: 8.45 us -> 1.38 us  [both_ways(): return jnp.stack([first, second], axis=axis)]
    convert_element_type x10 -> x4, other arithmetic: 6 us -> 0.54 us  [halving_stage(): return total if stage == stages - 1 else total.astype(bf16)]
  transfers between devices with their start and end apart: 41 -> 27, of which waited for: 22 -> 14; matrix products, arithmetic and copies ran while one was open for 29% -> 24% of each run, Pallas kernels for 8% -> 9%
where the time goes in v4:
time: 372 us; the launch traced here: 368 us
  waiting for transfers between devices  157 us (42%)
  matrix products  80 us (22%)
  Pallas kernels  34 us (9%)
  local copies, waits for them, and re-layouts  32.4 us (9%)
  other arithmetic  28.1 us (8%)
  starting transfers between devices  20.7 us (6%)
  between operations  15.3 us (4%)
    ppermute x11, waiting for transfers between devices, swap_tensor(): return lax.ppermute(values, 'tensor', [(0, 1), (1, 0)])  95.9 us
    ppermute x6, waiting for transfers between devices, halving_stage(): arrived = lax.ppermute(sent, 'dp', [(i, i ^ bit) for i in range(count)])  40.5 us
    dot_general x8, matrix products, nn(): lax.dot_general(left, right, (((1,), (0,)), ((), ())), preferred_element_...  29.7 us
    dot_general x7, matrix products, nt(): lax.dot_general(left, right, (((1,), (1,)), ((), ())), preferred_element_...  27.7 us
    dot_general x5, matrix products, tn(): lax.dot_general(left, right, (((0,), (0,)), ((), ())), preferred_element_...  22.1 us
    pallas_call x1, Pallas kernels, mixer_backward(): pl.pallas_call(functools.partial(backward_kernel, heads), grid_spec=pltpu...  21.4 us
    unnamed x112, local copies, waits for them, and re-layouts  15.5 us
    ppermute x11, starting transfers between devices, swap_tensor(): return lax.ppermute(values, 'tensor', [(0, 1), (1, 0)])  11.8 us
  transfers between devices with their start and end apart: 27, of which 14 were waited for; matrix products, arithmetic and copies ran while one was open for 24% of the time, Pallas kernels for 9%

profile of v4, /device:TPU:0, one launch (start us, length us, event | category | flops | bytes accessed | tf_op | source)
XLA Modules:
  0.0 367.6 jit_solution(10659943238275005424)
XLA Ops:
  20.1 43.2 %collective-permute-done = bf16[512,1024]{1,0:T(8,128)(2,1)} collective-permute-done((bf16[512,1024]{1,0:T(8,128)(2,1)S(1)}, bf16[512,1024]{1,0:T(8,128)(2,1)}, u32[]{:S(2)}, u32[]{:S(2)}) %collective-permute-start) | collective-permute-done | bytes 1048608 | tf_op jit(solution)/shard_map/ppermute | solution.py:383
  69.0 5.6 %convolution_convert_fusion.2.projected = bf16[1024,1536]{1,0:T(8,128)(2,1)S(1)} fusion(bf16[512,1024]{1,0:T(8,128)(2,1)} %collective-permute-done, bf16[512,1024]{1,0:T(8,128)(2,1)S(1)} %fusion.38, bf16[1024,2048]{1,0:T(8,128)(2,1)} %all-gather.3.cloned.1.call-done), kind=kOutput, calls=%fused_computation.20 | convolution fusion | flops 3226992640 | bytes 8388608 | tf_op jit(solution)/shard_map/dot_general | solution.py:56
  74.6 11.6 %mixer_forward.1 = (bf16[1024,512]{1,0:T(8,128)(2,1)S(1)}, bf16[1024,512]{1,0:T(8,128)(2,1)S(1)}, bf16[16,2,256,128]{3,2,1,0:T(8,128)(2,1)S(1)}) custom-call(s32[17]{0:T(128)S(1)} %pad_add_fusion.scal, bf16[1024,1536]{1,0:T(8,128)(2,1)S(1)} %convolution_convert_fusion.2.projected, f32[1024,256]{1,0:T(8,128)S(1)} %convolution_add_fusion.z, ...), custom_call_target="tpu_custom_call" | custom-call | flops 10000000000 | bytes 15000000 | tf_op jit(solution)/shard_map/mixer_forward/pallas_call | solution.py:302
  92.3 11.7 %collective-permute-done.3 = bf16[512,512]{1,0:T(8,128)(2,1)S(1)} collective-permute-done((bf16[512,512]{1,0:T(8,128)(2,1)}, bf16[512,512]{1,0:T(8,128)(2,1)S(1)}, u32[]{:S(2)}, u32[]{:S(2)}) %collective-permute-start.3) | collective-permute-done | bytes 524320 | tf_op jit(solution)/shard_map/ppermute | solution.py:383
  108.6 24.9 %collective-permute-done.5 = bf16[512,1024]{1,0:T(8,128)(2,1)} collective-permute-done((bf16[512,1024]{1,0:T(8,128)(2,1)}, bf16[512,1024]{1,0:T(8,128)(2,1)}, u32[]{:S(2)}, u32[]{:S(2)}) %collective-permute-start.5) | collective-permute-done | bytes 1048608 | tf_op jit(solution)/shard_map/ppermute | solution.py:383
  133.4 9.5 %all-gather.5.cloned.1.call-done = bf16[1024,4224]{1,0:T(8,128)(2,1)} async-done(((bf16[64,4224]{1,0:T(8,128)(2,1)}), bf16[1024,4224]{1,0:T(8,128)(2,1)}) %all-gather.5.cloned.1.call-update) | async-done | bytes 8650768 | tf_op jit(solution)/shard_map/all_gather | solution.py:504
  142.9 6.2 %fusion.18 = f32[512,2816]{1,0:T(8,128)S(1)} fusion(bf16[512,1024]{1,0:T(8,128)(2,1)} %collective-permute-done.5, bf16[1024,4224]{1,0:T(8,128)(2,1)} %all-gather.5.cloned.1.call-done), kind=kOutput, calls=%fused_computation.27 | convolution fusion | flops 2952790016 | bytes 12582912 | tf_op jit(solution)/shard_map/dot_general | solution.py:56
  149.2 5.0 %multiply_convert_fusion.5 = (bf16[512,1408]{1,0:T(8,128)(2,1)S(1)}, bf16[512,1408]{1,0:T(8,128)(2,1)S(1)}, bf16[512,1408]{1,0:T(8,128)(2,1)}) fusion(f32[512,2816]{1,0:T(8,128)S(1)} %fusion.18, bf16[512,1024]{1,0:T(8,128)(2,1)} %collective-permute-done.1, bf16[1024,4224]{1,0:T(8,128)(2,1)S(1)} %copy-done.45), kind=kOutput, calls=%fused_computation.51 | convolution fusion | flops 1486487552 | bytes 14024704 | tf_op jit(solution)/shard_map/dot_general | solution.py:56
  154.1 4.2 %fusion.62 = bf16[512,1024]{1,0:T(8,128)(2,1)} fusion(bf16[1024,4224]{1,0:T(8,128)(2,1)S(1)} %copy-done.45, bf16[512,1408]{1,0:T(8,128)(2,1)S(1)} %get-tuple-element.133, bf16[512,1408]{1,0:T(8,128)(2,1)S(1)} %get-tuple-element.132), kind=kOutput, calls=%fused_computation.93 | convolution fusion | flops 2959081472 | bytes 9699328 | tf_op jit(solution)/shard_map/dot_general | solution.py:60
  159.8 4.4 %fusion.14 = f32[512,2816]{1,0:T(8,128)S(1)} fusion(bf16[512,1024]{1,0:T(8,128)(2,1)} %multiply_convert_fusion.6, bf16[1024,4224]{1,0:T(8,128)(2,1)S(1)} %copy-done.45), kind=kOutput, calls=%fused_computation.23 | convolution fusion | flops 2952790016 | bytes 12582912 | tf_op jit(solution)/shard_map/dot_general | solution.py:56
  168.1 9.7 %fusion.9 = bf16[1024,2816]{1,0:T(8,128)(2,1)S(1)} fusion(bf16[512,1408]{1,0:T(8,128)(2,1)} %copy-done.52, bf16[512,1408]{1,0:T(8,128)(2,1)} %copy-done.51, bf16[512,1408]{1,0:T(8,128)(2,1)S(1)} %get-tuple-element.131, bf16[512,1408]{1,0:T(8,128)(2,1)S(1)} %get-tuple-element.130, bf16[512,1024]{1,0:T(8,128)(2,1)} %collective-permute-done.5, ...), kind=kOutput, calls=%fused_computation.11 | convolution fusion | flops 5935726592 | bytes 13631488 | tf_op jit(solution)/shard_map/dot_general | solution.py:64
  177.8 5.6 %convolution_convert_fusion.1 = bf16[1024,1408]{1,0:T(8,128)(2,1)S(1)} fusion(bf16[512,1408]{1,0:T(8,128)(2,1)} %get-tuple-element.134, bf16[512,1408]{1,0:T(8,128)(2,1)} %get-tuple-element.61, bf16[512,1024]{1,0:T(8,128)(2,1)} %collective-permute-done.1, bf16[512,1024]{1,0:T(8,128)(2,1)S(1)} %copy-done.25), kind=kOutput, calls=%fused_computation.19 | convolution fusion | flops 2964193280 | bytes 7864320 | tf_op jit(solution)/shard_map/dot_general | solution.py:64
  187.5 8.0 %multiply_reduce_fusion.1 = (f32[1024]{0:T(1024)S(1)}, f32[512]{0:T(512)S(1)}, f32[512,1024]{1,0:T(8,128)S(1)}) fusion(f32[512,1024]{1,0:T(8,128)} %copy-done.10, f32[512]{0:T(512)S(1)} %get-tuple-element.151, bf16[512,1024]{1,0:T(8,128)(2,1)} %collective-permute-done.6, f32[1024]{0:T(1024)S(1)} %convert_element_type.227, ...), kind=kOutput, calls=%fused_computation.72 | convolution fusion | flops 2962749952 | bytes 13905920 | tf_op jit(solution)/shard_map/dot_general | solution.py:60
  210.0 4.9 %fusion.59 = bf16[512,1024]{1,0:T(8,128)(2,1)} fusion(bf16[512,1408]{1,0:T(8,128)(2,1)S(1)} %copy-done.48, bf16[1024,4224]{1,0:T(8,128)(2,1)} %all-gather.5.cloned.1.call-done), kind=kOutput, calls=%fused_computation.90 | convolution fusion | flops 1476919296 | bytes 5373952 | tf_op jit(solution)/shard_map/dot_general | solution.py:60
  215.6 8.1 %collective-permute-done.7 = bf16[512,512]{1,0:T(8,128)(2,1)S(1)} collective-permute-done((bf16[512,512]{1,0:T(8,128)(2,1)S(1)}, bf16[512,512]{1,0:T(8,128)(2,1)S(1)}, u32[]{:S(2)}, u32[]{:S(2)}) %collective-permute-start.7) | collective-permute-done | bytes 524320 | tf_op jit(solution)/shard_map/ppermute | solution.py:383
  229.7 21.4 %mixer_backward.1 = (bf16[1024,1664]{1,0:T(8,128)(2,1)S(1)}, f32[8,256]{1,0:T(8,128)S(1)}, f32[128,256]{1,0:T(8,128)S(1)}, f32[8,256]{1,0:T(8,128)S(1)}) custom-call(s32[17]{0:T(128)S(1)} %pad_add_fusion.scal, bf16[1024,1536]{1,0:T(8,128)(2,1)S(1)} %copy-done.5, f32[1024,256]{1,0:T(8,128)S(1)} %convolution_add_fusion.z, f32[1024,1]{1,0:T(8,128)S(1)} %copy.51.live, ...), custom_call_target="tpu_custom_call" | custom-call | flops 24999999488 | bytes 20000000 | tf_op jit(solution)/shard_map/mixer_backward/pallas_call | solution.py:334
  251.1 5.3 %convolution_convert_fusion = bf16[1024,1664]{1,0:T(8,128)(2,1)S(1)} fusion(bf16[1024,1664]{1,0:T(8,128)(2,1)S(1)} %get-tuple-element.58, bf16[512,1024]{1,0:T(8,128)(2,1)} %collective-permute-done, bf16[512,1024]{1,0:T(8,128)(2,1)S(1)} %copy-done.30), kind=kOutput, calls=%fused_computation.18 | convolution fusion | flops 3495559168 | bytes 8912896 | tf_op jit(solution)/shard_map/dot_general | solution.py:64
  262.0 5.3 %multiply_reduce_fusion = (f32[1024]{0:T(1024)S(1)}, bf16[1024,1024]{1,0:T(8,128)(2,1)S(1)}) fusion(bf16[512,1024]{1,0:T(8,128)(2,1)} %collective-permute-done, bf16[512,1024]{1,0:T(8,128)(2,1)S(1)} %copy-done.30, bf16[1024,1664]{1,0:T(8,128)(2,1)S(1)} %get-tuple-element.58, bf16[1024,16]{1,0:T(8,128)(2,1)S(1)} %copy-done.32, ...), kind=kOutput, calls=%fused_computation.12 | convolution fusion | flops 3507223552 | bytes 10784768 | tf_op jit(solution)/shard_map/dot_general | solution.py:60
  282.4 7.4 %collective-permute-done.13 = bf16[2,2,64,1024]{3,2,1,0:T(8,128)(2,1)S(1)} collective-permute-done((bf16[2,2,64,1024]{3,2,1,0:T(8,128)(2,1)S(1)}, bf16[2,2,64,1024]{3,2,1,0:T(8,128)(2,1)S(1)}, u32[]{:S(2)}, u32[]{:S(2)}) %collective-permute-start.13) | collective-permute-done | bytes 524320 | tf_op jit(solution)/shard_map/ppermute | solution.py:414
  290.0 5.4 %collective-permute-done.10 = bf16[512,1024]{1,0:T(8,128)(2,1)S(1)} collective-permute-done((bf16[512,1024]{1,0:T(8,128)(2,1)S(1)}, bf16[512,1024]{1,0:T(8,128)(2,1)S(1)}, u32[]{:S(2)}, u32[]{:S(2)}) %collective-permute-start.10) | collective-permute-done | bytes 1048608 | tf_op jit(solution)/shard_map/ppermute | solution.py:383
  296.2 13.7 %collective-permute-done.14 = bf16[2,2,64,1024]{3,2,1,0:T(8,128)(2,1)S(1)} collective-permute-done((bf16[2,2,64,1024]{3,2,1,0:T(8,128)(2,1)S(1)}, bf16[2,2,64,1024]{3,2,1,0:T(8,128)(2,1)S(1)}, u32[]{:S(2)}, u32[]{:S(2)}) %collective-permute-start.14) | collective-permute-done | bytes 524320 | tf_op jit(solution)/shard_map/ppermute | solution.py:414
  327.1 10.9 %collective-permute-done.23 = bf16[64,1024]{1,0:T(8,128)(2,1)S(1)} collective-permute-done((bf16[64,1024]{1,0:T(8,128)(2,1)S(1)}, bf16[64,1024]{1,0:T(8,128)(2,1)S(1)}, u32[]{:S(2)}, u32[]{:S(2)}) %collective-permute-start.23) | collective-permute-done | bytes 131104 | tf_op jit(solution)/shard_map/ppermute | solution.py:414
  338.8 8.5 %collective-permute-done.21 = bf16[64,1024]{1,0:T(8,128)(2,1)S(1)} collective-permute-done((bf16[64,1024]{1,0:T(8,128)(2,1)S(1)}, bf16[64,1024]{1,0:T(8,128)(2,1)S(1)}, u32[]{:S(2)}, u32[]{:S(2)}) %collective-permute-start.21) | collective-permute-done | bytes 131104 | tf_op jit(solution)/shard_map/ppermute | solution.py:414
  348.8 6.3 %collective-permute-done.19 = f32[214,128]{1,0:T(8,128)S(1)} collective-permute-done((f32[214,128]{1,0:T(8,128)S(1)}, f32[214,128]{1,0:T(8,128)S(1)}, u32[]{:S(2)}, u32[]{:S(2)}) %collective-permute-start.19) | collective-permute-done | bytes 109600 | tf_op jit(solution)/shard_map/ppermute | solution.py:449
  (257 shorter events, 105.5 us)
Async XLA Ops:
  7.2 58.6 %all-gather.3.cloned.1.call-start = ((), (), s32[]{:S(2)}) async-start(), calls=%async_computation.1 | async-start | bytes 4456448 | tf_op jit(solution)/shard_map/all_gather | solution.py:496
  12.2 130.8 %all-gather.5.cloned.1.call-start = ((), (), s32[]{:S(2)}) async-start(), calls=%async_computation.2 | async-start | bytes 9191424 | tf_op jit(solution)/shard_map/all_gather | solution.py:504
  14.2 344.3 %reduce-scatter.2.cloned.1.call-start = ((), (), s32[]{:S(2)}) async-start(), calls=%async_computation.3 | async-start | bytes 9191424 | tf_op jit(solution)/shard_map/reduce_scatter | solution.py:594
  14.3 51.6 %collective-permute-start.1 = (bf16[512,1024]{1,0:T(8,128)(2,1)}, bf16[512,1024]{1,0:T(8,128)(2,1)}, u32[]{:S(2)}, u32[]{:S(2)}) collective-permute-start(bf16[512,1024]{1,0:T(8,128)(2,1)} %param.21), channel_id=1, source_target_pairs={{0,1},{1,0},{2,3},{3,2},{4,5},{5,4},{6,7},{7,6},{8,9},{9,8},{10,11... | collective-permute-start | bytes 3145736 | tf_op jit(solution)/shard_map/ppermute | solution.py:383
  19.2 44.1 %collective-permute-start = (bf16[512,1024]{1,0:T(8,128)(2,1)S(1)}, bf16[512,1024]{1,0:T(8,128)(2,1)}, u32[]{:S(2)}, u32[]{:S(2)}) collective-permute-start(bf16[512,1024]{1,0:T(8,128)(2,1)S(1)} %fusion.38), channel_id=1, source_target_pairs={{0,1},{1,0},{2,3},{3,2},{4,5},{5,4},{6,7},{7,6},{8,9},{9,8},{10,11... | collective-permute-start | bytes 3145736 | tf_op jit(solution)/shard_map/ppermute | solution.py:383
  67.2 21.4 %collective-permute-start.2 = (bf16[512,512]{1,0:T(8,128)(2,1)S(1)}, bf16[512,512]{1,0:T(8,128)(2,1)}, u32[]{:S(2)}, u32[]{:S(2)}) collective-permute-start(bf16[512,512]{1,0:T(8,128)(2,1)S(1)} %constant_dynamic-slice_fusion), channel_id=1, source_target_pairs={{0,1},{1,0},{2,3},{3,2},{4,5},{5,4},{6,7},{7,6},{8,9},{9,8},{10,11... | collective-permute-start | bytes 1572872 | tf_op jit(solution)/shard_map/ppermute | solution.py:383
  89.4 14.5 %collective-permute-start.3 = (bf16[512,512]{1,0:T(8,128)(2,1)}, bf16[512,512]{1,0:T(8,128)(2,1)S(1)}, u32[]{:S(2)}, u32[]{:S(2)}) collective-permute-start(bf16[512,512]{1,0:T(8,128)(2,1)} %slice.87), channel_id=1, source_target_pairs={{0,1},{1,0},{2,3},{3,2},{4,5},{5,4},{6,7},{7,6},{8,9},{9,8},{10,11... | collective-permute-start | bytes 1572872 | tf_op jit(solution)/shard_map/ppermute | solution.py:383
  108.2 25.2 %collective-permute-start.5 = (bf16[512,1024]{1,0:T(8,128)(2,1)}, bf16[512,1024]{1,0:T(8,128)(2,1)}, u32[]{:S(2)}, u32[]{:S(2)}) collective-permute-start(bf16[512,1024]{1,0:T(8,128)(2,1)} %multiply_convert_fusion.6), channel_id=1, source_target_pairs={{0,1},{1,0},{2,3},{3,2},{4,5},{5,4},{6,7},{7,6},{8,9},{9,8},{10,11... | collective-permute-start | bytes 3145736 | tf_op jit(solution)/shard_map/ppermute | solution.py:383
  158.3 29.1 %collective-permute-start.6 = (bf16[512,1024]{1,0:T(8,128)(2,1)}, bf16[512,1024]{1,0:T(8,128)(2,1)}, u32[]{:S(2)}, u32[]{:S(2)}) collective-permute-start(bf16[512,1024]{1,0:T(8,128)(2,1)} %fusion.62), channel_id=1, source_target_pairs={{0,1},{1,0},{2,3},{3,2},{4,5},{5,4},{6,7},{7,6},{8,9},{9,8},{10,11... | collective-permute-start | bytes 3145736 | tf_op jit(solution)/shard_map/ppermute | solution.py:383
  207.3 16.5 %collective-permute-start.8 = (bf16[8,64,1024]{2,1,0:T(8,128)(2,1)S(1)}, bf16[8,64,1024]{2,1,0:T(8,128)(2,1)S(1)}, u32[]{:S(2)}, u32[]{:S(2)}) collective-permute-start(bf16[8,64,1024]{2,1,0:T(8,128)(2,1)S(1)} %dynamic-slice_bitcast_fusion.1), channel_id=1, source_target_pairs={{0,2},{2,0},{4,6},{6,4},{8,10},{10,8},{12,14},{14,12},{16,18},{18,... | collective-permute-start | bytes 3145736 | tf_op jit(solution)/shard_map/ppermute | solution.py:392
  209.3 14.4 %collective-permute-start.7 = (bf16[512,512]{1,0:T(8,128)(2,1)S(1)}, bf16[512,512]{1,0:T(8,128)(2,1)S(1)}, u32[]{:S(2)}, u32[]{:S(2)}) collective-permute-start(bf16[512,512]{1,0:T(8,128)(2,1)S(1)} %convolution_convert_fusion.5), channel_id=1, source_target_pairs={{0,1},{1,0},{2,3},{3,2},{4,5},{5,4},{6,7},{7,6},{8,9},{9,8},{10,11... | collective-permute-start | bytes 1572872 | tf_op jit(solution)/shard_map/ppermute | solution.py:383
  227.5 28.9 %collective-permute-start.11 = (bf16[512,512]{1,0:T(8,128)(2,1)S(1)}, bf16[512,512]{1,0:T(8,128)(2,1)S(1)}, u32[]{:S(2)}, u32[]{:S(2)}) collective-permute-start(bf16[512,512]{1,0:T(8,128)(2,1)S(1)} %slice.96), channel_id=1, source_target_pairs={{0,1},{1,0},{2,3},{3,2},{4,5},{5,4},{6,7},{7,6},{8,9},{9,8},{10,11... | collective-permute-start | bytes 1572872 | tf_op jit(solution)/shard_map/ppermute | solution.py:383
  228.2 42.2 %collective-permute-start.9 = (bf16[512,1024]{1,0:T(8,128)(2,1)}, bf16[512,1024]{1,0:T(8,128)(2,1)}, u32[]{:S(2)}, u32[]{:S(2)}) collective-permute-start(bf16[512,1024]{1,0:T(8,128)(2,1)} %fusion.59), channel_id=1, source_target_pairs={{0,1},{1,0},{2,3},{3,2},{4,5},{5,4},{6,7},{7,6},{8,9},{9,8},{10,11... | collective-permute-start | bytes 3145736 | tf_op jit(solution)/shard_map/ppermute | solution.py:383
  261.3 9.7 %collective-permute-start.12 = (bf16[8,64,1536]{2,1,0:T(8,128)(2,1)}, bf16[8,64,1536]{2,1,0:T(8,128)(2,1)}, u32[]{:S(2)}, u32[]{:S(2)}) collective-permute-start(bf16[8,64,1536]{2,1,0:T(8,128)(2,1)} %dynamic-slice_bitcast_fusion), channel_id=1, source_target_pairs={{0,2},{2,0},{4,6},{6,4},{8,10},{10,8},{12,14},{14,12},{16,18},{18,... | collective-permute-start | bytes 4718600 | tf_op jit(solution)/shard_map/ppermute | solution.py:392
  270.5 24.9 %collective-permute-start.10 = (bf16[512,1024]{1,0:T(8,128)(2,1)S(1)}, bf16[512,1024]{1,0:T(8,128)(2,1)S(1)}, u32[]{:S(2)}, u32[]{:S(2)}) collective-permute-start(bf16[512,1024]{1,0:T(8,128)(2,1)S(1)} %slice.95), channel_id=1, source_target_pairs={{0,1},{1,0},{2,3},{3,2},{4,5},{5,4},{6,7},{7,6},{8,9},{9,8},{10,11... | collective-permute-start | bytes 3145736 | tf_op jit(solution)/shard_map/ppermute | solution.py:383
  273.7 16.1 %collective-permute-start.13 = (bf16[2,2,64,1024]{3,2,1,0:T(8,128)(2,1)S(1)}, bf16[2,2,64,1024]{3,2,1,0:T(8,128)(2,1)S(1)}, u32[]{:S(2)}, u32[]{:S(2)}) collective-permute-start(bf16[2,2,64,1024]{3,2,1,0:T(8,128)(2,1)S(1)} %dynamic-slice_bitcast_fusion.3), channel_id=1, source_target_pairs={{0,4},{2,6},{4,0},{6,2},{8,12},{10,14},{12,8},{14,10},{16,20},{18,... | collective-permute-start | bytes 1572872 | tf_op jit(solution)/shard_map/ppermute | solution.py:414
  278.4 31.5 %collective-permute-start.14 = (bf16[2,2,64,1024]{3,2,1,0:T(8,128)(2,1)S(1)}, bf16[2,2,64,1024]{3,2,1,0:T(8,128)(2,1)S(1)}, u32[]{:S(2)}, u32[]{:S(2)}) collective-permute-start(bf16[2,2,64,1024]{3,2,1,0:T(8,128)(2,1)S(1)} %dynamic-slice_bitcast_fusion.2), channel_id=1, source_target_pairs={{0,4},{2,6},{4,0},{6,2},{8,12},{10,14},{12,8},{14,10},{16,20},{18,... | collective-permute-start | bytes 1572872 | tf_op jit(solution)/shard_map/ppermute | solution.py:414
  295.5 23.3 %collective-permute-start.22 = (bf16[2,64,1024]{2,1,0:T(8,128)(2,1)S(1)}, bf16[2,64,1024]{2,1,0:T(8,128)(2,1)S(1)}, u32[]{:S(2)}, u32[]{:S(2)}) collective-permute-start(bf16[2,64,1024]{2,1,0:T(8,128)(2,1)S(1)} %dynamic-slice_bitcast_fusion.4), channel_id=1, source_target_pairs={{0,8},{2,10},{4,12},{6,14},{8,0},{10,2},{12,4},{14,6},{16,24},{18,... | collective-permute-start | bytes 786440 | tf_op jit(solution)/shard_map/ppermute | solution.py:414
  310.1 10.0 %collective-permute-start.20 = (bf16[2,64,1024]{2,1,0:T(8,128)(2,1)S(1)}, bf16[2,64,1024]{2,1,0:T(8,128)(2,1)S(1)}, u32[]{:S(2)}, u32[]{:S(2)}) collective-permute-start(bf16[2,64,1024]{2,1,0:T(8,128)(2,1)S(1)} %dynamic-slice_bitcast_fusion.5), channel_id=1, source_target_pairs={{0,8},{2,10},{4,12},{6,14},{8,0},{10,2},{12,4},{14,6},{16,24},{18,... | collective-permute-start | bytes 786440 | tf_op jit(solution)/shard_map/ppermute | solution.py:414
  318.0 7.8 %collective-permute-start.17 = (f32[214,128]{1,0:T(8,128)S(1)}, f32[214,128]{1,0:T(8,128)S(1)}, u32[]{:S(2)}, u32[]{:S(2)}) collective-permute-start(f32[214,128]{1,0:T(8,128)S(1)} %add.245), channel_id=1, source_target_pairs={{0,4},{2,6},{4,0},{6,2},{8,12},{10,14},{12,8},{14,10},{16,20},{18,... | collective-permute-start | bytes 328712 | tf_op jit(solution)/shard_map/ppermute | solution.py:449
  318.9 19.1 %collective-permute-start.23 = (bf16[64,1024]{1,0:T(8,128)(2,1)S(1)}, bf16[64,1024]{1,0:T(8,128)(2,1)S(1)}, u32[]{:S(2)}, u32[]{:S(2)}) collective-permute-start(bf16[64,1024]{1,0:T(8,128)(2,1)S(1)} %dynamic-slice_bitcast_fusion.6), channel_id=1, source_target_pairs={{0,16},{2,18},{4,20},{6,22},{8,24},{10,26},{12,28},{14,30},{16,0},... | collective-permute-start | bytes 393224 | tf_op jit(solution)/shard_map/ppermute | solution.py:414
  320.2 27.1 %collective-permute-start.21 = (bf16[64,1024]{1,0:T(8,128)(2,1)S(1)}, bf16[64,1024]{1,0:T(8,128)(2,1)S(1)}, u32[]{:S(2)}, u32[]{:S(2)}) collective-permute-start(bf16[64,1024]{1,0:T(8,128)(2,1)S(1)} %dynamic-slice_bitcast_fusion.7), channel_id=1, source_target_pairs={{0,16},{2,18},{4,20},{6,22},{8,24},{10,26},{12,28},{14,30},{16,0},... | collective-permute-start | bytes 393224 | tf_op jit(solution)/shard_map/ppermute | solution.py:414
  325.8 21.6 %collective-permute-start.18 = (f32[214,128]{1,0:T(8,128)S(1)}, f32[214,128]{1,0:T(8,128)S(1)}, u32[]{:S(2)}, u32[]{:S(2)}) collective-permute-start(f32[214,128]{1,0:T(8,128)S(1)} %add.246), channel_id=1, source_target_pairs={{0,8},{2,10},{4,12},{6,14},{8,0},{10,2},{12,4},{14,6},{16,24},{18,... | collective-permute-start | bytes 328712 | tf_op jit(solution)/shard_map/ppermute | solution.py:449
  347.4 7.7 %collective-permute-start.19 = (f32[214,128]{1,0:T(8,128)S(1)}, f32[214,128]{1,0:T(8,128)S(1)}, u32[]{:S(2)}, u32[]{:S(2)}) collective-permute-start(f32[214,128]{1,0:T(8,128)S(1)} %add.247), channel_id=1, source_target_pairs={{0,16},{2,18},{4,20},{6,22},{8,24},{10,26},{12,28},{14,30},{16,0},... | collective-permute-start | bytes 328712 | tf_op jit(solution)/shard_map/ppermute | solution.py:449
  (57 other events, 626.5 us)
Sparse Core Ops, SparseCore 0:
  12.3 53.2 all-gather.2
  67.9 75.0 all-gather.4
  225.3 129.5 reduce-scatter.1
